TPU v7x, 32 devices: a whole 2x2x4 slice. The times are simulated.
32 devices in a mesh: req: 8 (over z, x), head: 4 (over y, core).
Axes of the slice: x: 2, y: 2, z: 4, core: 2. Of those that a mesh axis runs over, the one named last changes fastest.
Arguments:
- hidden: bfloat16 [192, 1280], P('req'), may hold values from -6 to 6
- w_qkv: bfloat16 [3, 1280, 1280], P(None, None, 'head'), may hold values from -0.15625 to 0.15625
- w_out: bfloat16 [1280, 1280], P('head'), may hold values from -0.15625 to 0.15625
- s_qk: float32 [1280], P('head'), may hold values from 0.5 to 2
- alpha_attn: float32 [1280], replicated, may hold values from 0.05 to 0.5
- w_gate_up: bfloat16 [2, 1280, 2560], P(None, None, 'head'), may hold values from -0.15625 to 0.15625
- w_down: bfloat16 [2560, 1280], P('head'), may hold values from -0.125 to 0.125
- s_up: float32 [2560], P('head'), may hold values from 0.5 to 2
- s_gate: float32 [2560], P('head'), may hold values from 0.5 to 2
- alpha_mlp: float32 [1280], replicated, may hold values from 0.05 to 0.5
- short_keys: bfloat16 [192, 128, 1280], P('req', None, 'head')
- short_values: bfloat16 [192, 128, 1280], P('req', None, 'head'), may hold values from -6 to 6
- cache_lengths: int32 [192], P('req'), may hold values from 1 to 128, as said below
- long_keys: bfloat16 [4, 2048, 1280], P(None, 'req', 'head')
- long_values: bfloat16 [4, 2048, 1280], P(None, 'req', 'head'), may hold values from -6 to 6
- long_rows: int32 [4], replicated, may hold values from 0 to 191, as said below
Outputs:
- updated: bfloat16 [192, 1280], P('req')
Inputs may be any that keep to these rules, and one draw needn't show every extreme that they name: `cache_lengths`: the entries of the rows named by long_rows are not read. `long_rows`: 4 distinct request rows.
All inputs are finite; a program needn't handle non-finite values.
Results may differ from a plain program's by a relative error of at most 0.011.
Values may be sent and summed in bfloat16 or wider, within the bound.
No kernel may reach another device: no remote copies, remote signals or barrier semaphores. Data moves between devices by JAX's collectives and lax.ppermute only.
A program may use at most 64 MiB of HBM per device.

v0:
```python
import math

import jax
import jax.numpy as jnp
from jax import lax
from jax.sharding import PartitionSpec as P

HEAD_DIM = 64


EPS = 1e-06


def joined(part, axis, combine):
    gathered = jax.tree.map(lambda a: lax.all_gather(a, axis), part)

    def take(source):
        return jax.tree.map(lambda a: lax.dynamic_index_in_dim(a, source, 0, False), gathered)

    return lax.fori_loop(
        1, lax.axis_size(axis), lambda source, state: combine(state, take(source)), take(0)
    )


def row_norm(values):
    return values * lax.rsqrt(jnp.mean(values * values, axis=-1, keepdims=True) + EPS)


def head_unit(values, gains):
    shaped = values.reshape(values.shape[:-1] + (values.shape[-1] // HEAD_DIM, HEAD_DIM))
    scaled = shaped * lax.rsqrt(jnp.sum(shaped * shaped, axis=-1, keepdims=True) + EPS)
    return scaled.reshape(values.shape) * gains


def combine_parts(first, second):
    top = jnp.maximum(first[0], second[0])
    left = jnp.exp(first[0] - top)
    right = jnp.exp(second[0] - top)
    return (
        top,
        first[1] * left + second[1] * right,
        first[2] * left[..., None] + second[2] * right[..., None],
    )


def renormed_update(partial_value, base, alpha):
    total = lax.psum(partial_value.astype(jnp.bfloat16), "head").astype(jnp.float32)
    return row_norm(base + alpha * (row_norm(total) - base)).astype(jnp.bfloat16)


def on_device(
    hidden,
    w_qkv,
    w_out,
    s_qk,
    alpha_attn,
    w_gate_up,
    w_down,
    s_up,
    s_gate,
    alpha_mlp,
    short_keys,
    short_values,
    cache_lengths,
    long_keys,
    long_values,
    long_rows,
):
    rows = hidden.shape[0]
    local_width = w_qkv.shape[2]
    local_heads = local_width // HEAD_DIM
    scale = math.sqrt(HEAD_DIM)
    query = jnp.dot(hidden, w_qkv[0], preferred_element_type=jnp.float32)
    key_new = jnp.dot(hidden, w_qkv[1], preferred_element_type=jnp.float32)
    value_new = jnp.dot(hidden, w_qkv[2], preferred_element_type=jnp.float32)
    query_unit = head_unit(query, s_qk).astype(jnp.bfloat16)
    key_unit = head_unit(key_new, s_qk).astype(jnp.bfloat16)
    query_heads = query_unit.reshape(rows, local_heads, HEAD_DIM)
    key_heads = key_unit.reshape(rows, local_heads, HEAD_DIM)
    value_heads = value_new.astype(jnp.bfloat16).reshape(rows, local_heads, HEAD_DIM)
    slots = short_keys.shape[1]
    cache_k = short_keys.reshape(rows, slots, local_heads, HEAD_DIM)
    cache_v = short_values.reshape(rows, slots, local_heads, HEAD_DIM)
    scores = scale * jnp.einsum(
        "rhd,rjhd->rhj", query_heads, cache_k, preferred_element_type=jnp.float32
    )
    valid = (jnp.arange(slots, dtype=jnp.int32)[None, :] < cache_lengths[:, None])[:, None, :]
    scores = jnp.where(valid, scores, -1e30)
    own = scale * jnp.sum(query_heads.astype(jnp.float32) * key_heads.astype(jnp.float32), axis=-1)
    top = jnp.maximum(jnp.max(scores, axis=-1), own)
    weights = jnp.where(valid, jnp.exp(scores - top[..., None]), 0.0)
    own_weight = jnp.exp(own - top)
    denominator = jnp.sum(weights, axis=-1) + own_weight
    summed = jnp.einsum(
        "rhj,rjhd->rhd", weights.astype(jnp.bfloat16), cache_v, preferred_element_type=jnp.float32
    )
    summed = summed + own_weight.astype(jnp.bfloat16).astype(jnp.float32)[
        ..., None
    ] * value_heads.astype(jnp.float32)
    short_out = summed / denominator[..., None]
    offset = lax.axis_index("req") * rows
    local_rows = long_rows - offset
    safe_rows = jnp.clip(local_rows, 0, rows - 1)
    every_query = lax.all_gather(query_unit, "req", axis=0, tiled=True)
    long_query = jnp.take(every_query, long_rows, axis=0)
    longs = long_keys.shape[0]
    span = long_keys.shape[1]
    long_q = long_query.reshape(longs, local_heads, HEAD_DIM)
    long_k = long_keys.reshape(longs, span, local_heads, HEAD_DIM)
    long_v = long_values.reshape(longs, span, local_heads, HEAD_DIM)
    long_scores = scale * jnp.einsum(
        "lhd,ljhd->lhj", long_q, long_k, preferred_element_type=jnp.float32
    )
    long_top = jnp.max(long_scores, axis=-1)
    long_weights = jnp.exp(long_scores - long_top[..., None])
    long_total = jnp.sum(long_weights, axis=-1)
    long_acc = jnp.einsum(
        "lhj,ljhd->lhd",
        long_weights.astype(jnp.bfloat16),
        long_v,
        preferred_element_type=jnp.float32,
    )
    merged_top, merged_total, merged_acc = joined(
        (long_top, long_total, long_acc), "req", combine_parts
    )
    owner_keys = jnp.take(key_heads, safe_rows, axis=0).astype(jnp.float32)
    owner_values = jnp.take(value_heads, safe_rows, axis=0).astype(jnp.float32)
    own_long = scale * jnp.sum(long_q.astype(jnp.float32) * owner_keys, axis=-1)
    final_top = jnp.maximum(merged_top, own_long)
    carried = jnp.exp(merged_top - final_top)
    fresh = jnp.exp(own_long - final_top)
    long_out = (
        merged_acc * carried[..., None]
        + fresh.astype(jnp.bfloat16).astype(jnp.float32)[..., None] * owner_values
    )
    long_out = long_out / (merged_total * carried + fresh)[..., None]
    matches = jnp.arange(rows, dtype=jnp.int32)[:, None] + offset == long_rows[None, :]
    placed = jnp.einsum(
        "rl,lhd->rhd", matches.astype(jnp.float32), long_out, precision=lax.Precision.HIGHEST
    )
    attended = jnp.where(jnp.any(matches, axis=1)[:, None, None], placed, short_out)
    attended = attended.astype(jnp.bfloat16).reshape(rows, local_width)
    projected = jnp.dot(attended, w_out, preferred_element_type=jnp.float32)
    middle = renormed_update(projected, hidden.astype(jnp.float32), alpha_attn)
    gate = jnp.dot(middle, w_gate_up[0], preferred_element_type=jnp.float32) * s_gate
    upward = jnp.dot(middle, w_gate_up[1], preferred_element_type=jnp.float32) * s_up
    gated = (jax.nn.silu(gate) * upward).astype(jnp.bfloat16)
    downward = jnp.dot(gated, w_down, preferred_element_type=jnp.float32)
    return renormed_update(downward, middle.astype(jnp.float32), alpha_mlp)


def solution(mesh):
    return jax.shard_map(
        on_device,
        mesh=mesh,
        in_specs=(
            P("req", None),
            P(None, None, "head"),
            P("head", None),
            P("head"),
            P(),
            P(None, None, "head"),
            P("head", None),
            P("head"),
            P("head"),
            P(),
            P("req", None, "head"),
            P("req", None, "head"),
            P("req"),
            P(None, "req", "head"),
            P(None, "req", "head"),
            P(),
        ),
        out_specs=P("req", None),
        check_vma=False,
    )
```

profile of v0, /device:TPU:0, one launch (start us, length us, event | category | flops | bytes accessed | tf_op | source)
XLA Modules:
  0.0 155.9 jit_solution(2318626464521364571)
XLA Ops:
  0.0 1.6 %fusion.69 = (bf16[1,1280,320]{1,2,0:T(8,128)(2,1)S(1)}, bf16[1,1280,320]{1,2,0:T(8,128)(2,1)S(1)}) fusion(bf16[3,1280,320]{1,2,0:T(8,128)(2,1)} %param.21), kind=kLoop, calls=%fused_computation.123 | loop fusion | bytes 3276800 | tf_op jit(solution)/shard_map/slice | solution.py:73
  1.7 0.5 multiply_reduce_fusion.3
  2.2 0.5 multiply_reduce_fusion.4
  2.8 0.2 multiply_reduce_fusion.2
  3.1 32.3 %all_gather.21 = bf16[192,320]{1,0:T(8,128)(2,1)S(1)} all-gather(bf16[24,320]{1,0:T(8,128)(2,1)S(1)} %multiply_convert_fusion.4), channel_id=1, replica_groups=mesh['req'=8,'head'=4] {'req'}, dimensions={0}, use_global_device_ids=true | all-gather | bytes 138240 | tf_op jit(solution)/shard_map/all_gather | solution.py:104
  35.4 0.6 gather_fusion
  36.2 0.2 fusion.57
  36.5 0.2 fusion.56
  36.6 1.4 fusion.51
  38.0 30.5 %all-gather.2 = f32[32,5,64]{2,1,0:T(8,128)S(1)} all-gather(f32[4,5,64]{2,1,0:T(8,128)S(1)} %bitcast.127), channel_id=4, replica_groups=mesh['req'=8,'head'=4] {'req'}, dimensions={0}, use_global_device_ids=true | all-gather | bytes 46080 | tf_op jit(solution)/shard_map/all_gather | solution.py:15
  68.6 26.0 %all-gather.4 = f32[8,4,5]{2,1,0:T(4,128)S(1)} all-gather(f32[1,4,5]{2,1,0:T(4,128)S(1)} %bitcast.128), channel_id=3, replica_groups=mesh['req'=8,'head'=4] {'req'}, dimensions={0}, use_global_device_ids=true | all-gather | bytes 720 | tf_op jit(solution)/shard_map/all_gather | solution.py:15
  94.7 26.0 %all-gather.3 = f32[8,4,5]{2,1,0:T(4,128)S(1)} all-gather(f32[1,4,5]{2,1,0:T(4,128)S(1)} %bitcast.129), channel_id=2, replica_groups=mesh['req'=8,'head'=4] {'req'}, dimensions={0}, use_global_device_ids=true | all-gather | bytes 720 | tf_op jit(solution)/shard_map/all_gather | solution.py:15
  120.7 0.7 while.19
  121.4 0.6 gather_fusion.1
  122.0 0.2 multiply_reduce_fusion.5
  122.2 1.5 convolution_convert_fusion.2
  123.8 0.6 gather_fusion.2
  124.5 0.6 fusion.38
  125.3 0.2 fusion.45
  125.5 0.4 copy-done.11
  125.9 1.1 fusion.36
  127.1 0.3 fusion.21
  127.5 0.2 convolution_convert_fusion.1
  127.8 10.7 %psum.14 = bf16[24,1280]{1,0:T(8,128)(2,1)S(1)} all-reduce(bf16[24,1280]{1,0:T(8,128)(2,1)S(1)} %convolution_convert_fusion.1), channel_id=1, replica_groups=mesh['req'=8,'head'=4] {'head'}, use_global_device_ids=true, to_apply=%region_11.13 | all-reduce | flops 30720 | bytes 122880 | tf_op jit(solution)/shard_map/psum | solution.py:47
  138.5 0.1 fusion.27
  138.6 0.2 multiply_reduce_fusion.1
  139.0 1.8 %fusion.9 = f32[24,640]{1,0:T(8,128)S(1)} fusion(bf16[24,1280]{1,0:T(8,128)(2,1)S(1)} %multiply_convert_fusion.1, bf16[2,1280,640]{2,1,0:T(8,128)(2,1)} %param.25, f32[640]{0:T(1024)S(1)} %copy-done.7), kind=kOutput, calls=%fused_computation.20 | convolution fusion | flops 39336960 | bytes 1763840 | tf_op jit(solution)/shard_map/dot_general | solution.py:145
  140.8 2.6 %convolution_convert_fusion = bf16[24,1280]{1,0:T(8,128)(2,1)S(1)} fusion(bf16[640,1280]{1,0:T(8,128)(2,1)} %param.26, bf16[24,1280]{1,0:T(8,128)(2,1)S(1)} %multiply_convert_fusion.1, bf16[2,1280,640]{2,1,0:T(8,128)(2,1)} %param.25, f32[24,640]{1,0:T(8,128)S(1)} %fusion.9, f32[640]{0:T(1024)S(1)} %copy-done.8), kind=kOutput, calls=%fused_computation.11 | convolution fusion | flops 78781440 | bytes 3463680 | tf_op jit(solution)/shard_map/dot_general | solution.py:148
  143.4 11.4 %psum.15 = bf16[24,1280]{1,0:T(8,128)(2,1)S(1)} all-reduce(bf16[24,1280]{1,0:T(8,128)(2,1)S(1)} %convolution_convert_fusion), channel_id=1, replica_groups=mesh['req'=8,'head'=4] {'head'}, use_global_device_ids=true, to_apply=%region_14.16 | all-reduce | flops 30720 | bytes 122880 | tf_op jit(solution)/shard_map/psum | solution.py:47
  154.8 0.1 fusion.29
  155.0 0.2 multiply_reduce_fusion
  155.2 0.7 multiply_convert_fusion
  (73 shorter events, 2.2 us)
Async XLA Ops:
  0.0 124.4 %copy-start = (bf16[24,128,320]{1,2,0:T(8,128)(2,1)S(1)}, bf16[24,128,320]{1,2,0:T(8,128)(2,1)}, u32[]{:S(2)}) copy-start(bf16[24,128,320]{1,2,0:T(8,128)(2,1)} %param.30) | copy-start | bytes 5898244
  0.0 1.7 %copy-start.1 = (bf16[24,1280]{1,0:T(8,128)(2,1)S(1)}, bf16[24,1280]{1,0:T(8,128)(2,1)}, u32[]{:S(2)}) copy-start(bf16[24,1280]{1,0:T(8,128)(2,1)} %param.20) | copy-start | bytes 184324
  0.0 2.7 %copy-start.6 = (f32[320]{0:T(512)S(1)}, f32[320]{0:T(512)}, u32[]{:S(2)}) copy-start(f32[320]{0:T(512)} %param.23) | copy-start | bytes 3844
  1.6 33.8 %copy-start.10 = (s32[4]{0:T(128)S(1)}, s32[4]{0:T(128)}, u32[]{:S(2)}) copy-start(s32[4]{0:T(128)} %param.35) | copy-start | bytes 52
  1.7 34.5 %copy-start.3 = (bf16[4,256,320]{1,2,0:T(8,128)(2,1)S(1)}, bf16[4,256,320]{1,2,0:T(8,128)(2,1)}, u32[]{:S(2)}) copy-start(bf16[4,256,320]{1,2,0:T(8,128)(2,1)} %param.33) | copy-start | bytes 1966084
  120.7 4.4 %copy-start.9 = (s32[24]{0:T(128)S(1)}, s32[24]{0:T(128)}, u32[]{:S(2)}) copy-start(s32[24]{0:T(128)} %param.32) | copy-start | bytes 292
  124.3 1.5 copy-start.11
  124.4 3.1 %copy-start.2 = (bf16[320,1280]{1,0:T(8,128)(2,1)S(1)}, bf16[320,1280]{1,0:T(8,128)(2,1)}, u32[]{:S(2)}) copy-start(bf16[320,1280]{1,0:T(8,128)(2,1)} %param.22) | copy-start | bytes 2457604
  125.1 13.5 %copy-start.4 = (f32[1280]{0:T(1024)S(1)}, f32[1280]{0:T(1024)}, u32[]{:S(2)}) copy-start(f32[1280]{0:T(1024)} %param.24) | copy-start | bytes 15364
  125.9 13.1 %copy-start.7 = (f32[640]{0:T(1024)S(1)}, f32[640]{0:T(1024)}, u32[]{:S(2)}) copy-start(f32[640]{0:T(1024)} %param.28) | copy-start | bytes 7684
  127.0 13.8 %copy-start.8 = (f32[640]{0:T(1024)S(1)}, f32[640]{0:T(1024)}, u32[]{:S(2)}) copy-start(f32[640]{0:T(1024)} %param.27) | copy-start | bytes 7684
  140.8 14.2 %copy-start.5 = (f32[1280]{0:T(1024)S(1)}, f32[1280]{0:T(1024)}, u32[]{:S(2)}) copy-start(f32[1280]{0:T(1024)} %param.29) | copy-start | bytes 15364
where the time goes:
time: 156 us
  blocking collectives  137 us (88%)
  matrix products  10.6 us (7%)
  local copies, waits for them, and re-layouts  4.47 us (3%)
  other arithmetic  3.51 us (2%)
    all_gather x3, blocking collectives, joined(): gathered = jax.tree.map(lambda a: lax.all_gather(a, axis), part)  82.5 us
    all_gather x1, blocking collectives, on_device(): every_query = lax.all_gather(query_unit, 'req', axis=0, tiled=True)  32.3 us
    psum x2, blocking collectives, renormed_update(): lax.psum(partial_value.astype(jnp.bfloat16), 'head').astype(jnp.float32)  22.2 us

commit v1 on v0

v1 whole, which is shorter than its diff:
```python
import functools
import math

import jax
import jax.numpy as jnp
from jax import lax
from jax.experimental import pallas as pl
from jax.experimental.pallas import tpu as pltpu
from jax.sharding import PartitionSpec as P

HEAD_DIM = 64
EPS = 1e-06
LOW = -1e30
F32 = jnp.float32
BF16 = jnp.bfloat16

VMEM = pl.BlockSpec(memory_space=pltpu.VMEM)
SMEM = pl.BlockSpec(memory_space=pltpu.SMEM)


def head_masks(width):
    lane = lax.broadcasted_iota(jnp.int32, (1, width), 1)
    return [
        (lane >= h * HEAD_DIM) & (lane < (h + 1) * HEAD_DIM) for h in range(width // HEAD_DIM)
    ]


def spread(columns, masks):
    total = jnp.where(masks[0], columns[0], 0.0)
    for mask, column in zip(masks[1:], columns[1:]):
        total = jnp.where(mask, column, total)
    return total


def head_sums(values, masks):
    return [jnp.sum(jnp.where(mask, values, 0.0), axis=-1, keepdims=True) for mask in masks]


def head_unit(values, gains, masks):
    scales = [lax.rsqrt(s + EPS) for s in head_sums(values * values, masks)]
    return (values * spread(scales, masks) * gains).astype(BF16).astype(F32)


def row_norm(values):
    return values * lax.rsqrt(jnp.mean(values * values, axis=-1, keepdims=True) + EPS)


def by_head(values, masks):
    return jnp.concatenate([jnp.where(mask, values, 0.0) for mask in masks], axis=0)


def attend(query, keys, values, valid, own, own_value, masks):
    rows = query.shape[0]
    scores = lax.dot_general(
        by_head(query, masks).astype(BF16),
        keys,
        (((1,), (1,)), ((), ())),
        preferred_element_type=F32,
    )
    tops, totals, fresh, weights = [], [], [], []
    for h in range(len(masks)):
        part = jnp.where(valid, scores[h * rows : (h + 1) * rows], LOW)
        top = jnp.max(part, axis=-1, keepdims=True)
        if own is not None:
            top = jnp.maximum(top, own[h])
        weight = jnp.where(valid, jnp.exp(part - top), 0.0)
        total = jnp.sum(weight, axis=-1, keepdims=True)
        if own is not None:
            fresh.append(jnp.exp(own[h] - top))
            total = total + fresh[-1]
        tops.append(top)
        totals.append(total)
        weights.append(weight)
    summed = jnp.dot(
        jnp.concatenate(weights, axis=0).astype(BF16), values, preferred_element_type=F32
    )
    acc = jnp.zeros(query.shape, F32)
    for h, mask in enumerate(masks):
        acc = jnp.where(mask, summed[h * rows : (h + 1) * rows], acc)
    if own is not None:
        acc = acc + spread(fresh, masks).astype(BF16).astype(F32) * own_value
    total = spread(totals, masks)
    return acc / total, spread(tops, masks) + jnp.log(total)


def short_kernel(
    lengths_ref, local_ref, hidden_ref, w_ref, gains_ref, keys_ref, values_ref, out_ref, lse_ref
):
    rows, width = out_ref.shape
    slots = keys_ref.shape[0] // rows
    masks = head_masks(width)
    hidden = hidden_ref[...]
    gains = gains_ref[...]
    query = jnp.dot(hidden, w_ref[0], preferred_element_type=F32)
    key_new = jnp.dot(hidden, w_ref[1], preferred_element_type=F32)
    value_new = jnp.dot(hidden, w_ref[2], preferred_element_type=F32).astype(BF16).astype(F32)
    query = head_unit(query, gains, masks) * math.sqrt(HEAD_DIM)
    key_new = head_unit(key_new, gains, masks)
    own = head_sums(query * key_new, masks)
    group = 8
    sub = lax.broadcasted_iota(jnp.int32, (group, slots), 0)
    lane = lax.broadcasted_iota(jnp.int32, (group, slots), 1)
    for start in range(0, rows, group):
        pieces = []
        for r in range(group):
            length = lengths_ref[start + r]
            for index in range(local_ref.shape[0]):
                length = jnp.where(local_ref[index] == start + r, 0, length)
            pieces.append((sub == r) & (lane < length))
        valid = jnp.concatenate([p.astype(F32) for p in pieces], axis=1) > 0.5
        span = slice(start, start + group)
        cached = slice(start * slots, (start + group) * slots)
        out, lse = attend(
            query[span],
            keys_ref[cached, :],
            values_ref[cached, :],
            valid,
            [o[span] for o in own],
            value_new[span],
            masks,
        )
        out_ref[span, :] = out
        lse_ref[span, :] = lse


def long_kernel(hidden_ref, w_ref, gains_ref, keys_ref, values_ref, sent_ref):
    longs = hidden_ref.shape[0]
    parties, rows, width = sent_ref.shape
    span = keys_ref.shape[0] // longs
    masks = head_masks(width)
    query = jnp.dot(hidden_ref[...], w_ref[0], preferred_element_type=F32)
    query = jnp.concatenate([query, jnp.zeros((rows - longs, width), F32)], axis=0)
    query = head_unit(query, gains_ref[...], masks) * math.sqrt(HEAD_DIM)
    sub = lax.broadcasted_iota(jnp.int32, (rows, span * longs), 0)
    lane = lax.broadcasted_iota(jnp.int32, (rows, span * longs), 1)
    valid = (lane >= sub * span) & (lane < (sub + 1) * span)
    valid = valid | ((sub >= longs) & (lane < span))
    out, lse = attend(query, keys_ref[...], values_ref[...], valid, None, None, masks)
    packed = jnp.concatenate([out[:longs], lse[:longs]], axis=0)
    for party in range(parties):
        sent_ref[party] = packed


def project_kernel(local_ref, parts_ref, short_ref, lse_ref, w_ref, out_ref):
    parties, doubled, width = parts_ref.shape
    longs = doubled // 2
    rows = short_ref.shape[0]
    top = parts_ref[0]
    for party in range(1, parties):
        top = jnp.maximum(top, parts_ref[party])
    top = top[longs:]
    total = jnp.zeros((longs, width), F32)
    acc = jnp.zeros((longs, width), F32)
    for party in range(parties):
        part = parts_ref[party]
        weight = jnp.exp(part[longs:] - top)
        total = total + weight
        acc = acc + weight * part[:longs]
    long_out = acc / total
    long_lse = top + jnp.log(total)
    row = lax.broadcasted_iota(jnp.int32, (rows, 1), 0)
    placed = jnp.zeros((rows, width), F32)
    placed_lse = jnp.full((rows, width), LOW, F32)
    for index in range(longs):
        here = row == local_ref[index]
        placed = jnp.where(here, long_out[index : index + 1], placed)
        placed_lse = jnp.where(here, long_lse[index : index + 1], placed_lse)
    short_lse = lse_ref[...]
    top = jnp.maximum(short_lse, placed_lse)
    near = jnp.exp(short_lse - top)
    far = jnp.exp(placed_lse - top)
    attended = (near * short_ref[...] + far * placed) / (near + far)
    out_ref[...] = jnp.dot(
        attended.astype(BF16), w_ref[...], preferred_element_type=F32
    ).astype(BF16)


def renormed(parts_ref, base, alpha):
    total = parts_ref[0].astype(F32)
    for part in range(1, parts_ref.shape[0]):
        total = total + parts_ref[part].astype(F32)
    return row_norm(base + alpha * (row_norm(total) - base)).astype(BF16)


def mlp_kernel(
    parts_ref, hidden_ref, alpha_ref, w_gate_up_ref, gate_ref, up_ref, w_down_ref, mid_ref, out_ref
):
    middle = renormed(parts_ref, hidden_ref[...].astype(F32), alpha_ref[...])
    mid_ref[...] = middle
    gate = jnp.dot(middle, w_gate_up_ref[0], preferred_element_type=F32) * gate_ref[...]
    upward = jnp.dot(middle, w_gate_up_ref[1], preferred_element_type=F32) * up_ref[...]
    gated = (gate / (1.0 + jnp.exp(-gate)) * upward).astype(BF16)
    out_ref[...] = jnp.dot(gated, w_down_ref[...], preferred_element_type=F32).astype(BF16)


def final_kernel(parts_ref, mid_ref, alpha_ref, out_ref):
    out_ref[...] = renormed(parts_ref, mid_ref[...].astype(F32), alpha_ref[...])


def call(kernel, specs, out_shape, cost, *operands):
    return pl.pallas_call(
        kernel,
        in_specs=specs,
        out_specs=jax.tree.map(lambda _: VMEM, out_shape),
        out_shape=out_shape,
        cost_estimate=pl.CostEstimate(flops=cost[0], bytes_accessed=cost[1], transcendentals=0),
        compiler_params=pltpu.CompilerParams(vmem_limit_bytes=24 * 1024 * 1024),
    )(*operands)


def on_device(
    hidden,
    w_qkv,
    w_out,
    s_qk,
    alpha_attn,
    w_gate_up,
    w_down,
    s_up,
    s_gate,
    alpha_mlp,
    short_keys,
    short_values,
    cache_lengths,
    long_keys,
    long_values,
    long_rows,
):
    rows, model = hidden.shape
    width = w_qkv.shape[2]
    longs, span = long_keys.shape[:2]
    slots = short_keys.shape[1]
    parties = lax.axis_size("req")
    local = long_rows - lax.axis_index("req") * rows
    with jax.named_scope("long_hidden"):
        matches = (local[:, None] == jnp.arange(rows, dtype=jnp.int32)[None, :]).astype(BF16)
        picked = jnp.dot(matches, hidden, preferred_element_type=F32).astype(BF16)
        sent = jnp.broadcast_to(picked[None], (parties, longs, model))
        long_hidden = jnp.sum(lax.all_to_all(sent, "req", 0, 0), axis=0, dtype=F32).astype(BF16)
    gains = s_qk[None, :]
    with jax.named_scope("short_attention"):
        short_out, short_lse = call(
            short_kernel,
            [SMEM, SMEM] + [VMEM] * 5,
            (jax.ShapeDtypeStruct((rows, width), F32),) * 2,
            (10**9, 64 * 10**5),
            cache_lengths,
            local,
            hidden,
            w_qkv,
            gains,
            short_keys.reshape(rows * slots, width),
            short_values.reshape(rows * slots, width),
        )
    with jax.named_scope("long_attention"):
        partial = call(
            long_kernel,
            [VMEM] * 5,
            jax.ShapeDtypeStruct((parties, 2 * longs, width), F32),
            (10**8, 2 * 10**6),
            long_hidden,
            w_qkv,
            gains,
            long_keys.reshape(longs * span, width),
            long_values.reshape(longs * span, width),
        )
    with jax.named_scope("long_parts"):
        parts = lax.all_to_all(partial, "req", 0, 0)
    with jax.named_scope("project"):
        projected = call(
            project_kernel,
            [SMEM] + [VMEM] * 4,
            jax.ShapeDtypeStruct((rows, model), BF16),
            (2 * rows * width * model, 10**6),
            local,
            parts,
            short_out,
            short_lse,
            w_out,
        )
    with jax.named_scope("sum_heads"):
        projected = lax.all_gather(projected, "head")
    with jax.named_scope("mlp"):
        middle, downward = call(
            mlp_kernel,
            [VMEM] * 7,
            (jax.ShapeDtypeStruct((rows, model), BF16),) * 2,
            (10**8, 5 * 10**6),
            projected,
            hidden,
            alpha_attn[None, :],
            w_gate_up,
            s_gate[None, :],
            s_up[None, :],
            w_down,
        )
    with jax.named_scope("sum_units"):
        downward = lax.all_gather(downward, "head")
    with jax.named_scope("final"):
        return call(
            final_kernel,
            [VMEM] * 3,
            jax.ShapeDtypeStruct((rows, model), BF16),
            (10**6, 10**5),
            downward,
            middle,
            alpha_mlp[None, :],
        )


def solution(mesh):
    return jax.shard_map(
        on_device,
        mesh=mesh,
        in_specs=(
            P("req", None),
            P(None, None, "head"),
            P("head", None),
            P("head"),
            P(),
            P(None, None, "head"),
            P("head", None),
            P("head"),
            P("head"),
            P(),
            P("req", None, "head"),
            P("req", None, "head"),
            P("req"),
            P(None, "req", "head"),
            P(None, "req", "head"),
            P(),
        ),
        out_specs=P("req", None),
        check_vma=False,
    )
```

time: 156 us -> 62.3 us (0.40)
  blocking collectives: 137 us -> 11.5 us
  local copies, waits for them, and re-layouts: 4.47 us -> 27.6 us
  starting transfers between devices: 0 us -> 13.2 us
  matrix products: 10.6 us -> 1.02 us
  Pallas kernels: 0 us -> 7.14 us
  other arithmetic: 3.51 us -> 0.7 us
    all_gather x4 -> x2, blocking collectives: 115 us -> 11.5 us  [the longest x1 5.79 us: on_device(): downward = lax.all_gather(downward, 'head')]
    unnamed x24 -> x33, local copies, waits for them, and re-layouts: 0.46 us -> 26.9 us
    psum x2 -> x0, blocking collectives: 22.2 us -> none  [renormed_update(): lax.psum(partial_value.astype(jnp.bfloat16), 'head').astype(jnp.float32)]
    all_to_all x0 -> x2, starting transfers between devices: none -> 13.2 us  [the longest x1 7.25 us: on_device(): lax.all_to_all(sent, 'req', 0, 0)]
    dot_general x11 -> x1, matrix products: 10.6 us -> 1.02 us  [on_device(): picked = jnp.dot(matches, hidden, preferred_element_type=F32).astype(BF16)]
    pallas_call x0 -> x5, Pallas kernels: none -> 7.14 us  [call(): pl.pallas_call(kernel, in_specs=specs, out_specs=jax.tree.map(lambda _: V...]
    gather x4 -> x0, local copies, waits for them, and re-layouts: 1.78 us -> none  [the longest x2 0.66 us: on_device(): long_query = jnp.take(every_query, long_rows, axis=0)]
    slice x1 -> x0, local copies, waits for them, and re-layouts: 1.64 us -> none  [on_device(): query = jnp.dot(hidden, w_qkv[0], preferred_element_type=jnp.float32)]
  transfers between devices with their start and end apart: 0 -> 2, of which waited for: 0 -> 0; matrix products, arithmetic and copies ran while one was open for 0% -> 27% of each run, Pallas kernels for 0% -> 4%
where the time goes in v1:
time: 62.3 us; the launch traced here: 61.4 us
  local copies, waits for them, and re-layouts  27.6 us (44%)
  starting transfers between devices  13.2 us (21%)
  blocking collectives  11.5 us (18%)
  Pallas kernels  7.14 us (11%)
  matrix products  1.02 us (2%)
  other arithmetic  0.7 us (1%)
    unnamed x33, local copies, waits for them, and re-layouts  26.9 us
    all_to_all x1, starting transfers between devices, on_device(): lax.all_to_all(sent, 'req', 0, 0)  7.25 us
    pallas_call x5, Pallas kernels, call(): pl.pallas_call(kernel, in_specs=specs, out_specs=jax.tree.map(lambda _: V...  7.14 us
    all_to_all x1, starting transfers between devices, on_device(): parts = lax.all_to_all(partial, 'req', 0, 0)  6 us
    all_gather x1, blocking collectives, on_device(): downward = lax.all_gather(downward, 'head')  5.79 us
    all_gather x1, blocking collectives, on_device(): projected = lax.all_gather(projected, 'head')  5.74 us
  transfers between devices with their start and end apart: 2, of which 0 were waited for; matrix products, arithmetic and copies ran while one was open for 27% of the time, Pallas kernels for 4%

profile of v1, /device:TPU:0, one launch (start us, length us, event | category | flops | bytes accessed | tf_op | source)
XLA Modules:
  0.0 61.4 jit_solution(345953955461505080)
XLA Ops:
  0.0 0.7 %broadcast_subtract_fusion.local_ref = s32[4]{0:T(128)S(1)} fusion(s32[4]{0:T(128)} %param.31, s32[]{:T(128)S(6)} %mul.3), kind=kLoop, calls=%fused_computation.3 | loop fusion | flops 4 | bytes 36 | tf_op jit(solution)/shard_map/sub | solution.py:234
  0.7 1.0 %convolution_convert_fusion = bf16[4,1280]{1,0:T(4,128)(2,1)S(1)} fusion(bf16[24,1280]{1,0:T(8,128)(2,1)} %hidden_ref.3, s32[4]{0:T(128)S(1)} %broadcast_subtract_fusion.local_ref), kind=kOutput, calls=%fused_computation | convolution fusion | flops 250976 | bytes 71696 | tf_op jit(solution)/shard_map/long_hidden/dot_general | solution.py:237
  1.7 0.7 %broadcast_in_dim.23 = bf16[8,4,1280]{2,1,0:T(4,128)(2,1)} broadcast(bf16[4,1280]{1,0:T(4,128)(2,1)S(1)} %convolution_convert_fusion), dimensions={1,2} | broadcast | bytes 92160 | tf_op jit(solution)/shard_map/long_hidden/broadcast_in_dim | solution.py:238
  2.3 7.3 %all-to-all-start = ((bf16[8,4,1280]{2,1,0:T(4,128)(2,1)}), bf16[8,4,1280]{2,1,0:T(4,128)(2,1)S(1)}, u32[]{:S(2)}, u32[]{:S(2)}) async-start(bf16[8,4,1280]{2,1,0:T(4,128)(2,1)} %broadcast_in_dim.23), calls=%async_computation | async-start | bytes 163840 | tf_op jit(solution)/shard_map/long_hidden/all_to_all | solution.py:239
  9.6 4.0 %copy.32.w_ref = bf16[3,1280,320]{2,1,0:T(8,128)(2,1)S(1)} copy(bf16[3,1280,320]{1,2,0:T(8,128)(2,1)} %param.17) | data formatting | bytes 4915200 | tf_op args[1]
  13.6 0.0 copy-done.13
  13.7 2.3 %copy.30 = bf16[4,256,320]{2,1,0:T(8,128)(2,1)} copy(bf16[4,256,320]{1,2,0:T(8,128)(2,1)} %param.29) | data formatting | bytes 1310720 | tf_op args[13]
  15.9 2.3 %copy.31 = bf16[4,256,320]{2,1,0:T(8,128)(2,1)} copy(bf16[4,256,320]{1,2,0:T(8,128)(2,1)} %param.30) | data formatting | bytes 1310720 | tf_op args[14]
  18.2 0.0 all-to-all-done
  18.3 1.1 %copy-done.3 = bf16[4,256,320]{2,1,0:T(8,128)(2,1)S(1)} copy-done((bf16[4,256,320]{2,1,0:T(8,128)(2,1)S(1)}, bf16[4,256,320]{2,1,0:T(8,128)(2,1)}, u32[]{:S(2)}) %copy-start.3) | copy-done | bytes 655384
  19.4 1.1 %copy-done.4 = bf16[4,256,320]{2,1,0:T(8,128)(2,1)S(1)} copy-done((bf16[4,256,320]{2,1,0:T(8,128)(2,1)S(1)}, bf16[4,256,320]{2,1,0:T(8,128)(2,1)}, u32[]{:S(2)}) %copy-start.4) | copy-done | bytes 655384
  20.5 1.6 %long_attention.1 = f32[8,8,320]{2,1,0:T(8,128)} custom-call(bf16[4,1280]{1,0:T(4,128)(2,1)S(1)} %reduce_sum.12.hidden_ref, bf16[3,1280,320]{2,1,0:T(8,128)(2,1)S(1)} %copy.32.w_ref, f32[1,320]{1,0:T(1,128)S(1)} %broadcast_in_dim.24.gains_ref, bf16[1024,320]{1,0:T(8,128)(2,1)S(1)} %bitcast.9, bf16[1024,320]{1,0:T(8,128)(2,1)S(1)} %bitcast.10), custom_call_target="tpu_custom_call" | custom-call | flops 100000000 | bytes 2000000 | tf_op jit(solution)/shard_map/long_attention/pallas_call | solution.py:201
  22.2 6.0 %all-to-all-start.1 = ((f32[8,8,320]{2,1,0:T(8,128)}), f32[8,8,320]{2,1,0:T(8,128)S(1)}, u32[]{:S(2)}, u32[]{:S(2)}) async-start(f32[8,8,320]{2,1,0:T(8,128)} %long_attention.1), calls=%async_computation.1 | async-start | bytes 196608 | tf_op jit(solution)/shard_map/long_parts/all_to_all | solution.py:268
  28.1 4.1 %copy.33 = bf16[24,128,320]{2,1,0:T(8,128)(2,1)} copy(bf16[24,128,320]{1,2,0:T(8,128)(2,1)} %param.26) | data formatting | bytes 3932160 | tf_op args[10]
  32.3 0.0 copy-start.7
  32.3 0.0 copy-start.8
  32.3 4.2 %copy.34 = bf16[24,128,320]{2,1,0:T(8,128)(2,1)} copy(bf16[24,128,320]{1,2,0:T(8,128)(2,1)} %param.27) | data formatting | bytes 3932160 | tf_op args[11]
  36.4 0.0 copy-done.9
  36.4 0.0 copy-done.11
  36.5 1.7 %copy-done = bf16[24,128,320]{2,1,0:T(8,128)(2,1)S(1)} copy-done((bf16[24,128,320]{2,1,0:T(8,128)(2,1)S(1)}, bf16[24,128,320]{2,1,0:T(8,128)(2,1)}, u32[]{:S(2)}) %copy-start) | copy-done | bytes 1966104
  38.2 1.7 %copy-done.1 = bf16[24,128,320]{2,1,0:T(8,128)(2,1)S(1)} copy-done((bf16[24,128,320]{2,1,0:T(8,128)(2,1)S(1)}, bf16[24,128,320]{2,1,0:T(8,128)(2,1)}, u32[]{:S(2)}) %copy-start.1) | copy-done | bytes 1966104
  39.9 2.7 %short_attention.1 = (f32[24,320]{1,0:T(8,128)S(1)}, f32[24,320]{1,0:T(8,128)S(1)}) custom-call(s32[24]{0:T(128)S(1)} %copy-done.8, s32[4]{0:T(128)S(1)} %broadcast_subtract_fusion.local_ref, bf16[24,1280]{1,0:T(8,128)(2,1)S(1)} %copy-done.7, bf16[3,1280,320]{2,1,0:T(8,128)(2,1)S(1)} %copy.32.w_ref, f32[1,320]{1,0:T(1,128)S(1)} %broadcast_in_dim.24.gains_ref, ...), custom_call_target="tpu_custom_call" | custom-call | flops 1000000000 | bytes 6400000 | tf_op jit(solution)/shard_map/short_attention/pallas_call | solution.py:201
  42.5 0.0 all-to-all-done.1.parts_ref
  42.6 0.0 copy-start.6
  42.6 1.1 %copy-done.6 = bf16[320,1280]{1,0:T(8,128)(2,1)S(1)} copy-done((bf16[320,1280]{1,0:T(8,128)(2,1)S(1)}, bf16[320,1280]{1,0:T(8,128)(2,1)}, u32[]{:S(2)}) %copy-start.6) | copy-done | bytes 819224
  43.7 0.8 %project.1 = bf16[24,1280]{1,0:T(8,128)(2,1)S(1)} custom-call(s32[4]{0:T(128)S(1)} %broadcast_subtract_fusion.local_ref, f32[8,8,320]{2,1,0:T(8,128)S(1)} %all-to-all-done.1.parts_ref, f32[24,320]{1,0:T(8,128)S(1)} %get-tuple-element.9.short_ref, f32[24,320]{1,0:T(8,128)S(1)} %get-tuple-element.10.lse_ref, bf16[320,1280]{1,0:T(8,128)(2,1)S(1)} %copy-done.6), custom_call_target="tpu_custom_call" | custom-call | flops 19660800 | bytes 1000000 | tf_op jit(solution)/shard_map/project/pallas_call | solution.py:201
  44.6 5.7 %all-gather = bf16[96,1280]{1,0:T(8,128)(2,1)S(1)} all-gather(bf16[24,1280]{1,0:T(8,128)(2,1)S(1)} %project.1), channel_id=2, replica_groups=mesh['req'=8,'head'=4] {'head'}, dimensions={0}, use_global_device_ids=true | all-gather | bytes 307200 | tf_op jit(solution)/shard_map/sum_heads/all_gather | solution.py:282
  50.3 1.9 %copy-done.2 = bf16[2,1280,640]{2,1,0:T(8,128)(2,1)S(1)} copy-done((bf16[2,1280,640]{2,1,0:T(8,128)(2,1)S(1)}, bf16[2,1280,640]{2,1,0:T(8,128)(2,1)}, u32[]{:S(2)}) %copy-start.2) | copy-done | bytes 3276824
  52.2 1.4 %copy-done.5 = bf16[640,1280]{1,0:T(8,128)(2,1)S(1)} copy-done((bf16[640,1280]{1,0:T(8,128)(2,1)S(1)}, bf16[640,1280]{1,0:T(8,128)(2,1)}, u32[]{:S(2)}) %copy-start.5) | copy-done | bytes 1638424
  53.7 1.1 %mlp.1 = (bf16[24,1280]{1,0:T(8,128)(2,1)S(1)}, bf16[24,1280]{1,0:T(8,128)(2,1)S(1)}) custom-call(bf16[4,24,1280]{2,1,0:T(8,128)(2,1)S(1)} %bitcast.11, bf16[24,1280]{1,0:T(8,128)(2,1)S(1)} %copy-done.7, f32[1,1280]{1,0:T(1,128)S(1)} %broadcast_in_dim.25.alpha_ref, bf16[2,1280,640]{2,1,0:T(8,128)(2,1)S(1)} %copy-done.2, ...), custom_call_target="tpu_custom_call" | custom-call | flops 100000000 | bytes 5000000 | tf_op jit(solution)/shard_map/mlp/pallas_call | solution.py:201
  54.8 5.8 %all-gather.1 = bf16[96,1280]{1,0:T(8,128)(2,1)S(1)} all-gather(bf16[24,1280]{1,0:T(8,128)(2,1)S(1)} %get-tuple-element.11), channel_id=3, replica_groups=mesh['req'=8,'head'=4] {'head'}, dimensions={0}, use_global_device_ids=true | all-gather | bytes 307200 | tf_op jit(solution)/shard_map/sum_units/all_gather | solution.py:298
  60.6 0.9 %final.1 = bf16[24,1280]{1,0:T(8,128)(2,1)} custom-call(bf16[4,24,1280]{2,1,0:T(8,128)(2,1)S(1)} %bitcast.12, bf16[24,1280]{1,0:T(8,128)(2,1)S(1)} %get-tuple-element.12.mid_ref, f32[1,1280]{1,0:T(1,128)S(1)} %broadcast_in_dim.28.alpha_ref), custom_call_target="tpu_custom_call" | custom-call | flops 1000000 | bytes 100000 | tf_op jit(solution)/shard_map/final/pallas_call | solution.py:201
  (21 shorter events, 0.1 us)
Async XLA Ops:
  2.3 15.9 %all-to-all-start = ((bf16[8,4,1280]{2,1,0:T(4,128)(2,1)}), bf16[8,4,1280]{2,1,0:T(4,128)(2,1)S(1)}, u32[]{:S(2)}, u32[]{:S(2)}) async-start(bf16[8,4,1280]{2,1,0:T(4,128)(2,1)} %broadcast_in_dim.23), calls=%async_computation | async-start | bytes 163840 | tf_op jit(solution)/shard_map/long_hidden/all_to_all | solution.py:239
  9.6 4.1 %copy-start.13 = (f32[320]{0:T(512)S(1)}, f32[320]{0:T(512)}, u32[]{:S(2)}) copy-start(f32[320]{0:T(512)} %param.19) | copy-start | bytes 3844
  18.2 1.1 %copy-start.3 = (bf16[4,256,320]{2,1,0:T(8,128)(2,1)S(1)}, bf16[4,256,320]{2,1,0:T(8,128)(2,1)}, u32[]{:S(2)}) copy-start(bf16[4,256,320]{2,1,0:T(8,128)(2,1)} %copy.30) | copy-start | bytes 1966084
  19.4 1.1 %copy-start.4 = (bf16[4,256,320]{2,1,0:T(8,128)(2,1)S(1)}, bf16[4,256,320]{2,1,0:T(8,128)(2,1)}, u32[]{:S(2)}) copy-start(bf16[4,256,320]{2,1,0:T(8,128)(2,1)} %copy.31) | copy-start | bytes 1966084
  22.2 20.4 %all-to-all-start.1 = ((f32[8,8,320]{2,1,0:T(8,128)}), f32[8,8,320]{2,1,0:T(8,128)S(1)}, u32[]{:S(2)}, u32[]{:S(2)}) async-start(f32[8,8,320]{2,1,0:T(8,128)} %long_attention.1), calls=%async_computation.1 | async-start | bytes 196608 | tf_op jit(solution)/shard_map/long_parts/all_to_all | solution.py:268
  32.2 4.2 %copy-start.9 = (f32[1280]{0:T(1024)S(1)}, f32[1280]{0:T(1024)}, u32[]{:S(2)}) copy-start(f32[1280]{0:T(1024)} %param.20) | copy-start | bytes 15364
  32.2 4.2 %copy-start.11 = (f32[640]{0:T(1024)S(1)}, f32[640]{0:T(1024)}, u32[]{:S(2)}) copy-start(f32[640]{0:T(1024)} %param.24) | copy-start | bytes 7684
  32.2 4.2 %copy-start.12 = (f32[640]{0:T(1024)S(1)}, f32[640]{0:T(1024)}, u32[]{:S(2)}) copy-start(f32[640]{0:T(1024)} %param.23) | copy-start | bytes 7684
  32.2 4.2 %copy-start.10 = (f32[1280]{0:T(1024)S(1)}, f32[1280]{0:T(1024)}, u32[]{:S(2)}) copy-start(f32[1280]{0:T(1024)} %param.25) | copy-start | bytes 15364
  32.3 4.3 %copy-start.7 = (bf16[24,1280]{1,0:T(8,128)(2,1)S(1)}, bf16[24,1280]{1,0:T(8,128)(2,1)}, u32[]{:S(2)}) copy-start(bf16[24,1280]{1,0:T(8,128)(2,1)} %hidden_ref.3) | copy-start | bytes 184324
  32.3 4.3 %copy-start.8 = (s32[24]{0:T(128)S(1)}, s32[24]{0:T(128)}, u32[]{:S(2)}) copy-start(s32[24]{0:T(128)} %lengths_ref.1) | copy-start | bytes 292
  36.5 1.7 %copy-start = (bf16[24,128,320]{2,1,0:T(8,128)(2,1)S(1)}, bf16[24,128,320]{2,1,0:T(8,128)(2,1)}, u32[]{:S(2)}) copy-start(bf16[24,128,320]{2,1,0:T(8,128)(2,1)} %copy.33) | copy-start | bytes 5898244
  38.2 1.7 %copy-start.1 = (bf16[24,128,320]{2,1,0:T(8,128)(2,1)S(1)}, bf16[24,128,320]{2,1,0:T(8,128)(2,1)}, u32[]{:S(2)}) copy-start(bf16[24,128,320]{2,1,0:T(8,128)(2,1)} %copy.34) | copy-start | bytes 5898244
  42.6 1.1 %copy-start.6 = (bf16[320,1280]{1,0:T(8,128)(2,1)S(1)}, bf16[320,1280]{1,0:T(8,128)(2,1)}, u32[]{:S(2)}) copy-start(bf16[320,1280]{1,0:T(8,128)(2,1)} %w_ref.3) | copy-start | bytes 2457604
  50.3 1.9 %copy-start.2 = (bf16[2,1280,640]{2,1,0:T(8,128)(2,1)S(1)}, bf16[2,1280,640]{2,1,0:T(8,128)(2,1)}, u32[]{:S(2)}) copy-start(bf16[2,1280,640]{2,1,0:T(8,128)(2,1)} %w_gate_up_ref.1) | copy-start | bytes 9830404
  52.2 1.4 %copy-start.5 = (bf16[640,1280]{1,0:T(8,128)(2,1)S(1)}, bf16[640,1280]{1,0:T(8,128)(2,1)}, u32[]{:S(2)}) copy-start(bf16[640,1280]{1,0:T(8,128)(2,1)} %w_down_ref.1) | copy-start | bytes 4915204

commit v2 on v1

v2 whole, which is shorter than its diff:
```python
import math

import jax
import jax.numpy as jnp
from jax import lax
from jax.experimental import pallas as pl
from jax.experimental.pallas import tpu as pltpu
from jax.sharding import PartitionSpec as P

HEAD_DIM = 64
EPS = 1e-06
LOW = -1e30
F32 = jnp.float32
BF16 = jnp.bfloat16
LANES = 8

VMEM = pl.BlockSpec(memory_space=pltpu.VMEM)
HBM = pl.BlockSpec(memory_space=pltpu.HBM)


def dot(left, right):
    return jnp.dot(left, right, preferred_element_type=F32)


def dot_t(left, right):
    return lax.dot_general(left, right, (((1,), (1,)), ((), ())), preferred_element_type=F32)


def head_masks(width):
    lane = lax.broadcasted_iota(jnp.int32, (1, width), 1)
    return [
        (lane >= h * HEAD_DIM) & (lane < (h + 1) * HEAD_DIM) for h in range(width // HEAD_DIM)
    ]


def head_rows(width):
    sub = lax.broadcasted_iota(jnp.int32, (LANES, width), 0)
    lane = lax.broadcasted_iota(jnp.int32, (LANES, width), 1)
    return (lane >= sub * HEAD_DIM) & (lane < (sub + 1) * HEAD_DIM)


def head_unit(values, gains, masks):
    squares = values * values
    scale = jnp.zeros_like(values)
    for mask in masks:
        total = jnp.sum(jnp.where(mask, squares, 0.0), axis=-1, keepdims=True)
        scale = jnp.where(mask, lax.rsqrt(total + EPS), scale)
    return (values * scale * gains).astype(BF16).astype(F32)


def row_norm(values):
    return values * lax.rsqrt(jnp.mean(values * values, axis=-1, keepdims=True) + EPS)


def gathered(values, diagonal):
    return jnp.sum(jnp.where(diagonal, values, 0.0), axis=0, keepdims=True)


def start_all(pairs, sems):
    copies = [pltpu.make_async_copy(s, d, sems.at[i]) for i, (s, d) in enumerate(pairs)]
    for copy in copies:
        copy.start()
    return copies


def select_kernel(
    longs_hbm,
    hidden_hbm,
    w_hbm,
    keys_hbm,
    values_hbm,
    sent_hbm,
    hidden_ref,
    w_query_ref,
    keys_ref,
    values_ref,
    longs_ref,
    sent_ref,
    sems,
):
    copies = start_all(
        [
            (longs_hbm, longs_ref),
            (hidden_hbm, hidden_ref),
            (w_hbm.at[0], w_query_ref),
            (keys_hbm, keys_ref),
            (values_hbm, values_ref),
        ],
        sems,
    )
    parties, longs, _ = sent_ref.shape
    rows = hidden_ref.shape[0]
    offset = lax.axis_index("req") * rows
    sub = lax.broadcasted_iota(jnp.int32, (8, rows), 0)
    lane = lax.broadcasted_iota(jnp.int32, (8, rows), 1) + offset
    here = jnp.zeros((8, rows), jnp.bool_)
    copies[0].wait()
    for index in range(longs):
        here = here | ((sub == index) & (lane == longs_ref[index]))
    copies[1].wait()
    picked = dot(here.astype(F32).astype(BF16), hidden_ref[...])[:longs].astype(BF16)
    for party in range(parties):
        sent_ref[party] = picked
    out = pltpu.make_async_copy(sent_ref, sent_hbm, sems.at[5])
    out.start()
    out.wait()
    for copy in copies[2:]:
        copy.wait()


def qkv_kernel(
    gains_hbm,
    w_hbm,
    hidden_ref,
    w_query_ref,
    query_ref,
    key_ref,
    value_ref,
    gains_ref,
    w_key_ref,
    w_value_ref,
    sems,
):
    copies = start_all(
        [(gains_hbm, gains_ref), (w_hbm.at[1], w_key_ref), (w_hbm.at[2], w_value_ref)], sems
    )
    masks = head_masks(query_ref.shape[1])
    hidden = hidden_ref[...]
    query = dot_t(hidden, w_query_ref[...])
    copies[0].wait()
    gains = gains_ref[...][None, :]
    query_ref[...] = head_unit(query, gains, masks) * math.sqrt(HEAD_DIM)
    copies[1].wait()
    key_ref[...] = head_unit(dot_t(hidden, w_key_ref[...]), gains, masks)
    copies[2].wait()
    value_ref[...] = dot_t(hidden, w_value_ref[...]).astype(BF16).astype(F32)


def long_kernel(
    received_ref,
    gains_ref,
    w_ref,
    keys_ref,
    values_ref,
    sent_hbm,
    sent_ref,
    sems,
):
    parties, longs, _ = received_ref.shape
    width = w_ref.shape[0]
    hidden = received_ref[0].astype(F32)
    for party in range(1, parties):
        hidden = hidden + received_ref[party].astype(F32)
    query = dot_t(hidden.astype(BF16), w_ref[...])
    query = head_unit(query, gains_ref[...][None, :], head_masks(width)) * math.sqrt(HEAD_DIM)
    diagonal = head_rows(width)
    scores = [
        dot(jnp.where(diagonal, query[i : i + 1], 0.0).astype(BF16), keys_ref[i])
        for i in range(longs)
    ]
    outs, lses = [], []
    for i in range(longs):
        top = jnp.max(scores[i], axis=-1, keepdims=True)
        weights = jnp.exp(scores[i] - top)
        total = jnp.sum(weights, axis=-1, keepdims=True)
        summed = dot_t(weights.astype(BF16), values_ref[i])
        outs.append(gathered(summed / total, diagonal))
        lses.append(gathered(top + jnp.log(total), diagonal))
    packed = jnp.concatenate(outs + lses, axis=0)
    for party in range(parties):
        sent_ref[party] = packed
    out = pltpu.make_async_copy(sent_ref, sent_hbm, sems.at[0])
    out.start()
    out.wait()


def short_kernel(
    lengths_hbm,
    longs_hbm,
    keys_hbm,
    values_hbm,
    w_out_hbm,
    query_ref,
    key_ref,
    value_ref,
    out_ref,
    lse_ref,
    match_ref,
    w_out_ref,
    lengths_ref,
    longs_ref,
    keys_ref,
    values_ref,
    sems,
):
    rows, width = out_ref.shape
    slots = keys_ref.shape[2]
    longs = longs_ref.shape[0]
    group = 8
    parts = [pl.ds(start, group) for start in range(0, rows, group)]
    copies = start_all(
        [(lengths_hbm, lengths_ref), (longs_hbm, longs_ref)]
        + [(keys_hbm.at[part], keys_ref.at[part]) for part in parts]
        + [(values_hbm.at[part], values_ref.at[part]) for part in parts]
        + [(w_out_hbm, w_out_ref)],
        sems,
    )
    key_copies = copies[2 : 2 + len(parts)]
    value_copies = copies[2 + len(parts) : -1]
    offset = lax.axis_index("req") * rows
    diagonal = head_rows(width)
    sub = lax.broadcasted_iota(jnp.int32, (2 * LANES, 2 * slots), 0)
    lane = lax.broadcasted_iota(jnp.int32, (2 * LANES, 2 * slots), 1)
    second = sub >= LANES
    first = jnp.where(second, slots, 0)
    query = query_ref[...]
    key = key_ref[...]
    value = value_ref[...]
    pairs, owns = [], []
    for r in range(0, rows, 2):
        pair = jnp.concatenate(
            [jnp.where(diagonal, query[r + i : r + i + 1], 0.0) for i in range(2)], axis=0
        )
        new = jnp.concatenate(
            [jnp.where(diagonal, key[r + i : r + i + 1], 0.0) for i in range(2)], axis=0
        )
        owns.append(jnp.sum(pair * new, axis=-1, keepdims=True))
        pairs.append(pair.astype(BF16))
    copies[0].wait()
    copies[1].wait()
    row = lax.broadcasted_iota(jnp.int32, match_ref.shape, 0) + offset
    column = lax.broadcasted_iota(jnp.int32, match_ref.shape, 1)
    match = jnp.zeros(match_ref.shape, F32)
    for index in range(longs):
        match = jnp.where((row == longs_ref[index]) & (column == index), 1.0, match)
    match_ref[...] = match
    weights, scales, fresh = [], [], []
    for p, r in enumerate(range(0, rows, 2)):
        if r % group == 0:
            key_copies[r // group].wait()
        scores = dot(pairs[p], jnp.concatenate([keys_ref[r], keys_ref[r + 1]], axis=1))
        lengths = []
        for i in range(2):
            length = lengths_ref[r + i]
            for index in range(longs):
                length = jnp.where(longs_ref[index] == offset + r + i, 0, length)
            lengths.append(length)
        valid = (lane >= first) & (lane < jnp.where(second, slots + lengths[1], lengths[0]))
        scores = jnp.where(valid, scores, LOW)
        top = jnp.maximum(jnp.max(scores, axis=-1, keepdims=True), owns[p])
        weight = jnp.where(valid, jnp.exp(scores - top), 0.0)
        own = jnp.exp(owns[p] - top)
        total = jnp.sum(weight, axis=-1, keepdims=True) + own
        weights.append(weight.astype(BF16))
        scales.append(total)
        fresh.append(own.astype(BF16).astype(F32))
        lse = top + jnp.log(total)
        for i in range(2):
            part = slice(i * LANES, (i + 1) * LANES)
            lse_ref[r + i : r + i + 1, :] = gathered(lse[part], diagonal)
    for p, r in enumerate(range(0, rows, 2)):
        if r % group == 0:
            value_copies[r // group].wait()
        summed = dot_t(
            weights[p], jnp.concatenate([values_ref[r], values_ref[r + 1]], axis=1)
        )
        for i in range(2):
            part = slice(i * LANES, (i + 1) * LANES)
            acc = summed[part] + fresh[p][part] * value[r + i : r + i + 1]
            out_ref[r + i : r + i + 1, :] = gathered(acc / scales[p][part], diagonal)
    copies[-1].wait()


def project_kernel(parts_ref, short_ref, lse_ref, match_ref, w_ref, out_ref):
    parties, doubled, width = parts_ref.shape
    longs = doubled // 2
    rows = short_ref.shape[0]
    top = parts_ref[0]
    for party in range(1, parties):
        top = jnp.maximum(top, parts_ref[party])
    top = top[longs:]
    total = jnp.zeros((longs, width), F32)
    acc = jnp.zeros((longs, width), F32)
    for party in range(parties):
        part = parts_ref[party]
        weight = jnp.exp(part[longs:] - top)
        total = total + weight
        acc = acc + weight * part[:longs]
    long_out = acc / total
    long_lse = top + jnp.log(total)
    placed = jnp.zeros((rows, width), F32)
    placed_lse = jnp.full((rows, width), LOW, F32)
    for index in range(longs):
        here = match_ref[:, index : index + 1] > 0.5
        placed = jnp.where(here, long_out[index : index + 1], placed)
        placed_lse = jnp.where(here, long_lse[index : index + 1], placed_lse)
    short_lse = lse_ref[...]
    top = jnp.maximum(short_lse, placed_lse)
    near = jnp.exp(short_lse - top)
    far = jnp.exp(placed_lse - top)
    attended = (near * short_ref[...] + far * placed) / (near + far)
    out_ref[...] = dot(attended.astype(BF16), w_ref[...]).astype(BF16)


def load_kernel(*refs):
    count = (len(refs) - 2) // 2
    copies = start_all(list(zip(refs[:count], refs[count + 1 : -1])), refs[-1])
    for copy in copies:
        copy.wait()


def add_kernel(left_ref, right_ref, *refs):
    out_ref = refs[-1]
    out_ref[...] = (left_ref[...].astype(F32) + right_ref[...].astype(F32)).astype(BF16)


def renormed(left_ref, right_ref, base, alpha_ref):
    total = left_ref[...].astype(F32) + right_ref[...].astype(F32)
    alpha = alpha_ref[...][None, :]
    return row_norm(base + alpha * (row_norm(total) - base)).astype(BF16)


def mlp_kernel(
    left_ref,
    right_ref,
    hidden_ref,
    alpha_ref,
    w_gate_up_ref,
    w_down_ref,
    s_gate_ref,
    s_up_ref,
    mid_ref,
    out_ref,
):
    middle = renormed(left_ref, right_ref, hidden_ref[...].astype(F32), alpha_ref)
    mid_ref[...] = middle
    gate = dot(middle, w_gate_up_ref[0]) * s_gate_ref[...][None, :]
    upward = dot(middle, w_gate_up_ref[1]) * s_up_ref[...][None, :]
    gated = (gate / (1.0 + jnp.exp(-gate)) * upward).astype(BF16)
    out_ref[...] = dot(gated, w_down_ref[...]).astype(BF16)


def final_kernel(left_ref, right_ref, mid_ref, alpha_ref, out_ref):
    out_ref[...] = renormed(left_ref, right_ref, mid_ref[...].astype(F32), alpha_ref)


def call(kernel, outs, cost, far=(), near=(), out_far=(), scratch=(), copies=0):
    far = [pltpu.with_memory_space_constraint(a, pltpu.HBM) for a in far]
    return pl.pallas_call(
        kernel,
        in_specs=[HBM] * len(far) + [VMEM] * len(near),
        out_specs=[HBM] * len(out_far) + [VMEM] * len(outs),
        out_shape=[pltpu.HBM(a.shape, a.dtype) for a in out_far] + list(outs),
        scratch_shapes=list(scratch) + [pltpu.SemaphoreType.DMA((copies,))] * (copies > 0),
        cost_estimate=pl.CostEstimate(flops=cost[0], bytes_accessed=cost[1], transcendentals=0),
        compiler_params=pltpu.CompilerParams(vmem_limit_bytes=32 * 1024 * 1024),
    )(*far, *near)


def like(array):
    return jax.ShapeDtypeStruct(array.shape, array.dtype)


def exchanged(value, step):
    places = lax.axis_size("head")
    return lax.ppermute(value, "head", [(i, i ^ step) for i in range(places)])


def on_device(
    hidden,
    w_qkv,
    w_out,
    s_qk,
    alpha_attn,
    w_gate_up,
    w_down,
    s_up,
    s_gate,
    alpha_mlp,
    short_keys,
    short_values,
    cache_lengths,
    long_keys,
    long_values,
    long_rows,
):
    rows, model = hidden.shape
    width = w_qkv.shape[2]
    longs = long_keys.shape[0]
    parties = lax.axis_size("req")
    shape = jax.ShapeDtypeStruct
    state = shape((rows, width), F32)
    wide = shape((rows, model), BF16)
    w_qkv, short_keys, short_values, long_keys, long_values = (
        jnp.swapaxes(a, 1, 2) for a in (w_qkv, short_keys, short_values, long_keys, long_values)
    )
    with jax.named_scope("long_hidden"):
        sent, hidden_near, w_query, keys, values = call(
            select_kernel,
            (wide, shape(w_qkv.shape[1:], BF16), like(long_keys), like(long_values)),
            (10**6, 3 * 10**6),
            far=(long_rows, hidden, w_qkv, long_keys, long_values),
            out_far=(shape((parties, longs, model), BF16),),
            scratch=(pltpu.SMEM((longs,), jnp.int32), pltpu.VMEM((parties, longs, model), BF16)),
            copies=6,
        )
        received = lax.all_to_all(sent, "req", 0, 0)
    with jax.named_scope("qkv"):
        query, key, value, gains = call(
            qkv_kernel,
            (state, state, state, like(s_qk)),
            (10**8, 4 * 10**6),
            far=(s_qk, w_qkv),
            near=(hidden_near, w_query),
            scratch=(pltpu.VMEM(w_qkv.shape[1:], BF16),) * 2,
            copies=3,
        )
    with jax.named_scope("long_attention"):
        (partial,) = call(
            long_kernel,
            (),
            (10**8, 4 * 10**6),
            near=(received, gains, w_query, keys, values),
            out_far=(shape((parties, 2 * longs, width), F32),),
            scratch=(pltpu.VMEM((parties, 2 * longs, width), F32),),
            copies=1,
        )
    with jax.named_scope("long_parts"):
        parts = lax.all_to_all(partial, "req", 0, 0)
    with jax.named_scope("short_attention"):
        short_out, short_lse, match, w_out = call(
            short_kernel,
            (state, state, shape((rows, 128), F32), like(w_out)),
            (10**9, 6 * 10**6),
            far=(cache_lengths, long_rows, short_keys, short_values, w_out),
            near=(query, key, value),
            scratch=(
                pltpu.SMEM((rows,), jnp.int32),
                pltpu.SMEM((longs,), jnp.int32),
                pltpu.VMEM(short_keys.shape, BF16),
                pltpu.VMEM(short_values.shape, BF16),
            ),
            copies=3 + 2 * (rows // 8),
        )
    with jax.named_scope("project"):
        (projected,) = call(
            project_kernel,
            (wide,),
            (2 * rows * width * model, 10**6),
            near=(parts, short_out, short_lse, match, w_out),
        )
    with jax.named_scope("load"):
        loads = (hidden, alpha_attn, w_gate_up, w_down, s_gate, s_up, alpha_mlp)
        hidden, alpha_attn, w_gate_up, w_down, s_gate, s_up, alpha_mlp = call(
            load_kernel,
            [like(a) for a in loads],
            (10**6, 6 * 10**6),
            far=loads,
            near=(projected,),
            copies=len(loads),
        )
    with jax.named_scope("sum_heads"):
        other = exchanged(projected, 3)
        (projected,) = call(add_kernel, (wide,), (10**5, 10**5), near=(projected, other, s_up))
        other = exchanged(projected, 1)
    with jax.named_scope("mlp"):
        middle, downward = call(
            mlp_kernel,
            (wide, wide),
            (10**8, 5 * 10**6),
            near=(projected, other, hidden, alpha_attn, w_gate_up, w_down, s_gate, s_up),
        )
    with jax.named_scope("sum_units"):
        other = exchanged(downward, 3)
        (downward,) = call(add_kernel, (wide,), (10**5, 10**5), near=(downward, other))
        other = exchanged(downward, 1)
    with jax.named_scope("final"):
        (updated,) = call(
            final_kernel, (wide,), (10**6, 10**5), near=(downward, other, middle, alpha_mlp)
        )
        return updated


def solution(mesh):
    return jax.shard_map(
        on_device,
        mesh=mesh,
        in_specs=(
            P("req", None),
            P(None, None, "head"),
            P("head", None),
            P("head"),
            P(),
            P(None, None, "head"),
            P("head", None),
            P("head"),
            P("head"),
            P(),
            P("req", None, "head"),
            P("req", None, "head"),
            P("req"),
            P(None, "req", "head"),
            P(None, "req", "head"),
            P(),
        ),
        out_specs=P("req", None),
        check_vma=False,
    )
```

time: 62.3 us -> 41.7 us (0.67)
  local copies, waits for them, and re-layouts: 27.6 us -> 0 us
  waiting for transfers between devices: 0.01 us -> 15.5 us
  blocking collectives: 11.5 us -> 0 us
  Pallas kernels: 7.14 us -> 13.9 us
  starting transfers between devices: 13.2 us -> 11.8 us
  matrix products: 1.02 us -> 0 us
  other arithmetic: 0.7 us -> 0 us
    unnamed x33 -> x0, local copies, waits for them, and re-layouts: 26.9 us -> none
    all_gather x2 -> x0, blocking collectives: 11.5 us -> none  [the longest x1 5.79 us: on_device(): downward = lax.all_gather(downward, 'head')]
    ppermute x0 -> x4, waiting for transfers between devices: none -> 7.15 us  [exchanged(): return lax.ppermute(value, 'head', [(i, i ^ step) for i in range(places)])]
    pallas_call x5 -> x10, Pallas kernels: 7.14 us -> 13.9 us  [call(): pl.pallas_call(kernel, in_specs=[HBM] * len(far) + [VMEM] * len(near), ou...]
    all_to_all x1, waiting for transfers between devices: 0.01 us -> 4.63 us  [on_device(): received = lax.all_to_all(sent, 'req', 0, 0)]
    all_to_all x1, waiting for transfers between devices: 0.01 us -> 3.73 us  [on_device(): parts = lax.all_to_all(partial, 'req', 0, 0)]
    all_to_all x1, starting transfers between devices: 6 us -> 3.37 us  [on_device(): parts = lax.all_to_all(partial, 'req', 0, 0)]
    ppermute x0 -> x4, starting transfers between devices: none -> 1.21 us  [exchanged(): return lax.ppermute(value, 'head', [(i, i ^ step) for i in range(places)])]
  transfers between devices with their start and end apart: 2 -> 6, of which waited for: 0 -> 6; matrix products, arithmetic and copies ran while one was open for 27% -> 0% of each run, Pallas kernels for 4% -> 20%
where the time goes in v2:
time: 41.7 us; the launch traced here: 41.3 us
  waiting for transfers between devices  15.5 us (37%)
  Pallas kernels  13.9 us (33%)
  starting transfers between devices  11.8 us (28%)
    pallas_call x10, Pallas kernels, call(): pl.pallas_call(kernel, in_specs=[HBM] * len(far) + [VMEM] * len(near), ou...  13.9 us
    all_to_all x1, starting transfers between devices, on_device(): received = lax.all_to_all(sent, 'req', 0, 0)  7.26 us
    ppermute x4, waiting for transfers between devices, exchanged(): return lax.ppermute(value, 'head', [(i, i ^ step) for i in range(places)])  7.15 us
    all_to_all x1, waiting for transfers between devices, on_device(): received = lax.all_to_all(sent, 'req', 0, 0)  4.63 us
    all_to_all x1, waiting for transfers between devices, on_device(): parts = lax.all_to_all(partial, 'req', 0, 0)  3.73 us
    all_to_all x1, starting transfers between devices, on_device(): parts = lax.all_to_all(partial, 'req', 0, 0)  3.37 us
    ppermute x4, starting transfers between devices, exchanged(): return lax.ppermute(value, 'head', [(i, i ^ step) for i in range(places)])  1.21 us
  transfers between devices with their start and end apart: 6, of which 6 were waited for; matrix products, arithmetic and copies ran while one was open for 0% of the time, Pallas kernels for 20%

profile of v2, /device:TPU:0, one launch (start us, length us, event | category | flops | bytes accessed | tf_op | source)
XLA Modules:
  0.0 41.3 jit_solution(16613707610528556904)
XLA Ops:
  0.0 1.6 %long_hidden.1 = (bf16[8,4,1280]{2,1,0:T(4,128)(2,1)}, bf16[24,1280]{1,0:T(8,128)(2,1)S(1)}, bf16[320,1280]{1,0:T(8,128)(2,1)S(1)}, bf16[4,320,256]{2,1,0:T(8,128)(2,1)S(1)}, bf16[4,320,256]{2,1,0:T(8,128)(2,1)S(1)}) custom-call(s32[4]{0:T(128)} %longs_hbm.3, bf16[24,1280]{1,0:T(8,128)(2,1)} %refs_0_.1, bf16[3,320,1280]{2,1,0:T(8,128)(2,1)} %bitcast.5, ...), custom_call_target="tpu_custom_call" | custom-call | flops 1000000 | bytes 3000000 | tf_op jit(solution)/shard_map/long_hidden/pallas_call | solution.py:349
  1.7 7.3 %all-to-all-start = ((bf16[8,4,1280]{2,1,0:T(4,128)(2,1)}), bf16[8,4,1280]{2,1,0:T(4,128)(2,1)S(1)}, u32[]{:S(2)}, u32[]{:S(2)}) async-start(bf16[8,4,1280]{2,1,0:T(4,128)(2,1)} %get-tuple-element.27), calls=%async_computation | async-start | bytes 163840 | tf_op jit(solution)/shard_map/long_hidden/all_to_all | solution.py:407
  8.9 2.4 %qkv.1 = (f32[24,320]{1,0:T(8,128)S(1)}, f32[24,320]{1,0:T(8,128)S(1)}, f32[24,320]{1,0:T(8,128)S(1)}, f32[320]{0:T(512)S(1)}) custom-call(f32[320]{0:T(512)} %gains_hbm.1, bf16[3,320,1280]{2,1,0:T(8,128)(2,1)} %bitcast.6, bf16[24,1280]{1,0:T(8,128)(2,1)S(1)} %get-tuple-element.28.hidden_ref, bf16[320,1280]{1,0:T(8,128)(2,1)S(1)} %get-tuple-element.29.w_query_ref.w_ref), custom_call_target="tpu_custom_call" | custom-call | flops 100000000 | bytes 4000000 | tf_op jit(solution)/shard_map/qkv/pallas_call | solution.py:349
  11.3 4.6 %all-to-all-done.received_ref = bf16[8,4,1280]{2,1,0:T(4,128)(2,1)S(1)} async-done(((bf16[8,4,1280]{2,1,0:T(4,128)(2,1)}), bf16[8,4,1280]{2,1,0:T(4,128)(2,1)S(1)}, u32[]{:S(2)}, u32[]{:S(2)}) %all-to-all-start) | async-done | bytes 81952 | tf_op jit(solution)/shard_map/long_hidden/all_to_all | solution.py:407
  15.9 1.7 %long_attention.1 = f32[8,8,320]{2,1,0:T(8,128)} custom-call(bf16[8,4,1280]{2,1,0:T(4,128)(2,1)S(1)} %all-to-all-done.received_ref, f32[320]{0:T(512)S(1)} %get-tuple-element.30.gains_ref, bf16[320,1280]{1,0:T(8,128)(2,1)S(1)} %get-tuple-element.29.w_query_ref.w_ref, bf16[4,320,256]{2,1,0:T(8,128)(2,1)S(1)} %get-tuple-element.31.keys_ref, ...), custom_call_target="tpu_custom_call" | custom-call | flops 100000000 | bytes 4000000 | tf_op jit(solution)/shard_map/long_attention/pallas_call | solution.py:349
  17.6 3.4 %all-to-all-start.1 = ((f32[8,8,320]{2,1,0:T(8,128)}), f32[8,8,320]{2,1,0:T(8,128)S(1)}, u32[]{:S(2)}, u32[]{:S(2)}) async-start(f32[8,8,320]{2,1,0:T(8,128)} %long_attention.1), calls=%async_computation.1 | async-start | bytes 196608 | tf_op jit(solution)/shard_map/long_parts/all_to_all | solution.py:429
  21.0 3.3 %short_attention.1 = (f32[24,320]{1,0:T(8,128)S(1)}, f32[24,320]{1,0:T(8,128)S(1)}, f32[24,128]{1,0:T(8,128)S(1)}, bf16[320,1280]{1,0:T(8,128)(2,1)S(1)}) custom-call(s32[24]{0:T(128)} %lengths_hbm.1, s32[4]{0:T(128)} %longs_hbm.3, bf16[24,320,128]{2,1,0:T(8,128)(2,1)} %bitcast.7, bf16[24,320,128]{2,1,0:T(8,128)(2,1)} %bitcast.8, ...), custom_call_target="tpu_custom_call" | custom-call | flops 1000000000 | bytes 6000000 | tf_op jit(solution)/shard_map/short_attention/pallas_call | solution.py:349
  24.3 3.7 %all-to-all-done.1.parts_ref = f32[8,8,320]{2,1,0:T(8,128)S(1)} async-done(((f32[8,8,320]{2,1,0:T(8,128)}), f32[8,8,320]{2,1,0:T(8,128)S(1)}, u32[]{:S(2)}, u32[]{:S(2)}) %all-to-all-start.1) | async-done | bytes 81952 | tf_op jit(solution)/shard_map/long_parts/all_to_all | solution.py:429
  28.1 0.3 project.1.refs_7_.left_ref
  28.4 0.1 collective-permute-start
  28.4 2.5 %load.1 = (bf16[24,1280]{1,0:T(8,128)(2,1)S(1)}, f32[1280]{0:T(1024)S(1)}, bf16[2,1280,640]{2,1,0:T(8,128)(2,1)S(1)}, bf16[640,1280]{1,0:T(8,128)(2,1)S(1)}, f32...) custom-call(bf16[24,1280]{1,0:T(8,128)(2,1)} %refs_0_.1, f32[1280]{0:T(1024)} %refs_1_.1, ...), custom_call_target="tpu_custom_call" | custom-call | flops 1000000 | bytes 6000000 | tf_op jit(solution)/shard_map/load/pallas_call | solution.py:349
  31.0 1.7 %collective-permute-done.right_ref = bf16[24,1280]{1,0:T(8,128)(2,1)S(1)} collective-permute-done((bf16[24,1280]{1,0:T(8,128)(2,1)S(1)}, bf16[24,1280]{1,0:T(8,128)(2,1)S(1)}, u32[]{:S(2)}, u32[]{:S(2)}) %collective-permute-start) | collective-permute-done | bytes 61472 | tf_op jit(solution)/shard_map/sum_heads/ppermute | solution.py:366
  32.7 0.2 collective-permute-start.1
  32.9 1.1 %collective-permute-done.1.right_ref = bf16[24,1280]{1,0:T(8,128)(2,1)S(1)} collective-permute-done((bf16[24,1280]{1,0:T(8,128)(2,1)S(1)}, bf16[24,1280]{1,0:T(8,128)(2,1)S(1)}, u32[]{:S(2)}, u32[]{:S(2)}) %collective-permute-start.1) | collective-permute-done | bytes 61472 | tf_op jit(solution)/shard_map/sum_heads/ppermute | solution.py:366
  34.0 1.1 %mlp.1 = (bf16[24,1280]{1,0:T(8,128)(2,1)S(1)}, bf16[24,1280]{1,0:T(8,128)(2,1)S(1)}) custom-call(bf16[24,1280]{1,0:T(8,128)(2,1)S(1)} %sum_heads.1.left_ref, bf16[24,1280]{1,0:T(8,128)(2,1)S(1)} %collective-permute-done.1.right_ref, bf16[24,1280]{1,0:T(8,128)(2,1)S(1)} %get-tuple-element.41.hidden_ref, f32[1280]{0:T(1024)S(1)} %get-tuple-element.42.alpha_ref, ...), custom_call_target="tpu_custom_call" | custom-call | flops 100000000 | bytes 5000000 | tf_op jit(solution)/shard_map/mlp/pallas_call | solution.py:349
  35.1 0.7 %collective-permute-start.2 = (bf16[24,1280]{1,0:T(8,128)(2,1)S(1)}, bf16[24,1280]{1,0:T(8,128)(2,1)S(1)}, u32[]{:S(2)}, u32[]{:S(2)}) collective-permute-start(bf16[24,1280]{1,0:T(8,128)(2,1)S(1)} %get-tuple-element.46.left_ref), channel_id=1, source_target_pairs={{0,3},{1,2},{2,1},{3,0},{4,7},{5,6},{6,5},{7,4},{8,11},{9,10},{10,... | collective-permute-start | bytes 184328 | tf_op jit(solution)/shard_map/sum_units/ppermute | solution.py:366
  35.9 3.3 %collective-permute-done.2.right_ref = bf16[24,1280]{1,0:T(8,128)(2,1)S(1)} collective-permute-done((bf16[24,1280]{1,0:T(8,128)(2,1)S(1)}, bf16[24,1280]{1,0:T(8,128)(2,1)S(1)}, u32[]{:S(2)}, u32[]{:S(2)}) %collective-permute-start.2) | collective-permute-done | bytes 61472 | tf_op jit(solution)/shard_map/sum_units/ppermute | solution.py:366
  39.1 0.2 collective-permute-start.3
  39.4 1.1 %collective-permute-done.3.right_ref = bf16[24,1280]{1,0:T(8,128)(2,1)S(1)} collective-permute-done((bf16[24,1280]{1,0:T(8,128)(2,1)S(1)}, bf16[24,1280]{1,0:T(8,128)(2,1)S(1)}, u32[]{:S(2)}, u32[]{:S(2)}) %collective-permute-start.3) | collective-permute-done | bytes 61472 | tf_op jit(solution)/shard_map/sum_units/ppermute | solution.py:366
  40.5 0.8 %final.1 = bf16[24,1280]{1,0:T(8,128)(2,1)} custom-call(bf16[24,1280]{1,0:T(8,128)(2,1)S(1)} %sum_units.1.left_ref, bf16[24,1280]{1,0:T(8,128)(2,1)S(1)} %collective-permute-done.3.right_ref, bf16[24,1280]{1,0:T(8,128)(2,1)S(1)} %get-tuple-element.47.mid_ref, f32[1280]{0:T(1024)S(1)} %get-tuple-element.48.alpha_ref), custom_call_target="tpu_custom_call" | custom-call | flops 1000000 | bytes 100000 | tf_op jit(solution)/shard_map/final/pallas_call | solution.py:349
  (2 shorter events, 0.0 us)
Async XLA Ops:
  1.7 14.3 %all-to-all-start = ((bf16[8,4,1280]{2,1,0:T(4,128)(2,1)}), bf16[8,4,1280]{2,1,0:T(4,128)(2,1)S(1)}, u32[]{:S(2)}, u32[]{:S(2)}) async-start(bf16[8,4,1280]{2,1,0:T(4,128)(2,1)} %get-tuple-element.27), calls=%async_computation | async-start | bytes 163840 | tf_op jit(solution)/shard_map/long_hidden/all_to_all | solution.py:407
  17.6 10.4 %all-to-all-start.1 = ((f32[8,8,320]{2,1,0:T(8,128)}), f32[8,8,320]{2,1,0:T(8,128)S(1)}, u32[]{:S(2)}, u32[]{:S(2)}) async-start(f32[8,8,320]{2,1,0:T(8,128)} %long_attention.1), calls=%async_computation.1 | async-start | bytes 196608 | tf_op jit(solution)/shard_map/long_parts/all_to_all | solution.py:429
  28.4 4.3 %collective-permute-start = (bf16[24,1280]{1,0:T(8,128)(2,1)S(1)}, bf16[24,1280]{1,0:T(8,128)(2,1)S(1)}, u32[]{:S(2)}, u32[]{:S(2)}) collective-permute-start(bf16[24,1280]{1,0:T(8,128)(2,1)S(1)} %project.1.refs_7_.left_ref), channel_id=1, source_target_pairs={{0,3},{1,2},{2,1},{3,0},{4,7},{5,6},{6,5},{7,4},{8,11},{9,10},{10,... | collective-permute-start | bytes 184328 | tf_op jit(solution)/shard_map/sum_heads/ppermute | solution.py:366
  32.7 1.3 %collective-permute-start.1 = (bf16[24,1280]{1,0:T(8,128)(2,1)S(1)}, bf16[24,1280]{1,0:T(8,128)(2,1)S(1)}, u32[]{:S(2)}, u32[]{:S(2)}) collective-permute-start(bf16[24,1280]{1,0:T(8,128)(2,1)S(1)} %sum_heads.1.left_ref), channel_id=1, source_target_pairs={{0,1},{1,0},{2,3},{3,2},{4,5},{5,4},{6,7},{7,6},{8,9},{9,8},{10,11... | collective-permute-start | bytes 184328 | tf_op jit(solution)/shard_map/sum_heads/ppermute | solution.py:366
  35.1 4.0 %collective-permute-start.2 = (bf16[24,1280]{1,0:T(8,128)(2,1)S(1)}, bf16[24,1280]{1,0:T(8,128)(2,1)S(1)}, u32[]{:S(2)}, u32[]{:S(2)}) collective-permute-start(bf16[24,1280]{1,0:T(8,128)(2,1)S(1)} %get-tuple-element.46.left_ref), channel_id=1, source_target_pairs={{0,3},{1,2},{2,1},{3,0},{4,7},{5,6},{6,5},{7,4},{8,11},{9,10},{10,... | collective-permute-start | bytes 184328 | tf_op jit(solution)/shard_map/sum_units/ppermute | solution.py:366
  39.1 1.3 %collective-permute-start.3 = (bf16[24,1280]{1,0:T(8,128)(2,1)S(1)}, bf16[24,1280]{1,0:T(8,128)(2,1)S(1)}, u32[]{:S(2)}, u32[]{:S(2)}) collective-permute-start(bf16[24,1280]{1,0:T(8,128)(2,1)S(1)} %sum_units.1.left_ref), channel_id=1, source_target_pairs={{0,1},{1,0},{2,3},{3,2},{4,5},{5,4},{6,7},{7,6},{8,9},{9,8},{10,11... | collective-permute-start | bytes 184328 | tf_op jit(solution)/shard_map/sum_units/ppermute | solution.py:366

commit v3 on v2

v3 whole, which is shorter than its diff:
```python
import math

import jax
import jax.numpy as jnp
from jax import lax
from jax.experimental import pallas as pl
from jax.experimental.pallas import tpu as pltpu
from jax.sharding import PartitionSpec as P

HEAD_DIM = 64
EPS = 1e-06
LOW = -1e30
F32 = jnp.float32
BF16 = jnp.bfloat16
LANES = 8

VMEM = pl.BlockSpec(memory_space=pltpu.VMEM)
HBM = pl.BlockSpec(memory_space=pltpu.HBM)


def dot(left, right):
    return jnp.dot(left, right, preferred_element_type=F32)


def dot_t(left, right):
    return lax.dot_general(left, right, (((1,), (1,)), ((), ())), preferred_element_type=F32)


def head_masks(width):
    lane = lax.broadcasted_iota(jnp.int32, (1, width), 1)
    return [
        (lane >= h * HEAD_DIM) & (lane < (h + 1) * HEAD_DIM) for h in range(width // HEAD_DIM)
    ]


def head_rows(width):
    sub = lax.broadcasted_iota(jnp.int32, (LANES, width), 0)
    lane = lax.broadcasted_iota(jnp.int32, (LANES, width), 1)
    return (lane >= sub * HEAD_DIM) & (lane < (sub + 1) * HEAD_DIM)


def spread_sums(values, masks, function):
    result = jnp.zeros_like(values)
    for mask in masks:
        total = jnp.sum(jnp.where(mask, values, 0.0), axis=-1, keepdims=True)
        result = jnp.where(mask, function(total), result)
    return result


def head_unit(values, gains, masks):
    scale = spread_sums(values * values, masks, lambda total: lax.rsqrt(total + EPS))
    return (values * scale * gains).astype(BF16).astype(F32)


def row_norm(values):
    return values * lax.rsqrt(jnp.mean(values * values, axis=-1, keepdims=True) + EPS)


def gathered(values, diagonal):
    return jnp.sum(jnp.where(diagonal, values, 0.0), axis=0, keepdims=True)


def start_all(pairs, sems):
    copies = [pltpu.make_async_copy(s, d, sems.at[i]) for i, (s, d) in enumerate(pairs)]
    for copy in copies:
        copy.start()
    return copies


def select_kernel(
    longs_hbm,
    hidden_hbm,
    gains_hbm,
    w_hbm,
    keys_hbm,
    sent_hbm,
    hidden_ref,
    match_ref,
    query_ref,
    gains_ref,
    w_query_ref,
    w_key_ref,
    keys_ref,
    longs_ref,
    sent_ref,
    sems,
):
    copies = start_all(
        [
            (longs_hbm, longs_ref),
            (hidden_hbm, hidden_ref),
            (gains_hbm, gains_ref),
            (w_hbm.at[0], w_query_ref),
            (w_hbm.at[1], w_key_ref),
            (keys_hbm, keys_ref),
        ],
        sems,
    )
    parties, longs, _ = sent_ref.shape
    rows = hidden_ref.shape[0]
    offset = lax.axis_index("req") * rows
    sub = lax.broadcasted_iota(jnp.int32, (8, rows), 0)
    lane = lax.broadcasted_iota(jnp.int32, (8, rows), 1) + offset
    here = jnp.zeros((8, rows), jnp.bool_)
    copies[0].wait()
    for index in range(longs):
        here = here | ((sub == index) & (lane == longs_ref[index]))
    copies[1].wait()
    picked = dot(here.astype(F32).astype(BF16), hidden_ref[...])[:longs].astype(BF16)
    for party in range(parties):
        sent_ref[party] = picked
    out = pltpu.make_async_copy(sent_ref, sent_hbm, sems.at[6])
    out.start()
    row = lax.broadcasted_iota(jnp.int32, match_ref.shape, 0) + offset
    column = lax.broadcasted_iota(jnp.int32, match_ref.shape, 1)
    match = jnp.zeros(match_ref.shape, F32)
    for index in range(longs):
        match = jnp.where((row == longs_ref[index]) & (column == index), 1.0, match)
    match_ref[...] = match
    copies[2].wait()
    copies[3].wait()
    query = dot_t(hidden_ref[...], w_query_ref[...])
    query = head_unit(query, gains_ref[...][None, :], head_masks(query.shape[1]))
    query_ref[...] = query * math.sqrt(HEAD_DIM)
    copies[4].wait()
    copies[5].wait()
    out.wait()


def short_kernel(
    lengths_hbm,
    w_hbm,
    keys_hbm,
    values_hbm,
    long_values_hbm,
    hidden_ref,
    query_ref,
    gains_ref,
    w_key_ref,
    out_ref,
    lse_ref,
    value_ref,
    own_ref,
    long_values_ref,
    lengths_ref,
    w_value_ref,
    keys_ref,
    values_ref,
    sems,
):
    copies = start_all(
        [
            (lengths_hbm, lengths_ref),
            (w_hbm.at[2], w_value_ref),
            (keys_hbm, keys_ref),
            (values_hbm, values_ref),
            (long_values_hbm, long_values_ref),
        ],
        sems,
    )
    rows, width = out_ref.shape
    slots = keys_ref.shape[2]
    masks = head_masks(width)
    diagonal = head_rows(width)
    sub = lax.broadcasted_iota(jnp.int32, (2 * LANES, 2 * slots), 0)
    lane = lax.broadcasted_iota(jnp.int32, (2 * LANES, 2 * slots), 1)
    second = sub >= LANES
    first = jnp.where(second, slots, 0)
    hidden = hidden_ref[...]
    query = query_ref[...]
    pairs = [
        jnp.concatenate(
            [jnp.where(diagonal, query[r + i : r + i + 1], 0.0) for i in range(2)], axis=0
        ).astype(BF16)
        for r in range(0, rows, 2)
    ]
    key = head_unit(dot_t(hidden, w_key_ref[...]), gains_ref[...][None, :], masks)
    own_ref[...] = spread_sums(query * key, masks, lambda total: total)
    copies[0].wait()
    copies[1].wait()
    value_ref[...] = dot_t(hidden, w_value_ref[...]).astype(BF16).astype(F32)
    copies[2].wait()
    weights, scales = [], []
    for p, r in enumerate(range(0, rows, 2)):
        scores = dot(pairs[p], jnp.concatenate([keys_ref[r], keys_ref[r + 1]], axis=1))
        last = jnp.where(second, slots + lengths_ref[r + 1], lengths_ref[r])
        valid = (lane >= first) & (lane < last)
        scores = jnp.where(valid, scores, LOW)
        top = jnp.max(scores, axis=-1, keepdims=True)
        weight = jnp.where(valid, jnp.exp(scores - top), 0.0)
        total = jnp.sum(weight, axis=-1, keepdims=True)
        weights.append(weight.astype(BF16))
        scales.append(1.0 / total)
        lse = top + jnp.log(total)
        for i in range(2):
            part = slice(i * LANES, (i + 1) * LANES)
            lse_ref[r + i : r + i + 1, :] = gathered(lse[part], diagonal)
    copies[3].wait()
    for p, r in enumerate(range(0, rows, 2)):
        summed = dot_t(weights[p], jnp.concatenate([values_ref[r], values_ref[r + 1]], axis=1))
        summed = summed * scales[p]
        for i in range(2):
            part = slice(i * LANES, (i + 1) * LANES)
            out_ref[r + i : r + i + 1, :] = gathered(summed[part], diagonal)
    copies[4].wait()


def long_kernel(
    w_out_hbm,
    received_ref,
    gains_ref,
    w_ref,
    keys_ref,
    values_ref,
    sent_ref,
    w_out_ref,
    sems,
):
    copy = pltpu.make_async_copy(w_out_hbm, w_out_ref, sems.at[0])
    copy.start()
    parties, longs, _ = received_ref.shape
    width = w_ref.shape[0]
    hidden = received_ref[0].astype(F32)
    for party in range(1, parties):
        hidden = hidden + received_ref[party].astype(F32)
    query = dot_t(hidden.astype(BF16), w_ref[...])
    query = head_unit(query, gains_ref[...][None, :], head_masks(width)) * math.sqrt(HEAD_DIM)
    diagonal = head_rows(width)
    scores = [
        dot(jnp.where(diagonal, query[i : i + 1], 0.0).astype(BF16), keys_ref[i])
        for i in range(longs)
    ]
    outs, lses = [], []
    for i in range(longs):
        top = jnp.max(scores[i], axis=-1, keepdims=True)
        weights = jnp.exp(scores[i] - top)
        total = jnp.sum(weights, axis=-1, keepdims=True)
        summed = dot_t(weights.astype(BF16), values_ref[i])
        outs.append(gathered(summed / total, diagonal))
        lses.append(gathered(top + jnp.log(total), diagonal))
    packed = jnp.concatenate(outs + lses, axis=0)
    for party in range(parties):
        sent_ref[party] = packed
    copy.wait()


def project_kernel(
    parts_ref, short_ref, short_lse_ref, value_ref, own_ref, match_ref, w_ref, out_ref
):
    parties, doubled, width = parts_ref.shape
    longs = doubled // 2
    top = parts_ref[0]
    for party in range(1, parties):
        top = jnp.maximum(top, parts_ref[party])
    top = top[longs:]
    total = jnp.zeros((longs, width), F32)
    acc = jnp.zeros((longs, width), F32)
    for party in range(parties):
        part = parts_ref[party]
        weight = jnp.exp(part[longs:] - top)
        total = total + weight
        acc = acc + weight * part[:longs]
    long_out = acc / total
    long_lse = top + jnp.log(total)
    cached = short_ref[...]
    lse = short_lse_ref[...]
    for index in range(longs):
        here = match_ref[:, index : index + 1] > 0.5
        cached = jnp.where(here, long_out[index : index + 1], cached)
        lse = jnp.where(here, long_lse[index : index + 1], lse)
    own = own_ref[...]
    top = jnp.maximum(lse, own)
    old = jnp.exp(lse - top)
    new = jnp.exp(own - top)
    attended = (old * cached + new * value_ref[...]) / (old + new)
    out_ref[...] = dot(attended.astype(BF16), w_ref[...]).astype(BF16)


def load_kernel(*refs):
    count = (len(refs) - 2) // 2
    copies = start_all(list(zip(refs[:count], refs[count + 1 : -1])), refs[-1])
    for copy in copies:
        copy.wait()


def add_kernel(left_ref, right_ref, *refs):
    out_ref = refs[-1]
    out_ref[...] = (left_ref[...].astype(F32) + right_ref[...].astype(F32)).astype(BF16)


def renormed(left_ref, right_ref, base, alpha_ref):
    total = left_ref[...].astype(F32) + right_ref[...].astype(F32)
    alpha = alpha_ref[...][None, :]
    return row_norm(base + alpha * (row_norm(total) - base)).astype(BF16)


def mlp_kernel(
    left_ref,
    right_ref,
    hidden_ref,
    alpha_ref,
    w_gate_up_ref,
    w_down_ref,
    s_gate_ref,
    s_up_ref,
    mid_ref,
    out_ref,
):
    middle = renormed(left_ref, right_ref, hidden_ref[...].astype(F32), alpha_ref)
    mid_ref[...] = middle
    gate = dot(middle, w_gate_up_ref[0]) * s_gate_ref[...][None, :]
    upward = dot(middle, w_gate_up_ref[1]) * s_up_ref[...][None, :]
    gated = (gate / (1.0 + jnp.exp(-gate)) * upward).astype(BF16)
    out_ref[...] = dot(gated, w_down_ref[...]).astype(BF16)


def final_kernel(left_ref, right_ref, mid_ref, alpha_ref, out_ref):
    out_ref[...] = renormed(left_ref, right_ref, mid_ref[...].astype(F32), alpha_ref)


def call(kernel, outs, cost, far=(), near=(), out_far=(), scratch=(), copies=0):
    far = [pltpu.with_memory_space_constraint(a, pltpu.HBM) for a in far]
    return pl.pallas_call(
        kernel,
        in_specs=[HBM] * len(far) + [VMEM] * len(near),
        out_specs=[HBM] * len(out_far) + [VMEM] * len(outs),
        out_shape=[pltpu.HBM(a.shape, a.dtype) for a in out_far] + list(outs),
        scratch_shapes=list(scratch) + [pltpu.SemaphoreType.DMA((copies,))] * (copies > 0),
        cost_estimate=pl.CostEstimate(flops=cost[0], bytes_accessed=cost[1], transcendentals=0),
        compiler_params=pltpu.CompilerParams(vmem_limit_bytes=32 * 1024 * 1024),
    )(*far, *near)


def like(array):
    return jax.ShapeDtypeStruct(array.shape, array.dtype)


def exchanged(value, step):
    places = lax.axis_size("head")
    return lax.ppermute(value, "head", [(i, i ^ step) for i in range(places)])


def on_device(
    hidden,
    w_qkv,
    w_out,
    s_qk,
    alpha_attn,
    w_gate_up,
    w_down,
    s_up,
    s_gate,
    alpha_mlp,
    short_keys,
    short_values,
    cache_lengths,
    long_keys,
    long_values,
    long_rows,
):
    rows, model = hidden.shape
    width = w_qkv.shape[2]
    longs = long_keys.shape[0]
    parties = lax.axis_size("req")
    shape = jax.ShapeDtypeStruct
    state = shape((rows, width), F32)
    wide = shape((rows, model), BF16)
    w_qkv, short_keys, short_values, long_keys, long_values = (
        jnp.swapaxes(a, 1, 2) for a in (w_qkv, short_keys, short_values, long_keys, long_values)
    )
    with jax.named_scope("long_hidden"):
        sent, hidden_near, match, query, gains, w_query, w_key, keys = call(
            select_kernel,
            (
                wide,
                shape((rows, 128), F32),
                state,
                like(s_qk),
                shape(w_qkv.shape[1:], BF16),
                shape(w_qkv.shape[1:], BF16),
                like(long_keys),
            ),
            (10**6, 3 * 10**6),
            far=(long_rows, hidden, s_qk, w_qkv, long_keys),
            out_far=(shape((parties, longs, model), BF16),),
            scratch=(pltpu.SMEM((longs,), jnp.int32), pltpu.VMEM((parties, longs, model), BF16)),
            copies=7,
        )
        received = lax.all_to_all(sent, "req", 0, 0)
    with jax.named_scope("short_attention"):
        short_out, short_lse, value, own, values = call(
            short_kernel,
            (state, state, state, state, like(long_values)),
            (10**9, 6 * 10**6),
            far=(cache_lengths, w_qkv, short_keys, short_values, long_values),
            near=(hidden_near, query, gains, w_key),
            scratch=(
                pltpu.SMEM((rows,), jnp.int32),
                pltpu.VMEM(w_qkv.shape[1:], BF16),
                pltpu.VMEM(short_keys.shape, BF16),
                pltpu.VMEM(short_values.shape, BF16),
            ),
            copies=5,
        )
    with jax.named_scope("long_attention"):
        partial, w_out = call(
            long_kernel,
            (shape((parties, 2 * longs, width), F32), like(w_out)),
            (10**8, 4 * 10**6),
            far=(w_out,),
            near=(received, gains, w_query, keys, values),
            copies=1,
        )
    with jax.named_scope("long_parts"):
        parts = lax.all_to_all(partial, "req", 0, 0)
    with jax.named_scope("project"):
        (projected,) = call(
            project_kernel,
            (wide,),
            (2 * rows * width * model, 10**6),
            near=(parts, short_out, short_lse, value, own, match, w_out),
        )
    with jax.named_scope("load"):
        loads = (hidden, alpha_attn, w_gate_up, w_down, s_gate, s_up, alpha_mlp)
        hidden, alpha_attn, w_gate_up, w_down, s_gate, s_up, alpha_mlp = call(
            load_kernel,
            [like(a) for a in loads],
            (10**6, 6 * 10**6),
            far=loads,
            near=(projected,),
            copies=len(loads),
        )
    with jax.named_scope("sum_heads"):
        other = exchanged(projected, 3)
        (projected,) = call(add_kernel, (wide,), (10**5, 10**5), near=(projected, other, s_up))
        other = exchanged(projected, 1)
    with jax.named_scope("mlp"):
        middle, downward = call(
            mlp_kernel,
            (wide, wide),
            (10**8, 5 * 10**6),
            near=(projected, other, hidden, alpha_attn, w_gate_up, w_down, s_gate, s_up),
        )
    with jax.named_scope("sum_units"):
        other = exchanged(downward, 3)
        (downward,) = call(add_kernel, (wide,), (10**5, 10**5), near=(downward, other))
        other = exchanged(downward, 1)
    with jax.named_scope("final"):
        (updated,) = call(
            final_kernel, (wide,), (10**6, 10**5), near=(downward, other, middle, alpha_mlp)
        )
        return updated


def solution(mesh):
    return jax.shard_map(
        on_device,
        mesh=mesh,
        in_specs=(
            P("req", None),
            P(None, None, "head"),
            P("head", None),
            P("head"),
            P(),
            P(None, None, "head"),
            P("head", None),
            P("head"),
            P("head"),
            P(),
            P("req", None, "head"),
            P("req", None, "head"),
            P("req"),
            P(None, "req", "head"),
            P(None, "req", "head"),
            P(),
        ),
        out_specs=P("req", None),
        check_vma=False,
    )
```

time: 41.7 us -> 40.2 us (0.964)
  blocking collectives: 0 us -> 9.51 us
  waiting for transfers between devices: 15.5 us -> 10.8 us
  starting transfers between devices: 11.8 us -> 8.47 us
  Pallas kernels: 13.9 us -> 11.1 us
    all_to_all x0 -> x1, blocking collectives: none -> 9.51 us  [on_device(): parts = lax.all_to_all(partial, 'req', 0, 0)]
    all_to_all x1 -> x0, waiting for transfers between devices: 3.73 us -> none  [on_device(): parts = lax.all_to_all(partial, 'req', 0, 0)]
    all_to_all x1 -> x0, starting transfers between devices: 3.37 us -> none  [on_device(): parts = lax.all_to_all(partial, 'req', 0, 0)]
    pallas_call x10 -> x9, Pallas kernels: 13.9 us -> 11.1 us  [call(): pl.pallas_call(kernel, in_specs=[HBM] * len(far) + [VMEM] * len(near), ou...]
    all_to_all x1, waiting for transfers between devices: 4.63 us -> 3.61 us  [on_device(): received = lax.all_to_all(sent, 'req', 0, 0)]
  transfers between devices with their start and end apart: 6 -> 5, of which waited for: 6 -> 5; matrix products, arithmetic and copies ran while one was open for 0% -> 0% of each run, Pallas kernels for 20% -> 15%
where the time goes in v3:
time: 40.2 us; the launch traced here: 39.9 us
  Pallas kernels  11.1 us (28%)
  waiting for transfers between devices  10.8 us (27%)
  blocking collectives  9.51 us (24%)
  starting transfers between devices  8.47 us (21%)
    pallas_call x9, Pallas kernels, call(): pl.pallas_call(kernel, in_specs=[HBM] * len(far) + [VMEM] * len(near), ou...  11.1 us
    all_to_all x1, blocking collectives, on_device(): parts = lax.all_to_all(partial, 'req', 0, 0)  9.51 us
    all_to_all x1, starting transfers between devices, on_device(): received = lax.all_to_all(sent, 'req', 0, 0)  7.27 us
    ppermute x4, waiting for transfers between devices, exchanged(): return lax.ppermute(value, 'head', [(i, i ^ step) for i in range(places)])  7.15 us
    all_to_all x1, waiting for transfers between devices, on_device(): received = lax.all_to_all(sent, 'req', 0, 0)  3.61 us
    ppermute x4, starting transfers between devices, exchanged(): return lax.ppermute(value, 'head', [(i, i ^ step) for i in range(places)])  1.21 us
  transfers between devices with their start and end apart: 5, of which 5 were waited for; matrix products, arithmetic and copies ran while one was open for 0% of the time, Pallas kernels for 15%

profile of v3, /device:TPU:0, one launch (start us, length us, event | category | flops | bytes accessed | tf_op | source)
XLA Modules:
  0.0 39.9 jit_solution(17972227957105331504)
XLA Ops:
  0.0 1.7 %long_hidden.1 = (bf16[8,4,1280]{2,1,0:T(4,128)(2,1)}, bf16[24,1280]{1,0:T(8,128)(2,1)S(1)}, f32[24,128]{1,0:T(8,128)S(1)}, f32[24,320]{1,0:T(8,128)S(1)}, f32[3...) custom-call(s32[4]{0:T(128)} %longs_hbm.1, ...), custom_call_target="tpu_custom_call" | custom-call | flops 1000000 | bytes 3000000 | tf_op jit(solution)/shard_map/long_hidden/pallas_call | solution.py:323
  1.7 7.3 %all-to-all-start = ((bf16[8,4,1280]{2,1,0:T(4,128)(2,1)}), bf16[8,4,1280]{2,1,0:T(4,128)(2,1)S(1)}, u32[]{:S(2)}, u32[]{:S(2)}) async-start(bf16[8,4,1280]{2,1,0:T(4,128)(2,1)} %get-tuple-element.29), calls=%async_computation | async-start | bytes 163840 | tf_op jit(solution)/shard_map/long_hidden/all_to_all | solution.py:389
  9.0 3.4 %short_attention.1 = (f32[24,320]{1,0:T(8,128)S(1)}, f32[24,320]{1,0:T(8,128)S(1)}, f32[24,320]{1,0:T(8,128)S(1)}, f32[24,320]{1,0:T(8,128)S(1)}, bf16[4,320,256]{2,1,0:T(8,128)(2,1)S(1)}) custom-call(s32[24]{0:T(128)} %lengths_hbm.1, bf16[3,320,1280]{2,1,0:T(8,128)(2,1)} %bitcast.6, bf16[24,320,128]{2,1,0:T(8,128)(2,1)} %bitcast.7, ...), custom_call_target="tpu_custom_call" | custom-call | flops 1000000000 | bytes 6000000 | tf_op jit(solution)/shard_map/short_attention/pallas_call | solution.py:323
  12.4 3.6 %all-to-all-done.received_ref = bf16[8,4,1280]{2,1,0:T(4,128)(2,1)S(1)} async-done(((bf16[8,4,1280]{2,1,0:T(4,128)(2,1)}), bf16[8,4,1280]{2,1,0:T(4,128)(2,1)S(1)}, u32[]{:S(2)}, u32[]{:S(2)}) %all-to-all-start) | async-done | bytes 81952 | tf_op jit(solution)/shard_map/long_hidden/all_to_all | solution.py:389
  16.0 1.2 %long_attention.1 = (f32[8,8,320]{2,1,0:T(8,128)S(1)}, bf16[320,1280]{1,0:T(8,128)(2,1)S(1)}) custom-call(bf16[320,1280]{1,0:T(8,128)(2,1)} %w_out_hbm.1, bf16[8,4,1280]{2,1,0:T(4,128)(2,1)S(1)} %all-to-all-done.received_ref, f32[320]{0:T(512)S(1)} %get-tuple-element.30.gains_ref, bf16[320,1280]{1,0:T(8,128)(2,1)S(1)} %get-tuple-element.31.w_ref, ...), custom_call_target="tpu_custom_call" | custom-call | flops 100000000 | bytes 4000000 | tf_op jit(solution)/shard_map/long_attention/pallas_call | solution.py:323
  17.2 9.5 %all_to_all.10.parts_ref = f32[8,8,320]{2,1,0:T(8,128)S(1)} all-to-all(f32[8,8,320]{2,1,0:T(8,128)S(1)} %get-tuple-element.37), channel_id=1, replica_groups=mesh['req'=8,'head'=4] {'req'}, dimensions={0} | all-to-all | bytes 163840 | tf_op jit(solution)/shard_map/long_parts/all_to_all | solution.py:415
  26.7 0.3 project.1.refs_7_.left_ref
  27.0 0.1 collective-permute-start
  27.1 2.5 %load.1 = (bf16[24,1280]{1,0:T(8,128)(2,1)S(1)}, f32[1280]{0:T(1024)S(1)}, bf16[2,1280,640]{2,1,0:T(8,128)(2,1)S(1)}, bf16[640,1280]{1,0:T(8,128)(2,1)S(1)}, f32...) custom-call(bf16[24,1280]{1,0:T(8,128)(2,1)} %refs_0_.1, f32[1280]{0:T(1024)} %refs_1_.1, ...), custom_call_target="tpu_custom_call" | custom-call | flops 1000000 | bytes 6000000 | tf_op jit(solution)/shard_map/load/pallas_call | solution.py:323
  29.6 1.7 %collective-permute-done.right_ref = bf16[24,1280]{1,0:T(8,128)(2,1)S(1)} collective-permute-done((bf16[24,1280]{1,0:T(8,128)(2,1)S(1)}, bf16[24,1280]{1,0:T(8,128)(2,1)S(1)}, u32[]{:S(2)}, u32[]{:S(2)}) %collective-permute-start) | collective-permute-done | bytes 61472 | tf_op jit(solution)/shard_map/sum_heads/ppermute | solution.py:340
  31.3 0.2 collective-permute-start.1
  31.5 1.1 %collective-permute-done.1.right_ref = bf16[24,1280]{1,0:T(8,128)(2,1)S(1)} collective-permute-done((bf16[24,1280]{1,0:T(8,128)(2,1)S(1)}, bf16[24,1280]{1,0:T(8,128)(2,1)S(1)}, u32[]{:S(2)}, u32[]{:S(2)}) %collective-permute-start.1) | collective-permute-done | bytes 61472 | tf_op jit(solution)/shard_map/sum_heads/ppermute | solution.py:340
  32.6 1.1 %mlp.1 = (bf16[24,1280]{1,0:T(8,128)(2,1)S(1)}, bf16[24,1280]{1,0:T(8,128)(2,1)S(1)}) custom-call(bf16[24,1280]{1,0:T(8,128)(2,1)S(1)} %sum_heads.1.left_ref, bf16[24,1280]{1,0:T(8,128)(2,1)S(1)} %collective-permute-done.1.right_ref, bf16[24,1280]{1,0:T(8,128)(2,1)S(1)} %get-tuple-element.45.hidden_ref, f32[1280]{0:T(1024)S(1)} %get-tuple-element.46.alpha_ref, ...), custom_call_target="tpu_custom_call" | custom-call | flops 100000000 | bytes 5000000 | tf_op jit(solution)/shard_map/mlp/pallas_call | solution.py:323
  33.7 0.7 %collective-permute-start.2 = (bf16[24,1280]{1,0:T(8,128)(2,1)S(1)}, bf16[24,1280]{1,0:T(8,128)(2,1)S(1)}, u32[]{:S(2)}, u32[]{:S(2)}) collective-permute-start(bf16[24,1280]{1,0:T(8,128)(2,1)S(1)} %get-tuple-element.50.left_ref), channel_id=1, source_target_pairs={{0,3},{1,2},{2,1},{3,0},{4,7},{5,6},{6,5},{7,4},{8,11},{9,10},{10,... | collective-permute-start | bytes 184328 | tf_op jit(solution)/shard_map/sum_units/ppermute | solution.py:340
  34.5 3.3 %collective-permute-done.2.right_ref = bf16[24,1280]{1,0:T(8,128)(2,1)S(1)} collective-permute-done((bf16[24,1280]{1,0:T(8,128)(2,1)S(1)}, bf16[24,1280]{1,0:T(8,128)(2,1)S(1)}, u32[]{:S(2)}, u32[]{:S(2)}) %collective-permute-start.2) | collective-permute-done | bytes 61472 | tf_op jit(solution)/shard_map/sum_units/ppermute | solution.py:340
  37.8 0.2 collective-permute-start.3
  38.0 1.1 %collective-permute-done.3.right_ref = bf16[24,1280]{1,0:T(8,128)(2,1)S(1)} collective-permute-done((bf16[24,1280]{1,0:T(8,128)(2,1)S(1)}, bf16[24,1280]{1,0:T(8,128)(2,1)S(1)}, u32[]{:S(2)}, u32[]{:S(2)}) %collective-permute-start.3) | collective-permute-done | bytes 61472 | tf_op jit(solution)/shard_map/sum_units/ppermute | solution.py:340
  39.1 0.8 %final.1 = bf16[24,1280]{1,0:T(8,128)(2,1)} custom-call(bf16[24,1280]{1,0:T(8,128)(2,1)S(1)} %sum_units.1.left_ref, bf16[24,1280]{1,0:T(8,128)(2,1)S(1)} %collective-permute-done.3.right_ref, bf16[24,1280]{1,0:T(8,128)(2,1)S(1)} %get-tuple-element.51.mid_ref, f32[1280]{0:T(1024)S(1)} %get-tuple-element.52.alpha_ref), custom_call_target="tpu_custom_call" | custom-call | flops 1000000 | bytes 100000 | tf_op jit(solution)/shard_map/final/pallas_call | solution.py:323
  (2 shorter events, 0.0 us)
Async XLA Ops:
  1.7 14.3 %all-to-all-start = ((bf16[8,4,1280]{2,1,0:T(4,128)(2,1)}), bf16[8,4,1280]{2,1,0:T(4,128)(2,1)S(1)}, u32[]{:S(2)}, u32[]{:S(2)}) async-start(bf16[8,4,1280]{2,1,0:T(4,128)(2,1)} %get-tuple-element.29), calls=%async_computation | async-start | bytes 163840 | tf_op jit(solution)/shard_map/long_hidden/all_to_all | solution.py:389
  27.0 4.3 %collective-permute-start = (bf16[24,1280]{1,0:T(8,128)(2,1)S(1)}, bf16[24,1280]{1,0:T(8,128)(2,1)S(1)}, u32[]{:S(2)}, u32[]{:S(2)}) collective-permute-start(bf16[24,1280]{1,0:T(8,128)(2,1)S(1)} %project.1.refs_7_.left_ref), channel_id=1, source_target_pairs={{0,3},{1,2},{2,1},{3,0},{4,7},{5,6},{6,5},{7,4},{8,11},{9,10},{10,... | collective-permute-start | bytes 184328 | tf_op jit(solution)/shard_map/sum_heads/ppermute | solution.py:340
  31.3 1.3 %collective-permute-start.1 = (bf16[24,1280]{1,0:T(8,128)(2,1)S(1)}, bf16[24,1280]{1,0:T(8,128)(2,1)S(1)}, u32[]{:S(2)}, u32[]{:S(2)}) collective-permute-start(bf16[24,1280]{1,0:T(8,128)(2,1)S(1)} %sum_heads.1.left_ref), channel_id=1, source_target_pairs={{0,1},{1,0},{2,3},{3,2},{4,5},{5,4},{6,7},{7,6},{8,9},{9,8},{10,11... | collective-permute-start | bytes 184328 | tf_op jit(solution)/shard_map/sum_heads/ppermute | solution.py:340
  33.7 4.0 %collective-permute-start.2 = (bf16[24,1280]{1,0:T(8,128)(2,1)S(1)}, bf16[24,1280]{1,0:T(8,128)(2,1)S(1)}, u32[]{:S(2)}, u32[]{:S(2)}) collective-permute-start(bf16[24,1280]{1,0:T(8,128)(2,1)S(1)} %get-tuple-element.50.left_ref), channel_id=1, source_target_pairs={{0,3},{1,2},{2,1},{3,0},{4,7},{5,6},{6,5},{7,4},{8,11},{9,10},{10,... | collective-permute-start | bytes 184328 | tf_op jit(solution)/shard_map/sum_units/ppermute | solution.py:340
  37.8 1.3 %collective-permute-start.3 = (bf16[24,1280]{1,0:T(8,128)(2,1)S(1)}, bf16[24,1280]{1,0:T(8,128)(2,1)S(1)}, u32[]{:S(2)}, u32[]{:S(2)}) collective-permute-start(bf16[24,1280]{1,0:T(8,128)(2,1)S(1)} %sum_units.1.left_ref), channel_id=1, source_target_pairs={{0,1},{1,0},{2,3},{3,2},{4,5},{5,4},{6,7},{7,6},{8,9},{9,8},{10,11... | collective-permute-start | bytes 184328 | tf_op jit(solution)/shard_map/sum_units/ppermute | solution.py:340

commit v4 on v3

--- a/solution.py
+++ b/solution.py
@@ -148,17 +148,19 @@
     values_ref,
     sems,
 ):
+    rows, width = out_ref.shape
+    halves = [pl.ds(0, rows // 2), pl.ds(rows // 2, rows - rows // 2)]
     copies = start_all(
         [
             (lengths_hbm, lengths_ref),
+            (keys_hbm.at[halves[0]], keys_ref.at[halves[0]]),
+            (keys_hbm.at[halves[1]], keys_ref.at[halves[1]]),
             (w_hbm.at[2], w_value_ref),
-            (keys_hbm, keys_ref),
             (values_hbm, values_ref),
             (long_values_hbm, long_values_ref),
         ],
         sems,
     )
-    rows, width = out_ref.shape
     slots = keys_ref.shape[2]
     masks = head_masks(width)
     diagonal = head_rows(width)
@@ -177,11 +179,10 @@
     key = head_unit(dot_t(hidden, w_key_ref[...]), gains_ref[...][None, :], masks)
     own_ref[...] = spread_sums(query * key, masks, lambda total: total)
     copies[0].wait()
-    copies[1].wait()
-    value_ref[...] = dot_t(hidden, w_value_ref[...]).astype(BF16).astype(F32)
-    copies[2].wait()
     weights, scales = [], []
     for p, r in enumerate(range(0, rows, 2)):
+        if r in (0, rows // 2):
+            copies[1 + (r > 0)].wait()
         scores = dot(pairs[p], jnp.concatenate([keys_ref[r], keys_ref[r + 1]], axis=1))
         last = jnp.where(second, slots + lengths_ref[r + 1], lengths_ref[r])
         valid = (lane >= first) & (lane < last)
@@ -196,13 +197,15 @@
             part = slice(i * LANES, (i + 1) * LANES)
             lse_ref[r + i : r + i + 1, :] = gathered(lse[part], diagonal)
     copies[3].wait()
+    value_ref[...] = dot_t(hidden, w_value_ref[...]).astype(BF16).astype(F32)
+    copies[4].wait()
     for p, r in enumerate(range(0, rows, 2)):
         summed = dot_t(weights[p], jnp.concatenate([values_ref[r], values_ref[r + 1]], axis=1))
         summed = summed * scales[p]
         for i in range(2):
             part = slice(i * LANES, (i + 1) * LANES)
             out_ref[r + i : r + i + 1, :] = gathered(summed[part], diagonal)
-    copies[4].wait()
+    copies[5].wait()
 
 
 def long_kernel(
@@ -335,6 +338,13 @@
     return jax.ShapeDtypeStruct(array.shape, array.dtype)
 
 
+def mixed_groups(parties):
+    places = lax.axis_size("head")
+    return [
+        [r * places + (h ^ ((r // 2) % 2)) for r in range(parties)] for h in range(places)
+    ]
+
+
 def exchanged(value, step):
     places = lax.axis_size("head")
     return lax.ppermute(value, "head", [(i, i ^ step) for i in range(places)])
@@ -386,7 +396,9 @@
             scratch=(pltpu.SMEM((longs,), jnp.int32), pltpu.VMEM((parties, longs, model), BF16)),
             copies=7,
         )
-        received = lax.all_to_all(sent, "req", 0, 0)
+        received = lax.all_to_all(
+            sent, ("req", "head"), 0, 0, axis_index_groups=mixed_groups(parties)
+        )
     with jax.named_scope("short_attention"):
         short_out, short_lse, value, own, values = call(
             short_kernel,
@@ -400,7 +412,7 @@
                 pltpu.VMEM(short_keys.shape, BF16),
                 pltpu.VMEM(short_values.shape, BF16),
             ),
-            copies=5,
+            copies=6,
         )
     with jax.named_scope("long_attention"):
         partial, w_out = call(

time: 40.2 us -> 39.8 us (0.990)
  blocking collectives: 9.51 us -> 10.3 us
  waiting for transfers between devices: 10.8 us -> 10.1 us
  starting transfers between devices: 8.47 us -> 7.91 us
    all_to_all x1, blocking collectives: 9.51 us -> 10.3 us  [on_device(): parts = lax.all_to_all(partial, 'req', 0, 0)]
    all_to_all x1, waiting for transfers between devices: 3.61 us -> 2.96 us  [on_device(): lax.all_to_all(sent, ('req', 'head'), 0, 0, axis_index_groups=mixed_group...]
    all_to_all x1, starting transfers between devices: 7.27 us -> 6.7 us  [on_device(): lax.all_to_all(sent, ('req', 'head'), 0, 0, axis_index_groups=mixed_group...]
where the time goes in v4:
time: 39.8 us; the launch traced here: 39.5 us
  Pallas kernels  11.2 us (28%)
  blocking collectives  10.3 us (26%)
  waiting for transfers between devices  10.1 us (25%)
  starting transfers between devices  7.91 us (20%)
    pallas_call x9, Pallas kernels, call(): pl.pallas_call(kernel, in_specs=[HBM] * len(far) + [VMEM] * len(near), ou...  11.2 us
    all_to_all x1, blocking collectives, on_device(): parts = lax.all_to_all(partial, 'req', 0, 0)  10.3 us
    ppermute x4, waiting for transfers between devices, exchanged(): return lax.ppermute(value, 'head', [(i, i ^ step) for i in range(places)])  7.15 us
    all_to_all x1, starting transfers between devices, on_device(): lax.all_to_all(sent, ('req', 'head'), 0, 0, axis_index_groups=mixed_group...  6.7 us
    all_to_all x1, waiting for transfers between devices, on_device(): lax.all_to_all(sent, ('req', 'head'), 0, 0, axis_index_groups=mixed_group...  2.96 us
    ppermute x4, starting transfers between devices, exchanged(): return lax.ppermute(value, 'head', [(i, i ^ step) for i in range(places)])  1.21 us
  transfers between devices with their start and end apart: 5, of which 5 were waited for; matrix products, arithmetic and copies ran while one was open for 0% of the time, Pallas kernels for 15%

profile of v4, /device:TPU:0, one launch (start us, length us, event | category | flops | bytes accessed | tf_op | source)
XLA Modules:
  0.0 39.5 jit_solution(14194026117820447837)
XLA Ops:
  0.0 1.7 %long_hidden.1 = (bf16[8,4,1280]{2,1,0:T(4,128)(2,1)}, bf16[24,1280]{1,0:T(8,128)(2,1)S(1)}, f32[24,128]{1,0:T(8,128)S(1)}, f32[24,320]{1,0:T(8,128)S(1)}, f32[3...) custom-call(s32[4]{0:T(128)} %longs_hbm.1, ...), custom_call_target="tpu_custom_call" | custom-call | flops 1000000 | bytes 3000000 | tf_op jit(solution)/shard_map/long_hidden/pallas_call | solution.py:326
  1.7 6.7 %all-to-all-start = ((bf16[8,4,1280]{2,1,0:T(4,128)(2,1)}), bf16[8,4,1280]{2,1,0:T(4,128)(2,1)S(1)}, u32[]{:S(2)}, u32[]{:S(2)}) async-start(bf16[8,4,1280]{2,1,0:T(4,128)(2,1)} %get-tuple-element.29), calls=%async_computation | async-start | bytes 163840 | tf_op jit(solution)/shard_map/long_hidden/all_to_all | solution.py:399
  8.4 3.5 %short_attention.1 = (f32[24,320]{1,0:T(8,128)S(1)}, f32[24,320]{1,0:T(8,128)S(1)}, f32[24,320]{1,0:T(8,128)S(1)}, f32[24,320]{1,0:T(8,128)S(1)}, bf16[4,320,256]{2,1,0:T(8,128)(2,1)S(1)}) custom-call(s32[24]{0:T(128)} %lengths_hbm.1, bf16[3,320,1280]{2,1,0:T(8,128)(2,1)} %bitcast.6, bf16[24,320,128]{2,1,0:T(8,128)(2,1)} %bitcast.7, ...), custom_call_target="tpu_custom_call" | custom-call | flops 1000000000 | bytes 6000000 | tf_op jit(solution)/shard_map/short_attention/pallas_call | solution.py:326
  11.9 3.0 %all-to-all-done.received_ref = bf16[8,4,1280]{2,1,0:T(4,128)(2,1)S(1)} async-done(((bf16[8,4,1280]{2,1,0:T(4,128)(2,1)}), bf16[8,4,1280]{2,1,0:T(4,128)(2,1)S(1)}, u32[]{:S(2)}, u32[]{:S(2)}) %all-to-all-start) | async-done | bytes 81952 | tf_op jit(solution)/shard_map/long_hidden/all_to_all | solution.py:399
  14.9 1.2 %long_attention.1 = (f32[8,8,320]{2,1,0:T(8,128)S(1)}, bf16[320,1280]{1,0:T(8,128)(2,1)S(1)}) custom-call(bf16[320,1280]{1,0:T(8,128)(2,1)} %w_out_hbm.1, bf16[8,4,1280]{2,1,0:T(4,128)(2,1)S(1)} %all-to-all-done.received_ref, f32[320]{0:T(512)S(1)} %get-tuple-element.30.gains_ref, bf16[320,1280]{1,0:T(8,128)(2,1)S(1)} %get-tuple-element.31.w_ref, ...), custom_call_target="tpu_custom_call" | custom-call | flops 100000000 | bytes 4000000 | tf_op jit(solution)/shard_map/long_attention/pallas_call | solution.py:326
  16.0 10.3 %all_to_all.10.parts_ref = f32[8,8,320]{2,1,0:T(8,128)S(1)} all-to-all(f32[8,8,320]{2,1,0:T(8,128)S(1)} %get-tuple-element.37), channel_id=1, replica_groups=mesh['req'=8,'head'=4] {'req'}, dimensions={0} | all-to-all | bytes 163840 | tf_op jit(solution)/shard_map/long_parts/all_to_all | solution.py:427
  26.3 0.3 project.1.refs_7_.left_ref
  26.6 0.1 collective-permute-start
  26.7 2.5 %load.1 = (bf16[24,1280]{1,0:T(8,128)(2,1)S(1)}, f32[1280]{0:T(1024)S(1)}, bf16[2,1280,640]{2,1,0:T(8,128)(2,1)S(1)}, bf16[640,1280]{1,0:T(8,128)(2,1)S(1)}, f32...) custom-call(bf16[24,1280]{1,0:T(8,128)(2,1)} %refs_0_.1, f32[1280]{0:T(1024)} %refs_1_.1, ...), custom_call_target="tpu_custom_call" | custom-call | flops 1000000 | bytes 6000000 | tf_op jit(solution)/shard_map/load/pallas_call | solution.py:326
  29.2 1.7 %collective-permute-done.right_ref = bf16[24,1280]{1,0:T(8,128)(2,1)S(1)} collective-permute-done((bf16[24,1280]{1,0:T(8,128)(2,1)S(1)}, bf16[24,1280]{1,0:T(8,128)(2,1)S(1)}, u32[]{:S(2)}, u32[]{:S(2)}) %collective-permute-start) | collective-permute-done | bytes 61472 | tf_op jit(solution)/shard_map/sum_heads/ppermute | solution.py:350
  30.9 0.2 collective-permute-start.1
  31.1 1.1 %collective-permute-done.1.right_ref = bf16[24,1280]{1,0:T(8,128)(2,1)S(1)} collective-permute-done((bf16[24,1280]{1,0:T(8,128)(2,1)S(1)}, bf16[24,1280]{1,0:T(8,128)(2,1)S(1)}, u32[]{:S(2)}, u32[]{:S(2)}) %collective-permute-start.1) | collective-permute-done | bytes 61472 | tf_op jit(solution)/shard_map/sum_heads/ppermute | solution.py:350
  32.2 1.1 %mlp.1 = (bf16[24,1280]{1,0:T(8,128)(2,1)S(1)}, bf16[24,1280]{1,0:T(8,128)(2,1)S(1)}) custom-call(bf16[24,1280]{1,0:T(8,128)(2,1)S(1)} %sum_heads.1.left_ref, bf16[24,1280]{1,0:T(8,128)(2,1)S(1)} %collective-permute-done.1.right_ref, bf16[24,1280]{1,0:T(8,128)(2,1)S(1)} %get-tuple-element.45.hidden_ref, f32[1280]{0:T(1024)S(1)} %get-tuple-element.46.alpha_ref, ...), custom_call_target="tpu_custom_call" | custom-call | flops 100000000 | bytes 5000000 | tf_op jit(solution)/shard_map/mlp/pallas_call | solution.py:326
  33.3 0.7 %collective-permute-start.2 = (bf16[24,1280]{1,0:T(8,128)(2,1)S(1)}, bf16[24,1280]{1,0:T(8,128)(2,1)S(1)}, u32[]{:S(2)}, u32[]{:S(2)}) collective-permute-start(bf16[24,1280]{1,0:T(8,128)(2,1)S(1)} %get-tuple-element.50.left_ref), channel_id=1, source_target_pairs={{0,3},{1,2},{2,1},{3,0},{4,7},{5,6},{6,5},{7,4},{8,11},{9,10},{10,... | collective-permute-start | bytes 184328 | tf_op jit(solution)/shard_map/sum_units/ppermute | solution.py:350
  34.1 3.3 %collective-permute-done.2.right_ref = bf16[24,1280]{1,0:T(8,128)(2,1)S(1)} collective-permute-done((bf16[24,1280]{1,0:T(8,128)(2,1)S(1)}, bf16[24,1280]{1,0:T(8,128)(2,1)S(1)}, u32[]{:S(2)}, u32[]{:S(2)}) %collective-permute-start.2) | collective-permute-done | bytes 61472 | tf_op jit(solution)/shard_map/sum_units/ppermute | solution.py:350
  37.4 0.2 collective-permute-start.3
  37.6 1.1 %collective-permute-done.3.right_ref = bf16[24,1280]{1,0:T(8,128)(2,1)S(1)} collective-permute-done((bf16[24,1280]{1,0:T(8,128)(2,1)S(1)}, bf16[24,1280]{1,0:T(8,128)(2,1)S(1)}, u32[]{:S(2)}, u32[]{:S(2)}) %collective-permute-start.3) | collective-permute-done | bytes 61472 | tf_op jit(solution)/shard_map/sum_units/ppermute | solution.py:350
  38.7 0.8 %final.1 = bf16[24,1280]{1,0:T(8,128)(2,1)} custom-call(bf16[24,1280]{1,0:T(8,128)(2,1)S(1)} %sum_units.1.left_ref, bf16[24,1280]{1,0:T(8,128)(2,1)S(1)} %collective-permute-done.3.right_ref, bf16[24,1280]{1,0:T(8,128)(2,1)S(1)} %get-tuple-element.51.mid_ref, f32[1280]{0:T(1024)S(1)} %get-tuple-element.52.alpha_ref), custom_call_target="tpu_custom_call" | custom-call | flops 1000000 | bytes 100000 | tf_op jit(solution)/shard_map/final/pallas_call | solution.py:326
  (2 shorter events, 0.0 us)
Async XLA Ops:
  1.7 13.1 %all-to-all-start = ((bf16[8,4,1280]{2,1,0:T(4,128)(2,1)}), bf16[8,4,1280]{2,1,0:T(4,128)(2,1)S(1)}, u32[]{:S(2)}, u32[]{:S(2)}) async-start(bf16[8,4,1280]{2,1,0:T(4,128)(2,1)} %get-tuple-element.29), calls=%async_computation | async-start | bytes 163840 | tf_op jit(solution)/shard_map/long_hidden/all_to_all | solution.py:399
  26.6 4.3 %collective-permute-start = (bf16[24,1280]{1,0:T(8,128)(2,1)S(1)}, bf16[24,1280]{1,0:T(8,128)(2,1)S(1)}, u32[]{:S(2)}, u32[]{:S(2)}) collective-permute-start(bf16[24,1280]{1,0:T(8,128)(2,1)S(1)} %project.1.refs_7_.left_ref), channel_id=1, source_target_pairs={{0,3},{1,2},{2,1},{3,0},{4,7},{5,6},{6,5},{7,4},{8,11},{9,10},{10,... | collective-permute-start | bytes 184328 | tf_op jit(solution)/shard_map/sum_heads/ppermute | solution.py:350
  30.9 1.3 %collective-permute-start.1 = (bf16[24,1280]{1,0:T(8,128)(2,1)S(1)}, bf16[24,1280]{1,0:T(8,128)(2,1)S(1)}, u32[]{:S(2)}, u32[]{:S(2)}) collective-permute-start(bf16[24,1280]{1,0:T(8,128)(2,1)S(1)} %sum_heads.1.left_ref), channel_id=1, source_target_pairs={{0,1},{1,0},{2,3},{3,2},{4,5},{5,4},{6,7},{7,6},{8,9},{9,8},{10,11... | collective-permute-start | bytes 184328 | tf_op jit(solution)/shard_map/sum_heads/ppermute | solution.py:350
  33.3 4.0 %collective-permute-start.2 = (bf16[24,1280]{1,0:T(8,128)(2,1)S(1)}, bf16[24,1280]{1,0:T(8,128)(2,1)S(1)}, u32[]{:S(2)}, u32[]{:S(2)}) collective-permute-start(bf16[24,1280]{1,0:T(8,128)(2,1)S(1)} %get-tuple-element.50.left_ref), channel_id=1, source_target_pairs={{0,3},{1,2},{2,1},{3,0},{4,7},{5,6},{6,5},{7,4},{8,11},{9,10},{10,... | collective-permute-start | bytes 184328 | tf_op jit(solution)/shard_map/sum_units/ppermute | solution.py:350
  37.4 1.3 %collective-permute-start.3 = (bf16[24,1280]{1,0:T(8,128)(2,1)S(1)}, bf16[24,1280]{1,0:T(8,128)(2,1)S(1)}, u32[]{:S(2)}, u32[]{:S(2)}) collective-permute-start(bf16[24,1280]{1,0:T(8,128)(2,1)S(1)} %sum_units.1.left_ref), channel_id=1, source_target_pairs={{0,1},{1,0},{2,3},{3,2},{4,5},{5,4},{6,7},{7,6},{8,9},{9,8},{10,11... | collective-permute-start | bytes 184328 | tf_op jit(solution)/shard_map/sum_units/ppermute | solution.py:350

commit v5 on v4

--- a/solution.py
+++ b/solution.py
@@ -9,7 +9,7 @@
 
 HEAD_DIM = 64
 EPS = 1e-06
-LOW = -1e30
+LOW = -3e38
 F32 = jnp.float32
 BF16 = jnp.bfloat16
 LANES = 8
@@ -161,66 +161,63 @@
         ],
         sems,
     )
-    slots = keys_ref.shape[2]
-    masks = head_masks(width)
-    diagonal = head_rows(width)
-    sub = lax.broadcasted_iota(jnp.int32, (2 * LANES, 2 * slots), 0)
-    lane = lax.broadcasted_iota(jnp.int32, (2 * LANES, 2 * slots), 1)
-    second = sub >= LANES
-    first = jnp.where(second, slots, 0)
-    hidden = hidden_ref[...]
-    query = query_ref[...]
-    pairs = [
-        jnp.concatenate(
-            [jnp.where(diagonal, query[r + i : r + i + 1], 0.0) for i in range(2)], axis=0
-        ).astype(BF16)
-        for r in range(0, rows, 2)
-    ]
-    key = head_unit(dot_t(hidden, w_key_ref[...]), gains_ref[...][None, :], masks)
-    own_ref[...] = spread_sums(query * key, masks, lambda total: total)
-    copies[0].wait()
-    weights, scales = [], []
-    for p, r in enumerate(range(0, rows, 2)):
-        if r in (0, rows // 2):
-            copies[1 + (r > 0)].wait()
-        scores = dot(pairs[p], jnp.concatenate([keys_ref[r], keys_ref[r + 1]], axis=1))
-        last = jnp.where(second, slots + lengths_ref[r + 1], lengths_ref[r])
-        valid = (lane >= first) & (lane < last)
-        scores = jnp.where(valid, scores, LOW)
-        top = jnp.max(scores, axis=-1, keepdims=True)
-        weight = jnp.where(valid, jnp.exp(scores - top), 0.0)
-        total = jnp.sum(weight, axis=-1, keepdims=True)
-        weights.append(weight.astype(BF16))
-        scales.append(1.0 / total)
-        lse = top + jnp.log(total)
-        for i in range(2):
-            part = slice(i * LANES, (i + 1) * LANES)
-            lse_ref[r + i : r + i + 1, :] = gathered(lse[part], diagonal)
-    copies[3].wait()
-    value_ref[...] = dot_t(hidden, w_value_ref[...]).astype(BF16).astype(F32)
-    copies[4].wait()
-    for p, r in enumerate(range(0, rows, 2)):
-        summed = dot_t(weights[p], jnp.concatenate([values_ref[r], values_ref[r + 1]], axis=1))
-        summed = summed * scales[p]
-        for i in range(2):
-            part = slice(i * LANES, (i + 1) * LANES)
-            out_ref[r + i : r + i + 1, :] = gathered(summed[part], diagonal)
-    copies[5].wait()
+    @pl.when(lax.axis_index("req") >= 0)
+    def _():
+        slots = keys_ref.shape[2]
+        masks = head_masks(width)
+        diagonal = head_rows(width)
+        sub = lax.broadcasted_iota(jnp.int32, (2 * LANES, 2 * slots), 0)
+        lane = lax.broadcasted_iota(jnp.int32, (2 * LANES, 2 * slots), 1)
+        second = sub >= LANES
+        first = jnp.where(second, slots, 0)
+        hidden = hidden_ref[...]
+        query = query_ref[...]
+        pairs = [
+            jnp.concatenate(
+                [jnp.where(diagonal, query[r + i : r + i + 1], 0.0) for i in range(2)], axis=0
+            ).astype(BF16)
+            for r in range(0, rows, 2)
+        ]
+        key = head_unit(dot_t(hidden, w_key_ref[...]), gains_ref[...][None, :], masks)
+        own_ref[...] = spread_sums(query * key, masks, lambda total: total)
+        copies[0].wait()
+        weights, scales = [], []
+        for p, r in enumerate(range(0, rows, 2)):
+            if r in (0, rows // 2):
+                copies[1 + (r > 0)].wait()
+            scores = dot(pairs[p], jnp.concatenate([keys_ref[r], keys_ref[r + 1]], axis=1))
+            last = jnp.where(second, slots + lengths_ref[r + 1], lengths_ref[r])
+            valid = (lane >= first) & (lane < last)
+            scores = jnp.where(valid, scores, LOW)
+            top = jnp.max(scores, axis=-1, keepdims=True)
+            weight = jnp.where(valid, jnp.exp(scores - top), 0.0)
+            total = jnp.sum(weight, axis=-1, keepdims=True)
+            weights.append(weight.astype(BF16))
+            scales.append(1.0 / total)
+            lse = top + jnp.log(total)
+            for i in range(2):
+                part = slice(i * LANES, (i + 1) * LANES)
+                lse_ref[r + i : r + i + 1, :] = gathered(lse[part], diagonal)
+        copies[3].wait()
+        value_ref[...] = dot_t(hidden, w_value_ref[...]).astype(BF16).astype(F32)
+        copies[4].wait()
+        for p, r in enumerate(range(0, rows, 2)):
+            summed = dot_t(weights[p], jnp.concatenate([values_ref[r], values_ref[r + 1]], axis=1))
+            summed = summed * scales[p]
+            for i in range(2):
+                part = slice(i * LANES, (i + 1) * LANES)
+                out_ref[r + i : r + i + 1, :] = gathered(summed[part], diagonal)
+        copies[5].wait()
 
 
 def long_kernel(
-    w_out_hbm,
     received_ref,
     gains_ref,
     w_ref,
     keys_ref,
     values_ref,
     sent_ref,
-    w_out_ref,
-    sems,
-):
-    copy = pltpu.make_async_copy(w_out_hbm, w_out_ref, sems.at[0])
-    copy.start()
+):
     parties, longs, _ = received_ref.shape
     width = w_ref.shape[0]
     hidden = received_ref[0].astype(F32)
@@ -233,38 +230,53 @@
         dot(jnp.where(diagonal, query[i : i + 1], 0.0).astype(BF16), keys_ref[i])
         for i in range(longs)
     ]
-    outs, lses = [], []
+    padded = sent_ref.shape[2]
+    sub = lax.broadcasted_iota(jnp.int32, (LANES, padded), 0)
+    lane = lax.broadcasted_iota(jnp.int32, (LANES, padded), 1)
+    kept = ((lane >= sub * HEAD_DIM) & (lane < (sub + 1) * HEAD_DIM) & (lane < width)) | (
+        lane == width + sub
+    )
+    outs = []
     for i in range(longs):
         top = jnp.max(scores[i], axis=-1, keepdims=True)
         weights = jnp.exp(scores[i] - top)
         total = jnp.sum(weights, axis=-1, keepdims=True)
-        summed = dot_t(weights.astype(BF16), values_ref[i])
-        outs.append(gathered(summed / total, diagonal))
-        lses.append(gathered(top + jnp.log(total), diagonal))
-    packed = jnp.concatenate(outs + lses, axis=0)
+        summed = dot_t(weights.astype(BF16), values_ref[i]) / total
+        summed = jnp.concatenate([summed, jnp.zeros((LANES, padded - width), F32)], axis=1)
+        row = jnp.where(lane < width, summed, top + jnp.log(total))
+        outs.append(jnp.sum(jnp.where(kept, row, 0.0), axis=0, keepdims=True))
+    packed = jnp.concatenate(outs, axis=0)
     for party in range(parties):
         sent_ref[party] = packed
-    copy.wait()
 
 
 def project_kernel(
     parts_ref, short_ref, short_lse_ref, value_ref, own_ref, match_ref, w_ref, out_ref
 ):
-    parties, doubled, width = parts_ref.shape
-    longs = doubled // 2
-    top = parts_ref[0]
-    for party in range(1, parties):
-        top = jnp.maximum(top, parts_ref[party])
-    top = top[longs:]
-    total = jnp.zeros((longs, width), F32)
-    acc = jnp.zeros((longs, width), F32)
+    parties, longs, padded = parts_ref.shape
+    width = short_ref.shape[1]
+    masks = head_masks(width)
+    last = padded - 128
+    first = width - last
+
+    def on_heads(compact):
+        result = jnp.zeros((longs, width), F32)
+        for h, mask in enumerate(masks):
+            result = jnp.where(mask, compact[:, first + h : first + h + 1], result)
+        return result
+
+    lses = [parts_ref[party][:, last:] for party in range(parties)]
+    top = lses[0]
+    for lse in lses[1:]:
+        top = jnp.maximum(top, lse)
+    weights = [jnp.exp(lse - top) for lse in lses]
+    total = weights[0]
+    for weight in weights[1:]:
+        total = total + weight
+    long_out = jnp.zeros((longs, width), F32)
     for party in range(parties):
-        part = parts_ref[party]
-        weight = jnp.exp(part[longs:] - top)
-        total = total + weight
-        acc = acc + weight * part[:longs]
-    long_out = acc / total
-    long_lse = top + jnp.log(total)
+        long_out = long_out + on_heads(weights[party] / total) * parts_ref[party][:, :width]
+    long_lse = on_heads(top + jnp.log(total))
     cached = short_ref[...]
     lse = short_lse_ref[...]
     for index in range(longs):
@@ -279,15 +291,7 @@
     out_ref[...] = dot(attended.astype(BF16), w_ref[...]).astype(BF16)
 
 
-def load_kernel(*refs):
-    count = (len(refs) - 2) // 2
-    copies = start_all(list(zip(refs[:count], refs[count + 1 : -1])), refs[-1])
-    for copy in copies:
-        copy.wait()
-
-
-def add_kernel(left_ref, right_ref, *refs):
-    out_ref = refs[-1]
+def add_kernel(left_ref, right_ref, out_ref):
     out_ref[...] = (left_ref[...].astype(F32) + right_ref[...].astype(F32)).astype(BF16)
 
 
@@ -415,13 +419,11 @@
             copies=6,
         )
     with jax.named_scope("long_attention"):
-        partial, w_out = call(
+        (partial,) = call(
             long_kernel,
-            (shape((parties, 2 * longs, width), F32), like(w_out)),
-            (10**8, 4 * 10**6),
-            far=(w_out,),
+            (shape((parties, longs, (width // 128 + 1) * 128), F32),),
+            (10**9, 4 * 10**6),
             near=(received, gains, w_query, keys, values),
-            copies=1,
         )
     with jax.named_scope("long_parts"):
         parts = lax.all_to_all(partial, "req", 0, 0)
@@ -429,23 +431,13 @@
         (projected,) = call(
             project_kernel,
             (wide,),
-            (2 * rows * width * model, 10**6),
+            (2 * 10**10, 10**6),
             near=(parts, short_out, short_lse, value, own, match, w_out),
         )
-    with jax.named_scope("load"):
-        loads = (hidden, alpha_attn, w_gate_up, w_down, s_gate, s_up, alpha_mlp)
-        hidden, alpha_attn, w_gate_up, w_down, s_gate, s_up, alpha_mlp = call(
-            load_kernel,
-            [like(a) for a in loads],
-            (10**6, 6 * 10**6),
-            far=loads,
-            near=(projected,),
-            copies=len(loads),
-        )
     with jax.named_scope("sum_heads"):
+        other = exchanged(projected, 1)
+        (projected,) = call(add_kernel, (wide,), (10**5, 10**5), near=(projected, other))
         other = exchanged(projected, 3)
-        (projected,) = call(add_kernel, (wide,), (10**5, 10**5), near=(projected, other, s_up))
-        other = exchanged(projected, 1)
     with jax.named_scope("mlp"):
         middle, downward = call(
             mlp_kernel,

time: 39.8 us -> 39.2 us (0.985)
  Pallas kernels: 11.2 us -> 8.58 us
  starting transfers between devices: 7.91 us -> 9.66 us
  waiting for transfers between devices: 10.1 us -> 10.6 us
    pallas_call x9 -> x8, Pallas kernels: 11.2 us -> 8.58 us  [call(): pl.pallas_call(kernel, in_specs=[HBM] * len(far) + [VMEM] * len(near), ou...]
    ppermute x4, starting transfers between devices: 1.21 us -> 2.96 us  [exchanged(): return lax.ppermute(value, 'head', [(i, i ^ step) for i in range(places)])]
    ppermute x4, waiting for transfers between devices: 7.15 us -> 7.67 us  [exchanged(): return lax.ppermute(value, 'head', [(i, i ^ step) for i in range(places)])]
  transfers between devices with their start and end apart: 5 -> 5, of which waited for: 5 -> 5; matrix products, arithmetic and copies ran while one was open for 0% -> 0% of each run, Pallas kernels for 15% -> 9%
where the time goes in v5:
time: 39.2 us; the launch traced here: 39 us
  waiting for transfers between devices  10.6 us (27%)
  blocking collectives  9.92 us (25%)
  starting transfers between devices  9.66 us (25%)
  Pallas kernels  8.58 us (22%)
    all_to_all x1, blocking collectives, on_device(): parts = lax.all_to_all(partial, 'req', 0, 0)  9.92 us
    pallas_call x8, Pallas kernels, call(): pl.pallas_call(kernel, in_specs=[HBM] * len(far) + [VMEM] * len(near), ou...  8.58 us
    ppermute x4, waiting for transfers between devices, exchanged(): return lax.ppermute(value, 'head', [(i, i ^ step) for i in range(places)])  7.67 us
    all_to_all x1, starting transfers between devices, on_device(): lax.all_to_all(sent, ('req', 'head'), 0, 0, axis_index_groups=mixed_group...  6.7 us
    all_to_all x1, waiting for transfers between devices, on_device(): lax.all_to_all(sent, ('req', 'head'), 0, 0, axis_index_groups=mixed_group...  2.96 us
    ppermute x4, starting transfers between devices, exchanged(): return lax.ppermute(value, 'head', [(i, i ^ step) for i in range(places)])  2.96 us
  transfers between devices with their start and end apart: 5, of which 5 were waited for; matrix products, arithmetic and copies ran while one was open for 0% of the time, Pallas kernels for 9%

profile of v5, /device:TPU:0, one launch (start us, length us, event | category | flops | bytes accessed | tf_op | source)
XLA Modules:
  0.0 39.0 jit_solution(1239287300984722674)
XLA Ops:
  0.0 1.7 %long_hidden.1 = (bf16[8,4,1280]{2,1,0:T(4,128)(2,1)}, bf16[24,1280]{1,0:T(8,128)(2,1)S(1)}, f32[24,128]{1,0:T(8,128)S(1)}, f32[24,320]{1,0:T(8,128)S(1)}, f32[3...) custom-call(s32[4]{0:T(128)} %longs_hbm.1, ...), custom_call_target="tpu_custom_call" | custom-call | flops 1000000 | bytes 3000000 | tf_op jit(solution)/shard_map/long_hidden/pallas_call | solution.py:330
  1.7 6.7 %all-to-all-start = ((bf16[8,4,1280]{2,1,0:T(4,128)(2,1)}), bf16[8,4,1280]{2,1,0:T(4,128)(2,1)S(1)}, u32[]{:S(2)}, u32[]{:S(2)}) async-start(bf16[8,4,1280]{2,1,0:T(4,128)(2,1)} %get-tuple-element.20), calls=%async_computation | async-start | bytes 163840 | tf_op jit(solution)/shard_map/long_hidden/all_to_all | solution.py:403
  8.4 3.5 %short_attention.1 = (f32[24,320]{1,0:T(8,128)S(1)}, f32[24,320]{1,0:T(8,128)S(1)}, f32[24,320]{1,0:T(8,128)S(1)}, f32[24,320]{1,0:T(8,128)S(1)}, bf16[4,320,256]{2,1,0:T(8,128)(2,1)S(1)}) custom-call(s32[24]{0:T(128)} %lengths_hbm.1, bf16[3,320,1280]{2,1,0:T(8,128)(2,1)} %bitcast.6, bf16[24,320,128]{2,1,0:T(8,128)(2,1)} %bitcast.7, ...), custom_call_target="tpu_custom_call" | custom-call | flops 1000000000 | bytes 6000000 | tf_op jit(solution)/shard_map/short_attention/pallas_call | solution.py:330
  11.9 0.0 copy-start.7
  11.9 3.0 %all-to-all-done.received_ref = bf16[8,4,1280]{2,1,0:T(4,128)(2,1)S(1)} async-done(((bf16[8,4,1280]{2,1,0:T(4,128)(2,1)}), bf16[8,4,1280]{2,1,0:T(4,128)(2,1)S(1)}, u32[]{:S(2)}, u32[]{:S(2)}) %all-to-all-start) | async-done | bytes 81952 | tf_op jit(solution)/shard_map/long_hidden/all_to_all | solution.py:403
  14.9 1.0 %long_attention.1 = f32[8,4,384]{2,1,0:T(4,128)S(1)} custom-call(bf16[8,4,1280]{2,1,0:T(4,128)(2,1)S(1)} %all-to-all-done.received_ref, f32[320]{0:T(512)S(1)} %get-tuple-element.21.gains_ref, bf16[320,1280]{1,0:T(8,128)(2,1)S(1)} %get-tuple-element.22.w_ref, bf16[4,320,256]{2,1,0:T(8,128)(2,1)S(1)} %get-tuple-element.23.keys_ref, ...), custom_call_target="tpu_custom_call" | custom-call | flops 1000000000 | bytes 4000000 | tf_op jit(solution)/shard_map/long_attention/pallas_call | solution.py:330
  15.9 9.9 %all_to_all.10.parts_ref = f32[8,4,384]{2,1,0:T(4,128)S(1)} all-to-all(f32[8,4,384]{2,1,0:T(4,128)S(1)} %long_attention.1), channel_id=1, replica_groups=mesh['req'=8,'head'=4] {'req'}, dimensions={0} | all-to-all | bytes 98304 | tf_op jit(solution)/shard_map/long_parts/all_to_all | solution.py:429
  25.8 0.0 copy-done.7
  25.8 0.0 copy-start
  25.8 0.0 copy-start.1
  25.8 0.0 copy-start.3
  25.8 0.0 copy-start.5
  25.8 0.0 copy-start.6
  25.9 0.4 project.1.left_ref
  26.2 0.1 collective-permute-start
  26.3 1.2 %collective-permute-done.right_ref = bf16[24,1280]{1,0:T(8,128)(2,1)S(1)} collective-permute-done((bf16[24,1280]{1,0:T(8,128)(2,1)S(1)}, bf16[24,1280]{1,0:T(8,128)(2,1)S(1)}, u32[]{:S(2)}, u32[]{:S(2)}) %collective-permute-start) | collective-permute-done | bytes 61472 | tf_op jit(solution)/shard_map/sum_heads/ppermute | solution.py:354
  27.6 0.0 copy-start.4
  27.6 1.3 %collective-permute-start.1 = (bf16[24,1280]{1,0:T(8,128)(2,1)S(1)}, bf16[24,1280]{1,0:T(8,128)(2,1)S(1)}, u32[]{:S(2)}, u32[]{:S(2)}) collective-permute-start(bf16[24,1280]{1,0:T(8,128)(2,1)S(1)} %sum_heads.1.left_ref), channel_id=1, source_target_pairs={{0,3},{1,2},{2,1},{3,0},{4,7},{5,6},{6,5},{7,4},{8,11},{9,10},{10,... | collective-permute-start | bytes 184328 | tf_op jit(solution)/shard_map/sum_heads/ppermute | solution.py:354
  28.9 2.7 %collective-permute-done.1.right_ref = bf16[24,1280]{1,0:T(8,128)(2,1)S(1)} collective-permute-done((bf16[24,1280]{1,0:T(8,128)(2,1)S(1)}, bf16[24,1280]{1,0:T(8,128)(2,1)S(1)}, u32[]{:S(2)}, u32[]{:S(2)}) %collective-permute-start.1) | collective-permute-done | bytes 61472 | tf_op jit(solution)/shard_map/sum_heads/ppermute | solution.py:354
  31.6 0.0 copy-done
  31.6 0.0 copy-done.1
  31.6 0.0 copy-done.2
  31.6 0.0 copy-done.3
  31.6 0.0 copy-done.5
  31.6 0.0 copy-done.6
  31.7 1.1 %mlp.1 = (bf16[24,1280]{1,0:T(8,128)(2,1)S(1)}, bf16[24,1280]{1,0:T(8,128)(2,1)S(1)}) custom-call(bf16[24,1280]{1,0:T(8,128)(2,1)S(1)} %sum_heads.1.left_ref, bf16[24,1280]{1,0:T(8,128)(2,1)S(1)} %collective-permute-done.1.right_ref, bf16[24,1280]{1,0:T(8,128)(2,1)S(1)} %copy-done.2, f32[1280]{0:T(1024)S(1)} %copy-done.3, bf16[2,1280,640]{2,1,0:T(8,128)(2,1)S(1)} %copy-done, ...), custom_call_target="tpu_custom_call" | custom-call | flops 100000000 | bytes 5000000 | tf_op jit(solution)/shard_map/mlp/pallas_call | solution.py:330
  32.8 1.3 %collective-permute-start.2 = (bf16[24,1280]{1,0:T(8,128)(2,1)S(1)}, bf16[24,1280]{1,0:T(8,128)(2,1)S(1)}, u32[]{:S(2)}, u32[]{:S(2)}) collective-permute-start(bf16[24,1280]{1,0:T(8,128)(2,1)S(1)} %get-tuple-element.33.left_ref), channel_id=1, source_target_pairs={{0,3},{1,2},{2,1},{3,0},{4,7},{5,6},{6,5},{7,4},{8,11},{9,10},{10,... | collective-permute-start | bytes 184328 | tf_op jit(solution)/shard_map/sum_units/ppermute | solution.py:354
  34.1 2.7 %collective-permute-done.2.right_ref = bf16[24,1280]{1,0:T(8,128)(2,1)S(1)} collective-permute-done((bf16[24,1280]{1,0:T(8,128)(2,1)S(1)}, bf16[24,1280]{1,0:T(8,128)(2,1)S(1)}, u32[]{:S(2)}, u32[]{:S(2)}) %collective-permute-start.2) | collective-permute-done | bytes 61472 | tf_op jit(solution)/shard_map/sum_units/ppermute | solution.py:354
  36.8 0.2 collective-permute-start.3
  37.0 1.1 %collective-permute-done.3.right_ref = bf16[24,1280]{1,0:T(8,128)(2,1)S(1)} collective-permute-done((bf16[24,1280]{1,0:T(8,128)(2,1)S(1)}, bf16[24,1280]{1,0:T(8,128)(2,1)S(1)}, u32[]{:S(2)}, u32[]{:S(2)}) %collective-permute-start.3) | collective-permute-done | bytes 61472 | tf_op jit(solution)/shard_map/sum_units/ppermute | solution.py:354
  38.1 0.0 copy-done.4
  38.1 0.8 %final.1 = bf16[24,1280]{1,0:T(8,128)(2,1)} custom-call(bf16[24,1280]{1,0:T(8,128)(2,1)S(1)} %sum_units.1.left_ref, bf16[24,1280]{1,0:T(8,128)(2,1)S(1)} %collective-permute-done.3.right_ref, bf16[24,1280]{1,0:T(8,128)(2,1)S(1)} %get-tuple-element.34.mid_ref, f32[1280]{0:T(1024)S(1)} %copy-done.4), custom_call_target="tpu_custom_call" | custom-call | flops 1000000 | bytes 100000 | tf_op jit(solution)/shard_map/final/pallas_call | solution.py:330
  (3 shorter events, 0.0 us)
Async XLA Ops:
  1.7 13.1 %all-to-all-start = ((bf16[8,4,1280]{2,1,0:T(4,128)(2,1)}), bf16[8,4,1280]{2,1,0:T(4,128)(2,1)S(1)}, u32[]{:S(2)}, u32[]{:S(2)}) async-start(bf16[8,4,1280]{2,1,0:T(4,128)(2,1)} %get-tuple-element.20), calls=%async_computation | async-start | bytes 163840 | tf_op jit(solution)/shard_map/long_hidden/all_to_all | solution.py:403
  11.9 13.9 %copy-start.7 = (bf16[320,1280]{1,0:T(8,128)(2,1)S(1)}, bf16[320,1280]{1,0:T(8,128)(2,1)}, u32[]{:S(2)}) copy-start(bf16[320,1280]{1,0:T(8,128)(2,1)} %w_ref.1) | copy-start | bytes 2457604
  25.8 5.8 %copy-start = (bf16[2,1280,640]{2,1,0:T(8,128)(2,1)S(1)}, bf16[2,1280,640]{2,1,0:T(8,128)(2,1)}, u32[]{:S(2)}) copy-start(bf16[2,1280,640]{2,1,0:T(8,128)(2,1)} %w_gate_up_ref.1) | copy-start | bytes 9830404
  25.8 5.8 %copy-start.1 = (bf16[640,1280]{1,0:T(8,128)(2,1)S(1)}, bf16[640,1280]{1,0:T(8,128)(2,1)}, u32[]{:S(2)}) copy-start(bf16[640,1280]{1,0:T(8,128)(2,1)} %w_down_ref.1) | copy-start | bytes 4915204
  25.8 5.8 %copy-start.2 = (bf16[24,1280]{1,0:T(8,128)(2,1)S(1)}, bf16[24,1280]{1,0:T(8,128)(2,1)}, u32[]{:S(2)}) copy-start(bf16[24,1280]{1,0:T(8,128)(2,1)} %hidden_ref.1) | copy-start | bytes 184324
  25.8 5.8 %copy-start.3 = (f32[1280]{0:T(1024)S(1)}, f32[1280]{0:T(1024)}, u32[]{:S(2)}) copy-start(f32[1280]{0:T(1024)} %alpha_ref.2) | copy-start | bytes 15364
  25.8 5.8 %copy-start.5 = (f32[640]{0:T(1024)S(1)}, f32[640]{0:T(1024)}, u32[]{:S(2)}) copy-start(f32[640]{0:T(1024)} %s_gate_ref.1) | copy-start | bytes 7684
  25.8 5.8 %copy-start.6 = (f32[640]{0:T(1024)S(1)}, f32[640]{0:T(1024)}, u32[]{:S(2)}) copy-start(f32[640]{0:T(1024)} %s_up_ref.1) | copy-start | bytes 7684
  26.2 1.3 %collective-permute-start = (bf16[24,1280]{1,0:T(8,128)(2,1)S(1)}, bf16[24,1280]{1,0:T(8,128)(2,1)S(1)}, u32[]{:S(2)}, u32[]{:S(2)}) collective-permute-start(bf16[24,1280]{1,0:T(8,128)(2,1)S(1)} %project.1.left_ref), channel_id=1, source_target_pairs={{0,1},{1,0},{2,3},{3,2},{4,5},{5,4},{6,7},{7,6},{8,9},{9,8},{10,11... | collective-permute-start | bytes 184328 | tf_op jit(solution)/shard_map/sum_heads/ppermute | solution.py:354
  27.6 10.5 %copy-start.4 = (f32[1280]{0:T(1024)S(1)}, f32[1280]{0:T(1024)}, u32[]{:S(2)}) copy-start(f32[1280]{0:T(1024)} %alpha_ref.3) | copy-start | bytes 15364
  27.6 4.0 %collective-permute-start.1 = (bf16[24,1280]{1,0:T(8,128)(2,1)S(1)}, bf16[24,1280]{1,0:T(8,128)(2,1)S(1)}, u32[]{:S(2)}, u32[]{:S(2)}) collective-permute-start(bf16[24,1280]{1,0:T(8,128)(2,1)S(1)} %sum_heads.1.left_ref), channel_id=1, source_target_pairs={{0,3},{1,2},{2,1},{3,0},{4,7},{5,6},{6,5},{7,4},{8,11},{9,10},{10,... | collective-permute-start | bytes 184328 | tf_op jit(solution)/shard_map/sum_heads/ppermute | solution.py:354
  32.8 4.0 %collective-permute-start.2 = (bf16[24,1280]{1,0:T(8,128)(2,1)S(1)}, bf16[24,1280]{1,0:T(8,128)(2,1)S(1)}, u32[]{:S(2)}, u32[]{:S(2)}) collective-permute-start(bf16[24,1280]{1,0:T(8,128)(2,1)S(1)} %get-tuple-element.33.left_ref), channel_id=1, source_target_pairs={{0,3},{1,2},{2,1},{3,0},{4,7},{5,6},{6,5},{7,4},{8,11},{9,10},{10,... | collective-permute-start | bytes 184328 | tf_op jit(solution)/shard_map/sum_units/ppermute | solution.py:354
  36.8 1.3 %collective-permute-start.3 = (bf16[24,1280]{1,0:T(8,128)(2,1)S(1)}, bf16[24,1280]{1,0:T(8,128)(2,1)S(1)}, u32[]{:S(2)}, u32[]{:S(2)}) collective-permute-start(bf16[24,1280]{1,0:T(8,128)(2,1)S(1)} %sum_units.1.left_ref), channel_id=1, source_target_pairs={{0,1},{1,0},{2,3},{3,2},{4,5},{5,4},{6,7},{7,6},{8,9},{9,8},{10,11... | collective-permute-start | bytes 184328 | tf_op jit(solution)/shard_map/sum_units/ppermute | solution.py:354

commit v6 on v5

--- a/solution.py
+++ b/solution.py
@@ -342,10 +342,14 @@
     return jax.ShapeDtypeStruct(array.shape, array.dtype)
 
 
+def centre_first(parties):
+    return sorted(range(parties), key=lambda r: (r != parties // 2, r))
+
+
 def mixed_groups(parties):
     places = lax.axis_size("head")
     return [
-        [r * places + (h ^ ((r // 2) % 2)) for r in range(parties)] for h in range(places)
+        [r * places + (h ^ ((r // 2) % 2)) for r in centre_first(parties)] for h in range(places)
     ]
 
 
@@ -426,7 +430,9 @@
             near=(received, gains, w_query, keys, values),
         )
     with jax.named_scope("long_parts"):
-        parts = lax.all_to_all(partial, "req", 0, 0)
+        parts = lax.all_to_all(
+            partial, "req", 0, 0, axis_index_groups=[centre_first(parties)]
+        )
     with jax.named_scope("project"):
         (projected,) = call(
             project_kernel,

time: 39.2 us -> 36.5 us (0.931)
  waiting for transfers between devices: 10.6 us -> 8.27 us
  blocking collectives: 9.92 us -> 8.96 us
  starting transfers between devices: 9.66 us -> 10.3 us
    all_to_all x1, waiting for transfers between devices: 2.96 us -> 0.6 us  [on_device(): lax.all_to_all(sent, ('req', 'head'), 0, 0, axis_index_groups=mixed_group...]
    all_to_all x1, blocking collectives: 9.92 us -> 8.96 us  [on_device(): lax.all_to_all(partial, 'req', 0, 0, axis_index_groups=[centre_first(part...]
    all_to_all x1, starting transfers between devices: 6.7 us -> 7.31 us  [on_device(): lax.all_to_all(sent, ('req', 'head'), 0, 0, axis_index_groups=mixed_group...]
  transfers between devices with their start and end apart: 5 -> 5, of which waited for: 5 -> 5; matrix products, arithmetic and copies ran while one was open for 0% -> 0% of each run, Pallas kernels for 9% -> 10%
where the time goes in v6:
time: 36.5 us; the launch traced here: 36.2 us
  starting transfers between devices  10.3 us (28%)
  blocking collectives  8.96 us (25%)
  Pallas kernels  8.58 us (24%)
  waiting for transfers between devices  8.27 us (23%)
    all_to_all x1, blocking collectives, on_device(): lax.all_to_all(partial, 'req', 0, 0, axis_index_groups=[centre_first(part...  8.96 us
    pallas_call x8, Pallas kernels, call(): pl.pallas_call(kernel, in_specs=[HBM] * len(far) + [VMEM] * len(near), ou...  8.58 us
    ppermute x4, waiting for transfers between devices, exchanged(): return lax.ppermute(value, 'head', [(i, i ^ step) for i in range(places)])  7.67 us
    all_to_all x1, starting transfers between devices, on_device(): lax.all_to_all(sent, ('req', 'head'), 0, 0, axis_index_groups=mixed_group...  7.31 us
    ppermute x4, starting transfers between devices, exchanged(): return lax.ppermute(value, 'head', [(i, i ^ step) for i in range(places)])  2.96 us
  transfers between devices with their start and end apart: 5, of which 5 were waited for; matrix products, arithmetic and copies ran while one was open for 0% of the time, Pallas kernels for 10%

profile of v6, /device:TPU:0, one launch (start us, length us, event | category | flops | bytes accessed | tf_op | source)
XLA Modules:
  0.0 36.2 jit_solution(1558485952372009179)
XLA Ops:
  0.0 1.7 %long_hidden.1 = (bf16[8,4,1280]{2,1,0:T(4,128)(2,1)}, bf16[24,1280]{1,0:T(8,128)(2,1)S(1)}, f32[24,128]{1,0:T(8,128)S(1)}, f32[24,320]{1,0:T(8,128)S(1)}, f32[3...) custom-call(s32[4]{0:T(128)} %longs_hbm.1, ...), custom_call_target="tpu_custom_call" | custom-call | flops 1000000 | bytes 3000000 | tf_op jit(solution)/shard_map/long_hidden/pallas_call | solution.py:330
  1.7 7.3 %all-to-all-start = ((bf16[8,4,1280]{2,1,0:T(4,128)(2,1)}), bf16[8,4,1280]{2,1,0:T(4,128)(2,1)S(1)}, u32[]{:S(2)}, u32[]{:S(2)}) async-start(bf16[8,4,1280]{2,1,0:T(4,128)(2,1)} %get-tuple-element.20), calls=%async_computation | async-start | bytes 163840 | tf_op jit(solution)/shard_map/long_hidden/all_to_all | solution.py:407
  9.0 3.5 %short_attention.1 = (f32[24,320]{1,0:T(8,128)S(1)}, f32[24,320]{1,0:T(8,128)S(1)}, f32[24,320]{1,0:T(8,128)S(1)}, f32[24,320]{1,0:T(8,128)S(1)}, bf16[4,320,256]{2,1,0:T(8,128)(2,1)S(1)}) custom-call(s32[24]{0:T(128)} %lengths_hbm.1, bf16[3,320,1280]{2,1,0:T(8,128)(2,1)} %bitcast.6, bf16[24,320,128]{2,1,0:T(8,128)(2,1)} %bitcast.7, ...), custom_call_target="tpu_custom_call" | custom-call | flops 1000000000 | bytes 6000000 | tf_op jit(solution)/shard_map/short_attention/pallas_call | solution.py:330
  12.5 0.0 copy-start.7
  12.5 0.6 %all-to-all-done.received_ref = bf16[8,4,1280]{2,1,0:T(4,128)(2,1)S(1)} async-done(((bf16[8,4,1280]{2,1,0:T(4,128)(2,1)}), bf16[8,4,1280]{2,1,0:T(4,128)(2,1)S(1)}, u32[]{:S(2)}, u32[]{:S(2)}) %all-to-all-start) | async-done | bytes 81952 | tf_op jit(solution)/shard_map/long_hidden/all_to_all | solution.py:407
  13.1 1.0 %long_attention.1 = f32[8,4,384]{2,1,0:T(4,128)S(1)} custom-call(bf16[8,4,1280]{2,1,0:T(4,128)(2,1)S(1)} %all-to-all-done.received_ref, f32[320]{0:T(512)S(1)} %get-tuple-element.21.gains_ref, bf16[320,1280]{1,0:T(8,128)(2,1)S(1)} %get-tuple-element.22.w_ref, bf16[4,320,256]{2,1,0:T(8,128)(2,1)S(1)} %get-tuple-element.23.keys_ref, ...), custom_call_target="tpu_custom_call" | custom-call | flops 1000000000 | bytes 4000000 | tf_op jit(solution)/shard_map/long_attention/pallas_call | solution.py:330
  14.1 9.0 %all_to_all.10.parts_ref = f32[8,4,384]{2,1,0:T(4,128)S(1)} all-to-all(f32[8,4,384]{2,1,0:T(4,128)S(1)} %long_attention.1), channel_id=1, replica_groups={{16,0,4,8,12,20,24,28},{17,1,5,9,13,21,25,29},{18,2,6,10,14,22,26,30},{..., dimensions={0} | all-to-all | bytes 98304 | tf_op jit(solution)/shard_map/long_parts/all_to_all | solution.py:433
  23.1 0.0 copy-done.7
  23.1 0.0 copy-start
  23.1 0.0 copy-start.1
  23.1 0.0 copy-start.3
  23.1 0.0 copy-start.5
  23.1 0.0 copy-start.6
  23.1 0.4 %project.1.left_ref = bf16[24,1280]{1,0:T(8,128)(2,1)S(1)} custom-call(f32[8,4,384]{2,1,0:T(4,128)S(1)} %all_to_all.10.parts_ref, f32[24,320]{1,0:T(8,128)S(1)} %get-tuple-element.28.short_ref, f32[24,320]{1,0:T(8,128)S(1)} %get-tuple-element.29.short_lse_ref, f32[24,320]{1,0:T(8,128)S(1)} %get-tuple-element.30.value_ref, ...), custom_call_target="tpu_custom_call" | custom-call | flops 20000000000 | bytes 1000000 | tf_op jit(solution)/shard_map/project/pallas_call | solution.py:330
  23.5 0.1 collective-permute-start
  23.6 1.2 %collective-permute-done.right_ref = bf16[24,1280]{1,0:T(8,128)(2,1)S(1)} collective-permute-done((bf16[24,1280]{1,0:T(8,128)(2,1)S(1)}, bf16[24,1280]{1,0:T(8,128)(2,1)S(1)}, u32[]{:S(2)}, u32[]{:S(2)}) %collective-permute-start) | collective-permute-done | bytes 61472 | tf_op jit(solution)/shard_map/sum_heads/ppermute | solution.py:358
  24.9 0.0 copy-start.4
  24.9 1.3 %collective-permute-start.1 = (bf16[24,1280]{1,0:T(8,128)(2,1)S(1)}, bf16[24,1280]{1,0:T(8,128)(2,1)S(1)}, u32[]{:S(2)}, u32[]{:S(2)}) collective-permute-start(bf16[24,1280]{1,0:T(8,128)(2,1)S(1)} %sum_heads.1.left_ref), channel_id=1, source_target_pairs={{0,3},{1,2},{2,1},{3,0},{4,7},{5,6},{6,5},{7,4},{8,11},{9,10},{10,... | collective-permute-start | bytes 184328 | tf_op jit(solution)/shard_map/sum_heads/ppermute | solution.py:358
  26.2 2.7 %collective-permute-done.1.right_ref = bf16[24,1280]{1,0:T(8,128)(2,1)S(1)} collective-permute-done((bf16[24,1280]{1,0:T(8,128)(2,1)S(1)}, bf16[24,1280]{1,0:T(8,128)(2,1)S(1)}, u32[]{:S(2)}, u32[]{:S(2)}) %collective-permute-start.1) | collective-permute-done | bytes 61472 | tf_op jit(solution)/shard_map/sum_heads/ppermute | solution.py:358
  28.9 0.0 copy-done
  28.9 0.0 copy-done.1
  28.9 0.0 copy-done.2
  28.9 0.0 copy-done.3
  28.9 0.0 copy-done.5
  28.9 0.0 copy-done.6
  28.9 1.1 %mlp.1 = (bf16[24,1280]{1,0:T(8,128)(2,1)S(1)}, bf16[24,1280]{1,0:T(8,128)(2,1)S(1)}) custom-call(bf16[24,1280]{1,0:T(8,128)(2,1)S(1)} %sum_heads.1.left_ref, bf16[24,1280]{1,0:T(8,128)(2,1)S(1)} %collective-permute-done.1.right_ref, bf16[24,1280]{1,0:T(8,128)(2,1)S(1)} %copy-done.2, f32[1280]{0:T(1024)S(1)} %copy-done.3, bf16[2,1280,640]{2,1,0:T(8,128)(2,1)S(1)} %copy-done, ...), custom_call_target="tpu_custom_call" | custom-call | flops 100000000 | bytes 5000000 | tf_op jit(solution)/shard_map/mlp/pallas_call | solution.py:330
  30.1 1.3 %collective-permute-start.2 = (bf16[24,1280]{1,0:T(8,128)(2,1)S(1)}, bf16[24,1280]{1,0:T(8,128)(2,1)S(1)}, u32[]{:S(2)}, u32[]{:S(2)}) collective-permute-start(bf16[24,1280]{1,0:T(8,128)(2,1)S(1)} %get-tuple-element.33.left_ref), channel_id=1, source_target_pairs={{0,3},{1,2},{2,1},{3,0},{4,7},{5,6},{6,5},{7,4},{8,11},{9,10},{10,... | collective-permute-start | bytes 184328 | tf_op jit(solution)/shard_map/sum_units/ppermute | solution.py:358
  31.4 2.7 %collective-permute-done.2.right_ref = bf16[24,1280]{1,0:T(8,128)(2,1)S(1)} collective-permute-done((bf16[24,1280]{1,0:T(8,128)(2,1)S(1)}, bf16[24,1280]{1,0:T(8,128)(2,1)S(1)}, u32[]{:S(2)}, u32[]{:S(2)}) %collective-permute-start.2) | collective-permute-done | bytes 61472 | tf_op jit(solution)/shard_map/sum_units/ppermute | solution.py:358
  34.1 0.2 collective-permute-start.3
  34.3 1.1 %collective-permute-done.3.right_ref = bf16[24,1280]{1,0:T(8,128)(2,1)S(1)} collective-permute-done((bf16[24,1280]{1,0:T(8,128)(2,1)S(1)}, bf16[24,1280]{1,0:T(8,128)(2,1)S(1)}, u32[]{:S(2)}, u32[]{:S(2)}) %collective-permute-start.3) | collective-permute-done | bytes 61472 | tf_op jit(solution)/shard_map/sum_units/ppermute | solution.py:358
  35.4 0.0 copy-done.4
  35.4 0.8 %final.1 = bf16[24,1280]{1,0:T(8,128)(2,1)} custom-call(bf16[24,1280]{1,0:T(8,128)(2,1)S(1)} %sum_units.1.left_ref, bf16[24,1280]{1,0:T(8,128)(2,1)S(1)} %collective-permute-done.3.right_ref, bf16[24,1280]{1,0:T(8,128)(2,1)S(1)} %get-tuple-element.34.mid_ref, f32[1280]{0:T(1024)S(1)} %copy-done.4), custom_call_target="tpu_custom_call" | custom-call | flops 1000000 | bytes 100000 | tf_op jit(solution)/shard_map/final/pallas_call | solution.py:330
  (3 shorter events, 0.0 us)
Async XLA Ops:
  1.7 11.4 %all-to-all-start = ((bf16[8,4,1280]{2,1,0:T(4,128)(2,1)}), bf16[8,4,1280]{2,1,0:T(4,128)(2,1)S(1)}, u32[]{:S(2)}, u32[]{:S(2)}) async-start(bf16[8,4,1280]{2,1,0:T(4,128)(2,1)} %get-tuple-element.20), calls=%async_computation | async-start | bytes 163840 | tf_op jit(solution)/shard_map/long_hidden/all_to_all | solution.py:407
  12.5 10.6 %copy-start.7 = (bf16[320,1280]{1,0:T(8,128)(2,1)S(1)}, bf16[320,1280]{1,0:T(8,128)(2,1)}, u32[]{:S(2)}) copy-start(bf16[320,1280]{1,0:T(8,128)(2,1)} %w_ref.1) | copy-start | bytes 2457604
  23.1 5.8 %copy-start = (bf16[2,1280,640]{2,1,0:T(8,128)(2,1)S(1)}, bf16[2,1280,640]{2,1,0:T(8,128)(2,1)}, u32[]{:S(2)}) copy-start(bf16[2,1280,640]{2,1,0:T(8,128)(2,1)} %w_gate_up_ref.1) | copy-start | bytes 9830404
  23.1 5.8 %copy-start.1 = (bf16[640,1280]{1,0:T(8,128)(2,1)S(1)}, bf16[640,1280]{1,0:T(8,128)(2,1)}, u32[]{:S(2)}) copy-start(bf16[640,1280]{1,0:T(8,128)(2,1)} %w_down_ref.1) | copy-start | bytes 4915204
  23.1 5.8 %copy-start.2 = (bf16[24,1280]{1,0:T(8,128)(2,1)S(1)}, bf16[24,1280]{1,0:T(8,128)(2,1)}, u32[]{:S(2)}) copy-start(bf16[24,1280]{1,0:T(8,128)(2,1)} %hidden_ref.1) | copy-start | bytes 184324
  23.1 5.8 %copy-start.3 = (f32[1280]{0:T(1024)S(1)}, f32[1280]{0:T(1024)}, u32[]{:S(2)}) copy-start(f32[1280]{0:T(1024)} %alpha_ref.2) | copy-start | bytes 15364
  23.1 5.8 %copy-start.5 = (f32[640]{0:T(1024)S(1)}, f32[640]{0:T(1024)}, u32[]{:S(2)}) copy-start(f32[640]{0:T(1024)} %s_gate_ref.1) | copy-start | bytes 7684
  23.1 5.8 %copy-start.6 = (f32[640]{0:T(1024)S(1)}, f32[640]{0:T(1024)}, u32[]{:S(2)}) copy-start(f32[640]{0:T(1024)} %s_up_ref.1) | copy-start | bytes 7684
  23.5 1.3 %collective-permute-start = (bf16[24,1280]{1,0:T(8,128)(2,1)S(1)}, bf16[24,1280]{1,0:T(8,128)(2,1)S(1)}, u32[]{:S(2)}, u32[]{:S(2)}) collective-permute-start(bf16[24,1280]{1,0:T(8,128)(2,1)S(1)} %project.1.left_ref), channel_id=1, source_target_pairs={{0,1},{1,0},{2,3},{3,2},{4,5},{5,4},{6,7},{7,6},{8,9},{9,8},{10,11... | collective-permute-start | bytes 184328 | tf_op jit(solution)/shard_map/sum_heads/ppermute | solution.py:358
  24.9 10.5 %copy-start.4 = (f32[1280]{0:T(1024)S(1)}, f32[1280]{0:T(1024)}, u32[]{:S(2)}) copy-start(f32[1280]{0:T(1024)} %alpha_ref.3) | copy-start | bytes 15364
  24.9 4.0 %collective-permute-start.1 = (bf16[24,1280]{1,0:T(8,128)(2,1)S(1)}, bf16[24,1280]{1,0:T(8,128)(2,1)S(1)}, u32[]{:S(2)}, u32[]{:S(2)}) collective-permute-start(bf16[24,1280]{1,0:T(8,128)(2,1)S(1)} %sum_heads.1.left_ref), channel_id=1, source_target_pairs={{0,3},{1,2},{2,1},{3,0},{4,7},{5,6},{6,5},{7,4},{8,11},{9,10},{10,... | collective-permute-start | bytes 184328 | tf_op jit(solution)/shard_map/sum_heads/ppermute | solution.py:358
  30.1 4.0 %collective-permute-start.2 = (bf16[24,1280]{1,0:T(8,128)(2,1)S(1)}, bf16[24,1280]{1,0:T(8,128)(2,1)S(1)}, u32[]{:S(2)}, u32[]{:S(2)}) collective-permute-start(bf16[24,1280]{1,0:T(8,128)(2,1)S(1)} %get-tuple-element.33.left_ref), channel_id=1, source_target_pairs={{0,3},{1,2},{2,1},{3,0},{4,7},{5,6},{6,5},{7,4},{8,11},{9,10},{10,... | collective-permute-start | bytes 184328 | tf_op jit(solution)/shard_map/sum_units/ppermute | solution.py:358
  34.1 1.3 %collective-permute-start.3 = (bf16[24,1280]{1,0:T(8,128)(2,1)S(1)}, bf16[24,1280]{1,0:T(8,128)(2,1)S(1)}, u32[]{:S(2)}, u32[]{:S(2)}) collective-permute-start(bf16[24,1280]{1,0:T(8,128)(2,1)S(1)} %sum_units.1.left_ref), channel_id=1, source_target_pairs={{0,1},{1,0},{2,3},{3,2},{4,5},{5,4},{6,7},{7,6},{8,9},{9,8},{10,11... | collective-permute-start | bytes 184328 | tf_op jit(solution)/shard_map/sum_units/ppermute | solution.py:358

commit v7 on v6

--- a/solution.py
+++ b/solution.py
@@ -233,9 +233,9 @@
     padded = sent_ref.shape[2]
     sub = lax.broadcasted_iota(jnp.int32, (LANES, padded), 0)
     lane = lax.broadcasted_iota(jnp.int32, (LANES, padded), 1)
-    kept = ((lane >= sub * HEAD_DIM) & (lane < (sub + 1) * HEAD_DIM) & (lane < width)) | (
-        lane == width + sub
-    )
+    heads = width // HEAD_DIM
+    own_columns = (lane >= sub * HEAD_DIM) & (lane < (sub + 1) * HEAD_DIM) & (lane < width)
+    slots = [(sub < heads) & (lane == width + k * heads + sub) for k in range(3)]
     outs = []
     for i in range(longs):
         top = jnp.max(scores[i], axis=-1, keepdims=True)
@@ -243,9 +243,14 @@
         total = jnp.sum(weights, axis=-1, keepdims=True)
         summed = dot_t(weights.astype(BF16), values_ref[i]) / total
         summed = jnp.concatenate([summed, jnp.zeros((LANES, padded - width), F32)], axis=1)
-        row = jnp.where(lane < width, summed, top + jnp.log(total))
-        outs.append(jnp.sum(jnp.where(kept, row, 0.0), axis=0, keepdims=True))
-    packed = jnp.concatenate(outs, axis=0)
+        row = jnp.where(own_columns, summed, 0.0)
+        left = top + jnp.log(total)
+        for slot in slots:
+            term = left.astype(BF16).astype(F32)
+            row = jnp.where(slot, term, row)
+            left = left - term
+        outs.append(jnp.sum(row, axis=0, keepdims=True))
+    packed = jnp.concatenate(outs, axis=0).astype(BF16)
     for party in range(parties):
         sent_ref[party] = packed
 
@@ -265,7 +270,14 @@
             result = jnp.where(mask, compact[:, first + h : first + h + 1], result)
         return result
 
-    lses = [parts_ref[party][:, last:] for party in range(parties)]
+    heads = len(masks)
+    parts = [parts_ref[party].astype(F32) for party in range(parties)]
+    lses = []
+    for part in parts:
+        terms = part[:, last:]
+        lses.append(
+            terms + pltpu.roll(terms, 128 - heads, 1) + pltpu.roll(terms, 128 - 2 * heads, 1)
+        )
     top = lses[0]
     for lse in lses[1:]:
         top = jnp.maximum(top, lse)
@@ -275,7 +287,7 @@
         total = total + weight
     long_out = jnp.zeros((longs, width), F32)
     for party in range(parties):
-        long_out = long_out + on_heads(weights[party] / total) * parts_ref[party][:, :width]
+        long_out = long_out + on_heads(weights[party] / total) * parts[party][:, :width]
     long_lse = on_heads(top + jnp.log(total))
     cached = short_ref[...]
     lse = short_lse_ref[...]
@@ -425,7 +437,7 @@
     with jax.named_scope("long_attention"):
         (partial,) = call(
             long_kernel,
-            (shape((parties, longs, (width // 128 + 1) * 128), F32),),
+            (shape((parties, longs, (width // 128 + 1) * 128), BF16),),
             (10**9, 4 * 10**6),
             near=(received, gains, w_query, keys, values),
         )

time: 36.5 us -> 36.5 us (level)
  no operation moved by 1% of the time
where the time goes in v7:
time: 36.5 us; the launch traced here: 36.2 us
  starting transfers between devices  10.3 us (28%)
  blocking collectives  8.86 us (24%)
  Pallas kernels  8.66 us (24%)
  waiting for transfers between devices  8.27 us (23%)
    all_to_all x1, blocking collectives, on_device(): lax.all_to_all(partial, 'req', 0, 0, axis_index_groups=[centre_first(part...  8.86 us
    pallas_call x8, Pallas kernels, call(): pl.pallas_call(kernel, in_specs=[HBM] * len(far) + [VMEM] * len(near), ou...  8.66 us
    ppermute x4, waiting for transfers between devices, exchanged(): return lax.ppermute(value, 'head', [(i, i ^ step) for i in range(places)])  7.67 us
    all_to_all x1, starting transfers between devices, on_device(): lax.all_to_all(sent, ('req', 'head'), 0, 0, axis_index_groups=mixed_group...  7.31 us
    ppermute x4, starting transfers between devices, exchanged(): return lax.ppermute(value, 'head', [(i, i ^ step) for i in range(places)])  2.96 us
  transfers between devices with their start and end apart: 5, of which 5 were waited for; matrix products, arithmetic and copies ran while one was open for 0% of the time, Pallas kernels for 10%

profile of v7, /device:TPU:0, one launch (start us, length us, event | category | flops | bytes accessed | tf_op | source)
XLA Modules:
  0.0 36.2 jit_solution(6313747908360584059)
XLA Ops:
  0.0 1.7 %long_hidden.1 = (bf16[8,4,1280]{2,1,0:T(4,128)(2,1)}, bf16[24,1280]{1,0:T(8,128)(2,1)S(1)}, f32[24,128]{1,0:T(8,128)S(1)}, f32[24,320]{1,0:T(8,128)S(1)}, f32[3...) custom-call(s32[4]{0:T(128)} %longs_hbm.1, ...), custom_call_target="tpu_custom_call" | custom-call | flops 1000000 | bytes 3000000 | tf_op jit(solution)/shard_map/long_hidden/pallas_call | solution.py:342
  1.7 7.3 %all-to-all-start = ((bf16[8,4,1280]{2,1,0:T(4,128)(2,1)}), bf16[8,4,1280]{2,1,0:T(4,128)(2,1)S(1)}, u32[]{:S(2)}, u32[]{:S(2)}) async-start(bf16[8,4,1280]{2,1,0:T(4,128)(2,1)} %get-tuple-element.20), calls=%async_computation | async-start | bytes 163840 | tf_op jit(solution)/shard_map/long_hidden/all_to_all | solution.py:419
  9.0 3.5 %short_attention.1 = (f32[24,320]{1,0:T(8,128)S(1)}, f32[24,320]{1,0:T(8,128)S(1)}, f32[24,320]{1,0:T(8,128)S(1)}, f32[24,320]{1,0:T(8,128)S(1)}, bf16[4,320,256]{2,1,0:T(8,128)(2,1)S(1)}) custom-call(s32[24]{0:T(128)} %lengths_hbm.1, bf16[3,320,1280]{2,1,0:T(8,128)(2,1)} %bitcast.6, bf16[24,320,128]{2,1,0:T(8,128)(2,1)} %bitcast.7, ...), custom_call_target="tpu_custom_call" | custom-call | flops 1000000000 | bytes 6000000 | tf_op jit(solution)/shard_map/short_attention/pallas_call | solution.py:342
  12.5 0.0 copy-start.7
  12.5 0.6 %all-to-all-done.received_ref = bf16[8,4,1280]{2,1,0:T(4,128)(2,1)S(1)} async-done(((bf16[8,4,1280]{2,1,0:T(4,128)(2,1)}), bf16[8,4,1280]{2,1,0:T(4,128)(2,1)S(1)}, u32[]{:S(2)}, u32[]{:S(2)}) %all-to-all-start) | async-done | bytes 81952 | tf_op jit(solution)/shard_map/long_hidden/all_to_all | solution.py:419
  13.1 1.0 %long_attention.1 = bf16[8,4,384]{2,1,0:T(4,128)(2,1)S(1)} custom-call(bf16[8,4,1280]{2,1,0:T(4,128)(2,1)S(1)} %all-to-all-done.received_ref, f32[320]{0:T(512)S(1)} %get-tuple-element.21.gains_ref, bf16[320,1280]{1,0:T(8,128)(2,1)S(1)} %get-tuple-element.22.w_ref, bf16[4,320,256]{2,1,0:T(8,128)(2,1)S(1)} %get-tuple-element.23.keys_ref, ...), custom_call_target="tpu_custom_call" | custom-call | flops 1000000000 | bytes 4000000 | tf_op jit(solution)/shard_map/long_attention/pallas_call | solution.py:342
  14.1 8.9 %all_to_all.10.parts_ref = bf16[8,4,384]{2,1,0:T(4,128)(2,1)S(1)} all-to-all(bf16[8,4,384]{2,1,0:T(4,128)(2,1)S(1)} %long_attention.1), channel_id=1, replica_groups={{16,0,4,8,12,20,24,28},{17,1,5,9,13,21,25,29},{18,2,6,10,14,22,26,30},{..., dimensions={0} | all-to-all | bytes 49152 | tf_op jit(solution)/shard_map/long_parts/all_to_all | solution.py:445
  23.0 0.0 copy-done.7
  23.0 0.0 copy-start
  23.0 0.0 copy-start.1
  23.0 0.0 copy-start.3
  23.0 0.0 copy-start.5
  23.0 0.0 copy-start.6
  23.0 0.5 %project.1.left_ref = bf16[24,1280]{1,0:T(8,128)(2,1)S(1)} custom-call(bf16[8,4,384]{2,1,0:T(4,128)(2,1)S(1)} %all_to_all.10.parts_ref, f32[24,320]{1,0:T(8,128)S(1)} %get-tuple-element.28.short_ref, f32[24,320]{1,0:T(8,128)S(1)} %get-tuple-element.29.short_lse_ref, f32[24,320]{1,0:T(8,128)S(1)} %get-tuple-element.30.value_ref, ...), custom_call_target="tpu_custom_call" | custom-call | flops 20000000000 | bytes 1000000 | tf_op jit(solution)/shard_map/project/pallas_call | solution.py:342
  23.5 0.1 collective-permute-start
  23.6 1.2 %collective-permute-done.right_ref = bf16[24,1280]{1,0:T(8,128)(2,1)S(1)} collective-permute-done((bf16[24,1280]{1,0:T(8,128)(2,1)S(1)}, bf16[24,1280]{1,0:T(8,128)(2,1)S(1)}, u32[]{:S(2)}, u32[]{:S(2)}) %collective-permute-start) | collective-permute-done | bytes 61472 | tf_op jit(solution)/shard_map/sum_heads/ppermute | solution.py:370
  24.8 0.0 copy-start.4
  24.9 1.3 %collective-permute-start.1 = (bf16[24,1280]{1,0:T(8,128)(2,1)S(1)}, bf16[24,1280]{1,0:T(8,128)(2,1)S(1)}, u32[]{:S(2)}, u32[]{:S(2)}) collective-permute-start(bf16[24,1280]{1,0:T(8,128)(2,1)S(1)} %sum_heads.1.left_ref), channel_id=1, source_target_pairs={{0,3},{1,2},{2,1},{3,0},{4,7},{5,6},{6,5},{7,4},{8,11},{9,10},{10,... | collective-permute-start | bytes 184328 | tf_op jit(solution)/shard_map/sum_heads/ppermute | solution.py:370
  26.2 2.7 %collective-permute-done.1.right_ref = bf16[24,1280]{1,0:T(8,128)(2,1)S(1)} collective-permute-done((bf16[24,1280]{1,0:T(8,128)(2,1)S(1)}, bf16[24,1280]{1,0:T(8,128)(2,1)S(1)}, u32[]{:S(2)}, u32[]{:S(2)}) %collective-permute-start.1) | collective-permute-done | bytes 61472 | tf_op jit(solution)/shard_map/sum_heads/ppermute | solution.py:370
  28.9 0.0 copy-done
  28.9 0.0 copy-done.1
  28.9 0.0 copy-done.2
  28.9 0.0 copy-done.3
  28.9 0.0 copy-done.5
  28.9 0.0 copy-done.6
  28.9 1.1 %mlp.1 = (bf16[24,1280]{1,0:T(8,128)(2,1)S(1)}, bf16[24,1280]{1,0:T(8,128)(2,1)S(1)}) custom-call(bf16[24,1280]{1,0:T(8,128)(2,1)S(1)} %sum_heads.1.left_ref, bf16[24,1280]{1,0:T(8,128)(2,1)S(1)} %collective-permute-done.1.right_ref, bf16[24,1280]{1,0:T(8,128)(2,1)S(1)} %copy-done.2, f32[1280]{0:T(1024)S(1)} %copy-done.3, bf16[2,1280,640]{2,1,0:T(8,128)(2,1)S(1)} %copy-done, ...), custom_call_target="tpu_custom_call" | custom-call | flops 100000000 | bytes 5000000 | tf_op jit(solution)/shard_map/mlp/pallas_call | solution.py:342
  30.1 1.3 %collective-permute-start.2 = (bf16[24,1280]{1,0:T(8,128)(2,1)S(1)}, bf16[24,1280]{1,0:T(8,128)(2,1)S(1)}, u32[]{:S(2)}, u32[]{:S(2)}) collective-permute-start(bf16[24,1280]{1,0:T(8,128)(2,1)S(1)} %get-tuple-element.33.left_ref), channel_id=1, source_target_pairs={{0,3},{1,2},{2,1},{3,0},{4,7},{5,6},{6,5},{7,4},{8,11},{9,10},{10,... | collective-permute-start | bytes 184328 | tf_op jit(solution)/shard_map/sum_units/ppermute | solution.py:370
  31.4 2.7 %collective-permute-done.2.right_ref = bf16[24,1280]{1,0:T(8,128)(2,1)S(1)} collective-permute-done((bf16[24,1280]{1,0:T(8,128)(2,1)S(1)}, bf16[24,1280]{1,0:T(8,128)(2,1)S(1)}, u32[]{:S(2)}, u32[]{:S(2)}) %collective-permute-start.2) | collective-permute-done | bytes 61472 | tf_op jit(solution)/shard_map/sum_units/ppermute | solution.py:370
  34.1 0.2 collective-permute-start.3
  34.3 1.1 %collective-permute-done.3.right_ref = bf16[24,1280]{1,0:T(8,128)(2,1)S(1)} collective-permute-done((bf16[24,1280]{1,0:T(8,128)(2,1)S(1)}, bf16[24,1280]{1,0:T(8,128)(2,1)S(1)}, u32[]{:S(2)}, u32[]{:S(2)}) %collective-permute-start.3) | collective-permute-done | bytes 61472 | tf_op jit(solution)/shard_map/sum_units/ppermute | solution.py:370
  35.4 0.0 copy-done.4
  35.4 0.8 %final.1 = bf16[24,1280]{1,0:T(8,128)(2,1)} custom-call(bf16[24,1280]{1,0:T(8,128)(2,1)S(1)} %sum_units.1.left_ref, bf16[24,1280]{1,0:T(8,128)(2,1)S(1)} %collective-permute-done.3.right_ref, bf16[24,1280]{1,0:T(8,128)(2,1)S(1)} %get-tuple-element.34.mid_ref, f32[1280]{0:T(1024)S(1)} %copy-done.4), custom_call_target="tpu_custom_call" | custom-call | flops 1000000 | bytes 100000 | tf_op jit(solution)/shard_map/final/pallas_call | solution.py:342
  (3 shorter events, 0.0 us)
Async XLA Ops:
  1.7 11.4 %all-to-all-start = ((bf16[8,4,1280]{2,1,0:T(4,128)(2,1)}), bf16[8,4,1280]{2,1,0:T(4,128)(2,1)S(1)}, u32[]{:S(2)}, u32[]{:S(2)}) async-start(bf16[8,4,1280]{2,1,0:T(4,128)(2,1)} %get-tuple-element.20), calls=%async_computation | async-start | bytes 163840 | tf_op jit(solution)/shard_map/long_hidden/all_to_all | solution.py:419
  12.5 10.5 %copy-start.7 = (bf16[320,1280]{1,0:T(8,128)(2,1)S(1)}, bf16[320,1280]{1,0:T(8,128)(2,1)}, u32[]{:S(2)}) copy-start(bf16[320,1280]{1,0:T(8,128)(2,1)} %w_ref.1) | copy-start | bytes 2457604
  23.0 5.9 %copy-start = (bf16[2,1280,640]{2,1,0:T(8,128)(2,1)S(1)}, bf16[2,1280,640]{2,1,0:T(8,128)(2,1)}, u32[]{:S(2)}) copy-start(bf16[2,1280,640]{2,1,0:T(8,128)(2,1)} %w_gate_up_ref.1) | copy-start | bytes 9830404
  23.0 5.9 %copy-start.1 = (bf16[640,1280]{1,0:T(8,128)(2,1)S(1)}, bf16[640,1280]{1,0:T(8,128)(2,1)}, u32[]{:S(2)}) copy-start(bf16[640,1280]{1,0:T(8,128)(2,1)} %w_down_ref.1) | copy-start | bytes 4915204
  23.0 5.9 %copy-start.2 = (bf16[24,1280]{1,0:T(8,128)(2,1)S(1)}, bf16[24,1280]{1,0:T(8,128)(2,1)}, u32[]{:S(2)}) copy-start(bf16[24,1280]{1,0:T(8,128)(2,1)} %hidden_ref.1) | copy-start | bytes 184324
  23.0 5.9 %copy-start.3 = (f32[1280]{0:T(1024)S(1)}, f32[1280]{0:T(1024)}, u32[]{:S(2)}) copy-start(f32[1280]{0:T(1024)} %alpha_ref.2) | copy-start | bytes 15364
  23.0 5.9 %copy-start.5 = (f32[640]{0:T(1024)S(1)}, f32[640]{0:T(1024)}, u32[]{:S(2)}) copy-start(f32[640]{0:T(1024)} %s_gate_ref.1) | copy-start | bytes 7684
  23.0 5.9 %copy-start.6 = (f32[640]{0:T(1024)S(1)}, f32[640]{0:T(1024)}, u32[]{:S(2)}) copy-start(f32[640]{0:T(1024)} %s_up_ref.1) | copy-start | bytes 7684
  23.5 1.3 %collective-permute-start = (bf16[24,1280]{1,0:T(8,128)(2,1)S(1)}, bf16[24,1280]{1,0:T(8,128)(2,1)S(1)}, u32[]{:S(2)}, u32[]{:S(2)}) collective-permute-start(bf16[24,1280]{1,0:T(8,128)(2,1)S(1)} %project.1.left_ref), channel_id=1, source_target_pairs={{0,1},{1,0},{2,3},{3,2},{4,5},{5,4},{6,7},{7,6},{8,9},{9,8},{10,11... | collective-permute-start | bytes 184328 | tf_op jit(solution)/shard_map/sum_heads/ppermute | solution.py:370
  24.8 10.5 %copy-start.4 = (f32[1280]{0:T(1024)S(1)}, f32[1280]{0:T(1024)}, u32[]{:S(2)}) copy-start(f32[1280]{0:T(1024)} %alpha_ref.3) | copy-start | bytes 15364
  24.9 4.0 %collective-permute-start.1 = (bf16[24,1280]{1,0:T(8,128)(2,1)S(1)}, bf16[24,1280]{1,0:T(8,128)(2,1)S(1)}, u32[]{:S(2)}, u32[]{:S(2)}) collective-permute-start(bf16[24,1280]{1,0:T(8,128)(2,1)S(1)} %sum_heads.1.left_ref), channel_id=1, source_target_pairs={{0,3},{1,2},{2,1},{3,0},{4,7},{5,6},{6,5},{7,4},{8,11},{9,10},{10,... | collective-permute-start | bytes 184328 | tf_op jit(solution)/shard_map/sum_heads/ppermute | solution.py:370
  30.1 4.0 %collective-permute-start.2 = (bf16[24,1280]{1,0:T(8,128)(2,1)S(1)}, bf16[24,1280]{1,0:T(8,128)(2,1)S(1)}, u32[]{:S(2)}, u32[]{:S(2)}) collective-permute-start(bf16[24,1280]{1,0:T(8,128)(2,1)S(1)} %get-tuple-element.33.left_ref), channel_id=1, source_target_pairs={{0,3},{1,2},{2,1},{3,0},{4,7},{5,6},{6,5},{7,4},{8,11},{9,10},{10,... | collective-permute-start | bytes 184328 | tf_op jit(solution)/shard_map/sum_units/ppermute | solution.py:370
  34.1 1.3 %collective-permute-start.3 = (bf16[24,1280]{1,0:T(8,128)(2,1)S(1)}, bf16[24,1280]{1,0:T(8,128)(2,1)S(1)}, u32[]{:S(2)}, u32[]{:S(2)}) collective-permute-start(bf16[24,1280]{1,0:T(8,128)(2,1)S(1)} %sum_units.1.left_ref), channel_id=1, source_target_pairs={{0,1},{1,0},{2,3},{3,2},{4,5},{5,4},{6,7},{7,6},{8,9},{9,8},{10,11... | collective-permute-start | bytes 184328 | tf_op jit(solution)/shard_map/sum_units/ppermute | solution.py:370

commit v8 on v6

--- a/solution.py
+++ b/solution.py
@@ -343,7 +343,8 @@
 
 
 def centre_first(parties):
-    return sorted(range(parties), key=lambda r: (r != parties // 2, r))
+    middle = parties // 2
+    return sorted(range(parties), key=lambda r: (r != middle, -abs(r // 2 - middle // 2), r))
 
 
 def mixed_groups(parties):

time: 36.5 us -> 36.4 us (level)
  no operation moved by 1% of the time
where the time goes in v8:
time: 36.4 us; the launch traced here: 36.1 us
  starting transfers between devices  10.3 us (28%)
  blocking collectives  9.13 us (25%)
  Pallas kernels  8.58 us (24%)
  waiting for transfers between devices  7.98 us (22%)
    all_to_all x1, blocking collectives, on_device(): lax.all_to_all(partial, 'req', 0, 0, axis_index_groups=[centre_first(part...  9.13 us
    pallas_call x8, Pallas kernels, call(): pl.pallas_call(kernel, in_specs=[HBM] * len(far) + [VMEM] * len(near), ou...  8.58 us
    ppermute x4, waiting for transfers between devices, exchanged(): return lax.ppermute(value, 'head', [(i, i ^ step) for i in range(places)])  7.69 us
    all_to_all x1, starting transfers between devices, on_device(): lax.all_to_all(sent, ('req', 'head'), 0, 0, axis_index_groups=mixed_group...  7.31 us
    ppermute x4, starting transfers between devices, exchanged(): return lax.ppermute(value, 'head', [(i, i ^ step) for i in range(places)])  2.96 us
  transfers between devices with their start and end apart: 5, of which 5 were waited for; matrix products, arithmetic and copies ran while one was open for 0% of the time, Pallas kernels for 10%

profile of v8, /device:TPU:0, one launch (start us, length us, event | category | flops | bytes accessed | tf_op | source)
XLA Modules:
  0.0 36.1 jit_solution(1893324475372714788)
XLA Ops:
  0.0 1.7 %long_hidden.1 = (bf16[8,4,1280]{2,1,0:T(4,128)(2,1)}, bf16[24,1280]{1,0:T(8,128)(2,1)S(1)}, f32[24,128]{1,0:T(8,128)S(1)}, f32[24,320]{1,0:T(8,128)S(1)}, f32[3...) custom-call(s32[4]{0:T(128)} %longs_hbm.1, ...), custom_call_target="tpu_custom_call" | custom-call | flops 1000000 | bytes 3000000 | tf_op jit(solution)/shard_map/long_hidden/pallas_call | solution.py:330
  1.7 7.3 %all-to-all-start = ((bf16[8,4,1280]{2,1,0:T(4,128)(2,1)}), bf16[8,4,1280]{2,1,0:T(4,128)(2,1)S(1)}, u32[]{:S(2)}, u32[]{:S(2)}) async-start(bf16[8,4,1280]{2,1,0:T(4,128)(2,1)} %get-tuple-element.20), calls=%async_computation | async-start | bytes 163840 | tf_op jit(solution)/shard_map/long_hidden/all_to_all | solution.py:408
  9.0 3.5 %short_attention.1 = (f32[24,320]{1,0:T(8,128)S(1)}, f32[24,320]{1,0:T(8,128)S(1)}, f32[24,320]{1,0:T(8,128)S(1)}, f32[24,320]{1,0:T(8,128)S(1)}, bf16[4,320,256]{2,1,0:T(8,128)(2,1)S(1)}) custom-call(s32[24]{0:T(128)} %lengths_hbm.1, bf16[3,320,1280]{2,1,0:T(8,128)(2,1)} %bitcast.6, bf16[24,320,128]{2,1,0:T(8,128)(2,1)} %bitcast.7, ...), custom_call_target="tpu_custom_call" | custom-call | flops 1000000000 | bytes 6000000 | tf_op jit(solution)/shard_map/short_attention/pallas_call | solution.py:330
  12.5 0.0 copy-start.7
  12.5 0.3 all-to-all-done.received_ref
  12.8 1.0 %long_attention.1 = f32[8,4,384]{2,1,0:T(4,128)S(1)} custom-call(bf16[8,4,1280]{2,1,0:T(4,128)(2,1)S(1)} %all-to-all-done.received_ref, f32[320]{0:T(512)S(1)} %get-tuple-element.21.gains_ref, bf16[320,1280]{1,0:T(8,128)(2,1)S(1)} %get-tuple-element.22.w_ref, bf16[4,320,256]{2,1,0:T(8,128)(2,1)S(1)} %get-tuple-element.23.keys_ref, ...), custom_call_target="tpu_custom_call" | custom-call | flops 1000000000 | bytes 4000000 | tf_op jit(solution)/shard_map/long_attention/pallas_call | solution.py:330
  13.8 9.1 %all_to_all.10.parts_ref = f32[8,4,384]{2,1,0:T(4,128)S(1)} all-to-all(f32[8,4,384]{2,1,0:T(4,128)S(1)} %long_attention.1), channel_id=1, replica_groups={{16,0,4,8,12,24,28,20},{17,1,5,9,13,25,29,21},{18,2,6,10,14,26,30,22},{..., dimensions={0} | all-to-all | bytes 98304 | tf_op jit(solution)/shard_map/long_parts/all_to_all | solution.py:434
  23.0 0.0 copy-done.7
  23.0 0.0 copy-start
  23.0 0.0 copy-start.1
  23.0 0.0 copy-start.3
  23.0 0.0 copy-start.5
  23.0 0.0 copy-start.6
  23.0 0.4 %project.1.left_ref = bf16[24,1280]{1,0:T(8,128)(2,1)S(1)} custom-call(f32[8,4,384]{2,1,0:T(4,128)S(1)} %all_to_all.10.parts_ref, f32[24,320]{1,0:T(8,128)S(1)} %get-tuple-element.28.short_ref, f32[24,320]{1,0:T(8,128)S(1)} %get-tuple-element.29.short_lse_ref, f32[24,320]{1,0:T(8,128)S(1)} %get-tuple-element.30.value_ref, ...), custom_call_target="tpu_custom_call" | custom-call | flops 20000000000 | bytes 1000000 | tf_op jit(solution)/shard_map/project/pallas_call | solution.py:330
  23.4 0.1 collective-permute-start
  23.5 1.2 %collective-permute-done.right_ref = bf16[24,1280]{1,0:T(8,128)(2,1)S(1)} collective-permute-done((bf16[24,1280]{1,0:T(8,128)(2,1)S(1)}, bf16[24,1280]{1,0:T(8,128)(2,1)S(1)}, u32[]{:S(2)}, u32[]{:S(2)}) %collective-permute-start) | collective-permute-done | bytes 61472 | tf_op jit(solution)/shard_map/sum_heads/ppermute | solution.py:359
  24.7 0.0 copy-start.4
  24.7 1.3 %collective-permute-start.1 = (bf16[24,1280]{1,0:T(8,128)(2,1)S(1)}, bf16[24,1280]{1,0:T(8,128)(2,1)S(1)}, u32[]{:S(2)}, u32[]{:S(2)}) collective-permute-start(bf16[24,1280]{1,0:T(8,128)(2,1)S(1)} %sum_heads.1.left_ref), channel_id=1, source_target_pairs={{0,3},{1,2},{2,1},{3,0},{4,7},{5,6},{6,5},{7,4},{8,11},{9,10},{10,... | collective-permute-start | bytes 184328 | tf_op jit(solution)/shard_map/sum_heads/ppermute | solution.py:359
  26.1 2.7 %collective-permute-done.1.right_ref = bf16[24,1280]{1,0:T(8,128)(2,1)S(1)} collective-permute-done((bf16[24,1280]{1,0:T(8,128)(2,1)S(1)}, bf16[24,1280]{1,0:T(8,128)(2,1)S(1)}, u32[]{:S(2)}, u32[]{:S(2)}) %collective-permute-start.1) | collective-permute-done | bytes 61472 | tf_op jit(solution)/shard_map/sum_heads/ppermute | solution.py:359
  28.8 0.0 copy-done
  28.8 0.0 copy-done.1
  28.8 0.0 copy-done.2
  28.8 0.0 copy-done.3
  28.8 0.0 copy-done.5
  28.8 0.0 copy-done.6
  28.8 1.1 %mlp.1 = (bf16[24,1280]{1,0:T(8,128)(2,1)S(1)}, bf16[24,1280]{1,0:T(8,128)(2,1)S(1)}) custom-call(bf16[24,1280]{1,0:T(8,128)(2,1)S(1)} %sum_heads.1.left_ref, bf16[24,1280]{1,0:T(8,128)(2,1)S(1)} %collective-permute-done.1.right_ref, bf16[24,1280]{1,0:T(8,128)(2,1)S(1)} %copy-done.2, f32[1280]{0:T(1024)S(1)} %copy-done.3, bf16[2,1280,640]{2,1,0:T(8,128)(2,1)S(1)} %copy-done, ...), custom_call_target="tpu_custom_call" | custom-call | flops 100000000 | bytes 5000000 | tf_op jit(solution)/shard_map/mlp/pallas_call | solution.py:330
  29.9 1.3 %collective-permute-start.2 = (bf16[24,1280]{1,0:T(8,128)(2,1)S(1)}, bf16[24,1280]{1,0:T(8,128)(2,1)S(1)}, u32[]{:S(2)}, u32[]{:S(2)}) collective-permute-start(bf16[24,1280]{1,0:T(8,128)(2,1)S(1)} %get-tuple-element.33.left_ref), channel_id=1, source_target_pairs={{0,3},{1,2},{2,1},{3,0},{4,7},{5,6},{6,5},{7,4},{8,11},{9,10},{10,... | collective-permute-start | bytes 184328 | tf_op jit(solution)/shard_map/sum_units/ppermute | solution.py:359
  31.2 2.7 %collective-permute-done.2.right_ref = bf16[24,1280]{1,0:T(8,128)(2,1)S(1)} collective-permute-done((bf16[24,1280]{1,0:T(8,128)(2,1)S(1)}, bf16[24,1280]{1,0:T(8,128)(2,1)S(1)}, u32[]{:S(2)}, u32[]{:S(2)}) %collective-permute-start.2) | collective-permute-done | bytes 61472 | tf_op jit(solution)/shard_map/sum_units/ppermute | solution.py:359
  33.9 0.2 collective-permute-start.3
  34.2 1.1 %collective-permute-done.3.right_ref = bf16[24,1280]{1,0:T(8,128)(2,1)S(1)} collective-permute-done((bf16[24,1280]{1,0:T(8,128)(2,1)S(1)}, bf16[24,1280]{1,0:T(8,128)(2,1)S(1)}, u32[]{:S(2)}, u32[]{:S(2)}) %collective-permute-start.3) | collective-permute-done | bytes 61472 | tf_op jit(solution)/shard_map/sum_units/ppermute | solution.py:359
  35.3 0.0 copy-done.4
  35.3 0.8 %final.1 = bf16[24,1280]{1,0:T(8,128)(2,1)} custom-call(bf16[24,1280]{1,0:T(8,128)(2,1)S(1)} %sum_units.1.left_ref, bf16[24,1280]{1,0:T(8,128)(2,1)S(1)} %collective-permute-done.3.right_ref, bf16[24,1280]{1,0:T(8,128)(2,1)S(1)} %get-tuple-element.34.mid_ref, f32[1280]{0:T(1024)S(1)} %copy-done.4), custom_call_target="tpu_custom_call" | custom-call | flops 1000000 | bytes 100000 | tf_op jit(solution)/shard_map/final/pallas_call | solution.py:330
  (3 shorter events, 0.0 us)
Async XLA Ops:
  1.7 11.1 %all-to-all-start = ((bf16[8,4,1280]{2,1,0:T(4,128)(2,1)}), bf16[8,4,1280]{2,1,0:T(4,128)(2,1)S(1)}, u32[]{:S(2)}, u32[]{:S(2)}) async-start(bf16[8,4,1280]{2,1,0:T(4,128)(2,1)} %get-tuple-element.20), calls=%async_computation | async-start | bytes 163840 | tf_op jit(solution)/shard_map/long_hidden/all_to_all | solution.py:408
  12.5 10.5 %copy-start.7 = (bf16[320,1280]{1,0:T(8,128)(2,1)S(1)}, bf16[320,1280]{1,0:T(8,128)(2,1)}, u32[]{:S(2)}) copy-start(bf16[320,1280]{1,0:T(8,128)(2,1)} %w_ref.1) | copy-start | bytes 2457604
  23.0 5.8 %copy-start = (bf16[2,1280,640]{2,1,0:T(8,128)(2,1)S(1)}, bf16[2,1280,640]{2,1,0:T(8,128)(2,1)}, u32[]{:S(2)}) copy-start(bf16[2,1280,640]{2,1,0:T(8,128)(2,1)} %w_gate_up_ref.1) | copy-start | bytes 9830404
  23.0 5.8 %copy-start.1 = (bf16[640,1280]{1,0:T(8,128)(2,1)S(1)}, bf16[640,1280]{1,0:T(8,128)(2,1)}, u32[]{:S(2)}) copy-start(bf16[640,1280]{1,0:T(8,128)(2,1)} %w_down_ref.1) | copy-start | bytes 4915204
  23.0 5.8 %copy-start.2 = (bf16[24,1280]{1,0:T(8,128)(2,1)S(1)}, bf16[24,1280]{1,0:T(8,128)(2,1)}, u32[]{:S(2)}) copy-start(bf16[24,1280]{1,0:T(8,128)(2,1)} %hidden_ref.1) | copy-start | bytes 184324
  23.0 5.8 %copy-start.3 = (f32[1280]{0:T(1024)S(1)}, f32[1280]{0:T(1024)}, u32[]{:S(2)}) copy-start(f32[1280]{0:T(1024)} %alpha_ref.2) | copy-start | bytes 15364
  23.0 5.8 %copy-start.5 = (f32[640]{0:T(1024)S(1)}, f32[640]{0:T(1024)}, u32[]{:S(2)}) copy-start(f32[640]{0:T(1024)} %s_gate_ref.1) | copy-start | bytes 7684
  23.0 5.8 %copy-start.6 = (f32[640]{0:T(1024)S(1)}, f32[640]{0:T(1024)}, u32[]{:S(2)}) copy-start(f32[640]{0:T(1024)} %s_up_ref.1) | copy-start | bytes 7684
  23.4 1.3 %collective-permute-start = (bf16[24,1280]{1,0:T(8,128)(2,1)S(1)}, bf16[24,1280]{1,0:T(8,128)(2,1)S(1)}, u32[]{:S(2)}, u32[]{:S(2)}) collective-permute-start(bf16[24,1280]{1,0:T(8,128)(2,1)S(1)} %project.1.left_ref), channel_id=1, source_target_pairs={{0,1},{1,0},{2,3},{3,2},{4,5},{5,4},{6,7},{7,6},{8,9},{9,8},{10,11... | collective-permute-start | bytes 184328 | tf_op jit(solution)/shard_map/sum_heads/ppermute | solution.py:359
  24.7 10.5 %copy-start.4 = (f32[1280]{0:T(1024)S(1)}, f32[1280]{0:T(1024)}, u32[]{:S(2)}) copy-start(f32[1280]{0:T(1024)} %alpha_ref.3) | copy-start | bytes 15364
  24.7 4.0 %collective-permute-start.1 = (bf16[24,1280]{1,0:T(8,128)(2,1)S(1)}, bf16[24,1280]{1,0:T(8,128)(2,1)S(1)}, u32[]{:S(2)}, u32[]{:S(2)}) collective-permute-start(bf16[24,1280]{1,0:T(8,128)(2,1)S(1)} %sum_heads.1.left_ref), channel_id=1, source_target_pairs={{0,3},{1,2},{2,1},{3,0},{4,7},{5,6},{6,5},{7,4},{8,11},{9,10},{10,... | collective-permute-start | bytes 184328 | tf_op jit(solution)/shard_map/sum_heads/ppermute | solution.py:359
  29.9 4.0 %collective-permute-start.2 = (bf16[24,1280]{1,0:T(8,128)(2,1)S(1)}, bf16[24,1280]{1,0:T(8,128)(2,1)S(1)}, u32[]{:S(2)}, u32[]{:S(2)}) collective-permute-start(bf16[24,1280]{1,0:T(8,128)(2,1)S(1)} %get-tuple-element.33.left_ref), channel_id=1, source_target_pairs={{0,3},{1,2},{2,1},{3,0},{4,7},{5,6},{6,5},{7,4},{8,11},{9,10},{10,... | collective-permute-start | bytes 184328 | tf_op jit(solution)/shard_map/sum_units/ppermute | solution.py:359
  33.9 1.3 %collective-permute-start.3 = (bf16[24,1280]{1,0:T(8,128)(2,1)S(1)}, bf16[24,1280]{1,0:T(8,128)(2,1)S(1)}, u32[]{:S(2)}, u32[]{:S(2)}) collective-permute-start(bf16[24,1280]{1,0:T(8,128)(2,1)S(1)} %sum_units.1.left_ref), channel_id=1, source_target_pairs={{0,1},{1,0},{2,3},{3,2},{4,5},{5,4},{6,7},{7,6},{8,9},{9,8},{10,11... | collective-permute-start | bytes 184328 | tf_op jit(solution)/shard_map/sum_units/ppermute | solution.py:359

commit v9 on v6

--- a/solution.py
+++ b/solution.py
@@ -321,8 +321,12 @@
     out_ref[...] = dot(gated, w_down_ref[...]).astype(BF16)
 
 
-def final_kernel(left_ref, right_ref, mid_ref, alpha_ref, out_ref):
-    out_ref[...] = renormed(left_ref, right_ref, mid_ref[...].astype(F32), alpha_ref)
+def final_kernel(own_ref, far_ref, near_ref, side_ref, mid_ref, alpha_ref, out_ref):
+    here = own_ref[...].astype(F32) + near_ref[...].astype(F32)
+    total = here + (far_ref[...].astype(F32) + side_ref[...].astype(F32))
+    base = mid_ref[...].astype(F32)
+    alpha = alpha_ref[...][None, :]
+    out_ref[...] = row_norm(base + alpha * (row_norm(total) - base)).astype(BF16)
 
 
 def call(kernel, outs, cost, far=(), near=(), out_far=(), scratch=(), copies=0):
@@ -452,12 +456,10 @@
             near=(projected, other, hidden, alpha_attn, w_gate_up, w_down, s_gate, s_up),
         )
     with jax.named_scope("sum_units"):
-        other = exchanged(downward, 3)
-        (downward,) = call(add_kernel, (wide,), (10**5, 10**5), near=(downward, other))
-        other = exchanged(downward, 1)
+        others = [exchanged(downward, step) for step in (3, 1, 2)]
     with jax.named_scope("final"):
         (updated,) = call(
-            final_kernel, (wide,), (10**6, 10**5), near=(downward, other, middle, alpha_mlp)
+            final_kernel, (wide,), (10**6, 10**5), near=(downward, *others, middle, alpha_mlp)
         )
         return updated
 

time: 36.5 us -> 36.4 us (level)
  waiting for transfers between devices: 8.27 us -> 7.54 us
  starting transfers between devices: 10.3 us -> 10.9 us
    ppermute x4 -> x5, waiting for transfers between devices: 7.67 us -> 6.94 us  [exchanged(): return lax.ppermute(value, 'head', [(i, i ^ step) for i in range(places)])]
    ppermute x4 -> x5, starting transfers between devices: 2.96 us -> 3.58 us  [exchanged(): return lax.ppermute(value, 'head', [(i, i ^ step) for i in range(places)])]
    pallas_call x8 -> x7, Pallas kernels: 8.58 us -> 8.58 us  [call(): pl.pallas_call(kernel, in_specs=[HBM] * len(far) + [VMEM] * len(near), ou...]
  transfers between devices with their start and end apart: 5 -> 6, of which waited for: 5 -> 5; matrix products, arithmetic and copies ran while one was open for 0% -> 0% of each run, Pallas kernels for 10% -> 10%
where the time goes in v9:
time: 36.4 us; the launch traced here: 36.1 us
  starting transfers between devices  10.9 us (30%)
  blocking collectives  8.96 us (25%)
  Pallas kernels  8.58 us (24%)
  waiting for transfers between devices  7.54 us (21%)
    all_to_all x1, blocking collectives, on_device(): lax.all_to_all(partial, 'req', 0, 0, axis_index_groups=[centre_first(part...  8.96 us
    pallas_call x7, Pallas kernels, call(): pl.pallas_call(kernel, in_specs=[HBM] * len(far) + [VMEM] * len(near), ou...  8.58 us
    all_to_all x1, starting transfers between devices, on_device(): lax.all_to_all(sent, ('req', 'head'), 0, 0, axis_index_groups=mixed_group...  7.31 us
    ppermute x5, waiting for transfers between devices, exchanged(): return lax.ppermute(value, 'head', [(i, i ^ step) for i in range(places)])  6.94 us
    ppermute x5, starting transfers between devices, exchanged(): return lax.ppermute(value, 'head', [(i, i ^ step) for i in range(places)])  3.58 us
  transfers between devices with their start and end apart: 6, of which 5 were waited for; matrix products, arithmetic and copies ran while one was open for 0% of the time, Pallas kernels for 10%

profile of v9, /device:TPU:0, one launch (start us, length us, event | category | flops | bytes accessed | tf_op | source)
XLA Modules:
  0.0 36.1 jit_solution(4822121505065561011)
XLA Ops:
  0.0 1.7 %long_hidden.1 = (bf16[8,4,1280]{2,1,0:T(4,128)(2,1)}, bf16[24,1280]{1,0:T(8,128)(2,1)S(1)}, f32[24,128]{1,0:T(8,128)S(1)}, f32[24,320]{1,0:T(8,128)S(1)}, f32[3...) custom-call(s32[4]{0:T(128)} %longs_hbm.1, ...), custom_call_target="tpu_custom_call" | custom-call | flops 1000000 | bytes 3000000 | tf_op jit(solution)/shard_map/long_hidden/pallas_call | solution.py:334
  1.7 7.3 %all-to-all-start = ((bf16[8,4,1280]{2,1,0:T(4,128)(2,1)}), bf16[8,4,1280]{2,1,0:T(4,128)(2,1)S(1)}, u32[]{:S(2)}, u32[]{:S(2)}) async-start(bf16[8,4,1280]{2,1,0:T(4,128)(2,1)} %get-tuple-element.20), calls=%async_computation | async-start | bytes 163840 | tf_op jit(solution)/shard_map/long_hidden/all_to_all | solution.py:411
  9.0 3.5 %short_attention.1 = (f32[24,320]{1,0:T(8,128)S(1)}, f32[24,320]{1,0:T(8,128)S(1)}, f32[24,320]{1,0:T(8,128)S(1)}, f32[24,320]{1,0:T(8,128)S(1)}, bf16[4,320,256]{2,1,0:T(8,128)(2,1)S(1)}) custom-call(s32[24]{0:T(128)} %lengths_hbm.1, bf16[3,320,1280]{2,1,0:T(8,128)(2,1)} %bitcast.6, bf16[24,320,128]{2,1,0:T(8,128)(2,1)} %bitcast.7, ...), custom_call_target="tpu_custom_call" | custom-call | flops 1000000000 | bytes 6000000 | tf_op jit(solution)/shard_map/short_attention/pallas_call | solution.py:334
  12.5 0.0 copy-start.7
  12.5 0.6 %all-to-all-done.received_ref = bf16[8,4,1280]{2,1,0:T(4,128)(2,1)S(1)} async-done(((bf16[8,4,1280]{2,1,0:T(4,128)(2,1)}), bf16[8,4,1280]{2,1,0:T(4,128)(2,1)S(1)}, u32[]{:S(2)}, u32[]{:S(2)}) %all-to-all-start) | async-done | bytes 81952 | tf_op jit(solution)/shard_map/long_hidden/all_to_all | solution.py:411
  13.1 1.0 %long_attention.1 = f32[8,4,384]{2,1,0:T(4,128)S(1)} custom-call(bf16[8,4,1280]{2,1,0:T(4,128)(2,1)S(1)} %all-to-all-done.received_ref, f32[320]{0:T(512)S(1)} %get-tuple-element.21.gains_ref, bf16[320,1280]{1,0:T(8,128)(2,1)S(1)} %get-tuple-element.22.w_ref, bf16[4,320,256]{2,1,0:T(8,128)(2,1)S(1)} %get-tuple-element.23.keys_ref, ...), custom_call_target="tpu_custom_call" | custom-call | flops 1000000000 | bytes 4000000 | tf_op jit(solution)/shard_map/long_attention/pallas_call | solution.py:334
  14.1 9.0 %all_to_all.10.parts_ref = f32[8,4,384]{2,1,0:T(4,128)S(1)} all-to-all(f32[8,4,384]{2,1,0:T(4,128)S(1)} %long_attention.1), channel_id=1, replica_groups={{16,0,4,8,12,20,24,28},{17,1,5,9,13,21,25,29},{18,2,6,10,14,22,26,30},{..., dimensions={0} | all-to-all | bytes 98304 | tf_op jit(solution)/shard_map/long_parts/all_to_all | solution.py:437
  23.1 0.0 copy-done.7
  23.1 0.0 copy-start.3
  23.1 0.0 copy-start.5
  23.1 0.0 copy-start.6
  23.1 0.4 %project.1.left_ref = bf16[24,1280]{1,0:T(8,128)(2,1)S(1)} custom-call(f32[8,4,384]{2,1,0:T(4,128)S(1)} %all_to_all.10.parts_ref, f32[24,320]{1,0:T(8,128)S(1)} %get-tuple-element.28.short_ref, f32[24,320]{1,0:T(8,128)S(1)} %get-tuple-element.29.short_lse_ref, f32[24,320]{1,0:T(8,128)S(1)} %get-tuple-element.30.value_ref, ...), custom_call_target="tpu_custom_call" | custom-call | flops 20000000000 | bytes 1000000 | tf_op jit(solution)/shard_map/project/pallas_call | solution.py:334
  23.5 0.1 collective-permute-start
  23.6 1.2 %collective-permute-done.right_ref = bf16[24,1280]{1,0:T(8,128)(2,1)S(1)} collective-permute-done((bf16[24,1280]{1,0:T(8,128)(2,1)S(1)}, bf16[24,1280]{1,0:T(8,128)(2,1)S(1)}, u32[]{:S(2)}, u32[]{:S(2)}) %collective-permute-start) | collective-permute-done | bytes 61472 | tf_op jit(solution)/shard_map/sum_heads/ppermute | solution.py:362
  24.9 0.0 copy-start.4
  24.9 1.3 %collective-permute-start.1 = (bf16[24,1280]{1,0:T(8,128)(2,1)S(1)}, bf16[24,1280]{1,0:T(8,128)(2,1)S(1)}, u32[]{:S(2)}, u32[]{:S(2)}) collective-permute-start(bf16[24,1280]{1,0:T(8,128)(2,1)S(1)} %sum_heads.1.left_ref), channel_id=1, source_target_pairs={{0,3},{1,2},{2,1},{3,0},{4,7},{5,6},{6,5},{7,4},{8,11},{9,10},{10,... | collective-permute-start | bytes 184328 | tf_op jit(solution)/shard_map/sum_heads/ppermute | solution.py:362
  26.2 2.7 %collective-permute-done.1.right_ref = bf16[24,1280]{1,0:T(8,128)(2,1)S(1)} collective-permute-done((bf16[24,1280]{1,0:T(8,128)(2,1)S(1)}, bf16[24,1280]{1,0:T(8,128)(2,1)S(1)}, u32[]{:S(2)}, u32[]{:S(2)}) %collective-permute-start.1) | collective-permute-done | bytes 61472 | tf_op jit(solution)/shard_map/sum_heads/ppermute | solution.py:362
  28.9 0.0 copy-done
  28.9 0.0 copy-done.1
  28.9 0.0 copy-done.2
  28.9 0.0 copy-done.3
  28.9 0.0 copy-done.5
  28.9 0.0 copy-done.6
  28.9 1.1 %mlp.1 = (bf16[24,1280]{1,0:T(8,128)(2,1)S(1)}, bf16[24,1280]{1,0:T(8,128)(2,1)S(1)}) custom-call(bf16[24,1280]{1,0:T(8,128)(2,1)S(1)} %sum_heads.1.left_ref, bf16[24,1280]{1,0:T(8,128)(2,1)S(1)} %collective-permute-done.1.right_ref, bf16[24,1280]{1,0:T(8,128)(2,1)S(1)} %copy-done.2, f32[1280]{0:T(1024)S(1)} %copy-done.3, bf16[2,1280,640]{2,1,0:T(8,128)(2,1)S(1)} %copy-done, ...), custom_call_target="tpu_custom_call" | custom-call | flops 100000000 | bytes 5000000 | tf_op jit(solution)/shard_map/mlp/pallas_call | solution.py:334
  30.1 1.5 %collective-permute-start.4 = (bf16[24,1280]{1,0:T(8,128)(2,1)S(1)}, bf16[24,1280]{1,0:T(8,128)(2,1)S(1)}, u32[]{:S(2)}, u32[]{:S(2)}) collective-permute-start(bf16[24,1280]{1,0:T(8,128)(2,1)S(1)} %get-tuple-element.33.own_ref), channel_id=1, source_target_pairs={{0,2},{1,3},{2,0},{3,1},{4,6},{5,7},{6,4},{7,5},{8,10},{9,11},{10,... | collective-permute-start | bytes 184328 | tf_op jit(solution)/shard_map/sum_units/ppermute | solution.py:362
  31.6 0.0 collective-permute-start.3
  31.6 0.6 %collective-permute-start.2 = (bf16[24,1280]{1,0:T(8,128)(2,1)S(1)}, bf16[24,1280]{1,0:T(8,128)(2,1)S(1)}, u32[]{:S(2)}, u32[]{:S(2)}) collective-permute-start(bf16[24,1280]{1,0:T(8,128)(2,1)S(1)} %get-tuple-element.33.own_ref), channel_id=1, source_target_pairs={{0,3},{1,2},{2,1},{3,0},{4,7},{5,6},{6,5},{7,4},{8,11},{9,10},{10,... | collective-permute-start | bytes 184328 | tf_op jit(solution)/shard_map/sum_units/ppermute | solution.py:362
  32.2 2.1 %collective-permute-done.4.side_ref = bf16[24,1280]{1,0:T(8,128)(2,1)S(1)} collective-permute-done((bf16[24,1280]{1,0:T(8,128)(2,1)S(1)}, bf16[24,1280]{1,0:T(8,128)(2,1)S(1)}, u32[]{:S(2)}, u32[]{:S(2)}) %collective-permute-start.4) | collective-permute-done | bytes 61472 | tf_op jit(solution)/shard_map/sum_units/ppermute | solution.py:362
  34.3 0.0 collective-permute-done.3.near_ref
  34.3 0.9 %collective-permute-done.2.far_ref = bf16[24,1280]{1,0:T(8,128)(2,1)S(1)} collective-permute-done((bf16[24,1280]{1,0:T(8,128)(2,1)S(1)}, bf16[24,1280]{1,0:T(8,128)(2,1)S(1)}, u32[]{:S(2)}, u32[]{:S(2)}) %collective-permute-start.2) | collective-permute-done | bytes 61472 | tf_op jit(solution)/shard_map/sum_units/ppermute | solution.py:362
  35.3 0.0 copy-done.4
  35.3 0.9 %final.1 = bf16[24,1280]{1,0:T(8,128)(2,1)} custom-call(bf16[24,1280]{1,0:T(8,128)(2,1)S(1)} %get-tuple-element.33.own_ref, bf16[24,1280]{1,0:T(8,128)(2,1)S(1)} %collective-permute-done.2.far_ref, bf16[24,1280]{1,0:T(8,128)(2,1)S(1)} %collective-permute-done.3.near_ref, bf16[24,1280]{1,0:T(8,128)(2,1)S(1)} %collective-permute-done.4.side_ref, ...), custom_call_target="tpu_custom_call" | custom-call | flops 1000000 | bytes 100000 | tf_op jit(solution)/shard_map/final/pallas_call | solution.py:334
  (4 shorter events, 0.0 us)
Async XLA Ops:
  1.7 11.4 %all-to-all-start = ((bf16[8,4,1280]{2,1,0:T(4,128)(2,1)}), bf16[8,4,1280]{2,1,0:T(4,128)(2,1)S(1)}, u32[]{:S(2)}, u32[]{:S(2)}) async-start(bf16[8,4,1280]{2,1,0:T(4,128)(2,1)} %get-tuple-element.20), calls=%async_computation | async-start | bytes 163840 | tf_op jit(solution)/shard_map/long_hidden/all_to_all | solution.py:411
  12.5 10.6 %copy-start.7 = (bf16[320,1280]{1,0:T(8,128)(2,1)S(1)}, bf16[320,1280]{1,0:T(8,128)(2,1)}, u32[]{:S(2)}) copy-start(bf16[320,1280]{1,0:T(8,128)(2,1)} %w_ref.1) | copy-start | bytes 2457604
  23.1 5.8 %copy-start = (bf16[2,1280,640]{2,1,0:T(8,128)(2,1)S(1)}, bf16[2,1280,640]{2,1,0:T(8,128)(2,1)}, u32[]{:S(2)}) copy-start(bf16[2,1280,640]{2,1,0:T(8,128)(2,1)} %w_gate_up_ref.1) | copy-start | bytes 9830404
  23.1 5.8 %copy-start.1 = (bf16[640,1280]{1,0:T(8,128)(2,1)S(1)}, bf16[640,1280]{1,0:T(8,128)(2,1)}, u32[]{:S(2)}) copy-start(bf16[640,1280]{1,0:T(8,128)(2,1)} %w_down_ref.1) | copy-start | bytes 4915204
  23.1 5.8 %copy-start.2 = (bf16[24,1280]{1,0:T(8,128)(2,1)S(1)}, bf16[24,1280]{1,0:T(8,128)(2,1)}, u32[]{:S(2)}) copy-start(bf16[24,1280]{1,0:T(8,128)(2,1)} %hidden_ref.1) | copy-start | bytes 184324
  23.1 5.8 %copy-start.3 = (f32[1280]{0:T(1024)S(1)}, f32[1280]{0:T(1024)}, u32[]{:S(2)}) copy-start(f32[1280]{0:T(1024)} %alpha_ref.2) | copy-start | bytes 15364
  23.1 5.8 %copy-start.5 = (f32[640]{0:T(1024)S(1)}, f32[640]{0:T(1024)}, u32[]{:S(2)}) copy-start(f32[640]{0:T(1024)} %s_gate_ref.1) | copy-start | bytes 7684
  23.1 5.8 %copy-start.6 = (f32[640]{0:T(1024)S(1)}, f32[640]{0:T(1024)}, u32[]{:S(2)}) copy-start(f32[640]{0:T(1024)} %s_up_ref.1) | copy-start | bytes 7684
  23.5 1.3 %collective-permute-start = (bf16[24,1280]{1,0:T(8,128)(2,1)S(1)}, bf16[24,1280]{1,0:T(8,128)(2,1)S(1)}, u32[]{:S(2)}, u32[]{:S(2)}) collective-permute-start(bf16[24,1280]{1,0:T(8,128)(2,1)S(1)} %project.1.left_ref), channel_id=1, source_target_pairs={{0,1},{1,0},{2,3},{3,2},{4,5},{5,4},{6,7},{7,6},{8,9},{9,8},{10,11... | collective-permute-start | bytes 184328 | tf_op jit(solution)/shard_map/sum_heads/ppermute | solution.py:362
  24.9 10.4 %copy-start.4 = (f32[1280]{0:T(1024)S(1)}, f32[1280]{0:T(1024)}, u32[]{:S(2)}) copy-start(f32[1280]{0:T(1024)} %alpha_ref.3) | copy-start | bytes 15364
  24.9 4.0 %collective-permute-start.1 = (bf16[24,1280]{1,0:T(8,128)(2,1)S(1)}, bf16[24,1280]{1,0:T(8,128)(2,1)S(1)}, u32[]{:S(2)}, u32[]{:S(2)}) collective-permute-start(bf16[24,1280]{1,0:T(8,128)(2,1)S(1)} %sum_heads.1.left_ref), channel_id=1, source_target_pairs={{0,3},{1,2},{2,1},{3,0},{4,7},{5,6},{6,5},{7,4},{8,11},{9,10},{10,... | collective-permute-start | bytes 184328 | tf_op jit(solution)/shard_map/sum_heads/ppermute | solution.py:362
  30.1 4.2 %collective-permute-start.4 = (bf16[24,1280]{1,0:T(8,128)(2,1)S(1)}, bf16[24,1280]{1,0:T(8,128)(2,1)S(1)}, u32[]{:S(2)}, u32[]{:S(2)}) collective-permute-start(bf16[24,1280]{1,0:T(8,128)(2,1)S(1)} %get-tuple-element.33.own_ref), channel_id=1, source_target_pairs={{0,2},{1,3},{2,0},{3,1},{4,6},{5,7},{6,4},{7,5},{8,10},{9,11},{10,... | collective-permute-start | bytes 184328 | tf_op jit(solution)/shard_map/sum_units/ppermute | solution.py:362
  31.6 2.7 %collective-permute-start.3 = (bf16[24,1280]{1,0:T(8,128)(2,1)S(1)}, bf16[24,1280]{1,0:T(8,128)(2,1)S(1)}, u32[]{:S(2)}, u32[]{:S(2)}) collective-permute-start(bf16[24,1280]{1,0:T(8,128)(2,1)S(1)} %get-tuple-element.33.own_ref), channel_id=1, source_target_pairs={{0,1},{1,0},{2,3},{3,2},{4,5},{5,4},{6,7},{7,6},{8,9},{9,8},{10,11... | collective-permute-start | bytes 184328 | tf_op jit(solution)/shard_map/sum_units/ppermute | solution.py:362
  31.6 3.6 %collective-permute-start.2 = (bf16[24,1280]{1,0:T(8,128)(2,1)S(1)}, bf16[24,1280]{1,0:T(8,128)(2,1)S(1)}, u32[]{:S(2)}, u32[]{:S(2)}) collective-permute-start(bf16[24,1280]{1,0:T(8,128)(2,1)S(1)} %get-tuple-element.33.own_ref), channel_id=1, source_target_pairs={{0,3},{1,2},{2,1},{3,0},{4,7},{5,6},{6,5},{7,4},{8,11},{9,10},{10,... | collective-permute-start | bytes 184328 | tf_op jit(solution)/shard_map/sum_units/ppermute | solution.py:362
